TPU v7x, 32 devices: a whole 2x2x4 slice. The times are simulated.
32 devices in a mesh: dp: 2 (over core), tensor: 4 (over y, x), corpus: 4 (over z).
Axes of the slice: x: 2, y: 2, z: 4, core: 2. Of those that a mesh axis runs over, the one named last changes fastest.
Arguments:
- queries: bfloat16 [512, 2048], P(('dp', 'tensor', 'corpus')), may hold values from -24 to 24
- passages: bfloat16 [8192, 2048], P(('dp', 'corpus'), 'tensor'), may hold values from -6 to 6
- pos_ids: int32 [512], P(('dp', 'tensor', 'corpus')), may hold values from 0 to 8191, as said below
- neg_ids: int32 [512, 32], P(('dp', 'tensor', 'corpus')), may hold values from 0 to 8191, as said below
Outputs:
- grad_query: float32 [512, 2048], P(('dp', 'tensor', 'corpus'))
- losses: float32 [512], P(('dp', 'tensor', 'corpus'))
- grad_pass: float32 [8192, 2048], P(('dp', 'corpus'), 'tensor')
Inputs may be any that keep to these rules, and one draw needn't show every extreme that they name: `pos_ids`: together with neg_ids: the ids named by the 16 queries of one device, positives and negatives together, fall at most 132 times into one block of 1024 passage rows (rows b * 1024 to (b + 1) * 1024 - 1), and exactly 132 times into one block that is the same for every device. Ids may repeat. `neg_ids`: counted together with pos_ids as stated there.
All inputs are finite; a program needn't handle non-finite values.
Results may differ from a plain program's by a relative error of at most 0.0035.
Values may be sent and summed in bfloat16 or wider, within the bound.
No kernel may reach another device: no remote copies, remote signals or barrier semaphores. Data moves between devices by JAX's collectives and lax.ppermute only.
A program may use at most 128 MiB of HBM per device.

v0:
```python
import jax
import jax.numpy as jnp
from jax import lax
from jax.sharding import PartitionSpec as P


def lookup_rows(row_table, asked_ids):
    return jnp.take(row_table, asked_ids, axis=0, mode="fill", fill_value=0)


def body(queries, passages, pos_ids, neg_ids):
    per_device, feat_width = queries.shape
    block_rows, shard_width = passages.shape
    neg_count = neg_ids.shape[1]
    owners = lax.axis_size("dp") * lax.axis_size("corpus")
    slot_count = 2 * per_device * (neg_count + 1) // owners
    score_scale = feat_width ** (-0.5)
    wanted = jnp.concatenate([pos_ids[:, None], neg_ids], axis=1).reshape(-1)
    owner_of = wanted // block_rows
    local_row = wanted % block_rows
    matches = (owner_of[:, None] == jnp.arange(owners)[None, :]).astype(jnp.int32)
    earlier = jnp.cumsum(matches, axis=0) - matches
    slot_of = owner_of * slot_count + jnp.sum(earlier * matches, axis=1)
    send_ids = jnp.full((owners * slot_count,), block_rows, jnp.int32).at[slot_of].set(local_row)
    send_ids = send_ids.reshape(owners, slot_count)
    row_table = lax.all_gather(passages, "tensor", axis=1, tiled=True)
    asked_ids = lax.all_to_all(send_ids, ("dp", "corpus"), split_axis=0, concat_axis=0, tiled=True)
    found = lookup_rows(row_table, asked_ids)
    fetched = lax.all_to_all(found, ("dp", "corpus"), split_axis=0, concat_axis=0, tiled=True)
    gathered = fetched.reshape(owners * slot_count, feat_width)[slot_of]
    gathered = gathered.reshape(per_device, neg_count + 1, feat_width)
    pos_rows = gathered[:, 0, :]
    neg_rows = gathered[:, 1:, :]
    in_batch = lax.all_gather(pos_rows, "dp", axis=0, tiled=True)
    columns = in_batch.shape[0]
    in_scores = (
        lax.dot_general(
            queries, in_batch, (((1,), (1,)), ((), ())), preferred_element_type=jnp.float32
        )
        * score_scale
    )
    neg_scores = (
        jnp.einsum("md,mkd->mk", queries, neg_rows, preferred_element_type=jnp.float32)
        * score_scale
    )
    logits = jnp.concatenate([in_scores, neg_scores], axis=1)
    row_max = jnp.max(logits, axis=1, keepdims=True)
    exponent = jnp.exp(logits - row_max)
    denominator = jnp.sum(exponent, axis=1, keepdims=True)
    own_col = lax.axis_index("dp") * per_device + jnp.arange(per_device)
    target = (jnp.arange(columns + neg_count)[None, :] == own_col[:, None]).astype(jnp.float32)
    losses = jnp.log(denominator[:, 0]) + row_max[:, 0] - jnp.sum(target * logits, axis=1)
    weights = (exponent / denominator - target).astype(jnp.bfloat16)
    in_weights = weights[:, :columns]
    neg_weights = weights[:, columns:]
    grad_query = jnp.dot(in_weights, in_batch, preferred_element_type=jnp.float32)
    grad_query = grad_query + jnp.einsum(
        "mk,mkd->md", neg_weights, neg_rows, preferred_element_type=jnp.float32
    )
    grad_query = grad_query * score_scale
    in_terms = lax.dot_general(
        in_weights, queries, (((0,), (0,)), ((), ())), preferred_element_type=jnp.float32
    )
    pos_grad = lax.psum_scatter(in_terms, "dp", scatter_dimension=0, tiled=True) * score_scale
    neg_grad = (
        neg_weights.astype(jnp.float32)[:, :, None]
        * queries.astype(jnp.float32)[:, None, :]
        * score_scale
    )
    row_grads = jnp.concatenate([pos_grad[:, None, :], neg_grad], axis=1).astype(jnp.bfloat16)
    row_grads = row_grads.reshape(-1, feat_width)
    grad_slots = (
        jnp.zeros((owners * slot_count, feat_width), jnp.bfloat16).at[slot_of].set(row_grads)
    )
    grad_slots = grad_slots.reshape(owners, slot_count, feat_width)
    arrived = lax.all_to_all(grad_slots, ("dp", "corpus"), split_axis=0, concat_axis=0, tiled=True)
    accum_grad = jnp.zeros((block_rows, feat_width), jnp.float32)
    accum_grad = accum_grad.at[asked_ids.reshape(-1)].add(
        arrived.reshape(-1, feat_width).astype(jnp.float32), mode="drop"
    )
    grad_pass = lax.psum_scatter(accum_grad, "tensor", scatter_dimension=1, tiled=True)
    return (grad_query, losses, grad_pass)


def solution(mesh):
    in_specs = (
        P(("dp", "tensor", "corpus"), None),
        P(("dp", "corpus"), "tensor"),
        P(("dp", "tensor", "corpus")),
        P(("dp", "tensor", "corpus"), None),
    )
    out_specs = (
        P(("dp", "tensor", "corpus"), None),
        P(("dp", "tensor", "corpus")),
        P(("dp", "corpus"), "tensor"),
    )
    return jax.shard_map(body, mesh=mesh, in_specs=in_specs, out_specs=out_specs, check_vma=False)
```

profile of v0, /device:TPU:0, one launch (start us, length us, event | category | flops | bytes accessed | tf_op | source)
XLA Modules:
  0.0 468.5 jit_solution(11466890494160415889)
XLA Ops:
  11.7 4.1 scatter_custom_fusion
  15.9 11.7 %all_to_all.25 = s32[8,1,132]{2,1,0:T(1,128)S(1)} all-to-all(s32[8,1,132]{2,1,0:T(1,128)S(1)} %all_to_all.16), channel_id=1, replica_groups=mesh['dp'=2,'tensor'=4,'corpus'=4] {'dp','corpus'}, dimensions={0} | all-to-all | bytes 8448 | tf_op jit(solution)/shard_map/all_to_all | solution.py:27
  27.7 37.4 %all-gather.3.cloned.1.call-done = bf16[1024,2048]{1,0:T(8,128)(2,1)} async-done(((bf16[1024,512]{1,0:T(8,128)(2,1)}), bf16[1024,2048]{1,0:T(8,128)(2,1)}) %all-gather.3.cloned.1.call-update) | async-done | bytes 4194320 | tf_op jit(solution)/shard_map/all_gather | solution.py:26
  65.1 13.2 %gather_fusion = bf16[1056,2048]{1,0:T(8,128)(2,1)} fusion(bf16[1024,2048]{1,0:T(8,128)(2,1)} %all-gather.3.cloned.1.call-done, s32[2048]{0:T(1024)S(1)} %pad_clamp_fusion), kind=kCustom, calls=%fused_computation | custom fusion | bytes 8654976 | tf_op jit(solution)/shard_map/jit(_take)/gather | solution.py:8
  78.4 5.2 %reshape.228 = bf16[8,132,2048]{2,1,0:T(8,128)(2,1)} reshape(bf16[1056,2048]{1,0:T(8,128)(2,1)} %gather_fusion) | data formatting | bytes 8650752 | tf_op jit(solution)/shard_map/jit(_take)/gather | solution.py:8
  83.5 4.7 %broadcast_select_fusion = bf16[8,132,2048]{2,1,0:T(8,128)(2,1)} fusion(bf16[8,132,2048]{2,1,0:T(8,128)(2,1)} %reshape.228, pred[8,132]{1,0:T(8,128)(4,1)S(1)} %compare_and_fusion), kind=kLoop, calls=%fused_computation.5 | loop fusion | flops 2162688 | bytes 8651808 | tf_op jit(solution)/shard_map/jit(_take)/select_n | solution.py:8
  88.3 4.7 %all-to-all-start.1 = ((bf16[8,132,2048]{2,1,0:T(8,128)(2,1)}), bf16[8,132,2048]{2,1,0:T(8,128)(2,1)}, u32[]{:S(2)}, u32[]{:S(2)}) async-start(bf16[8,132,2048]{2,1,0:T(8,128)(2,1)} %broadcast_select_fusion), calls=%async_computation.1 | async-start | bytes 8912896 | tf_op jit(solution)/shard_map/all_to_all | solution.py:29
  93.1 99.1 %all-to-all-done.1 = bf16[8,132,2048]{2,1,0:T(8,128)(2,1)} async-done(((bf16[8,132,2048]{2,1,0:T(8,128)(2,1)}), bf16[8,132,2048]{2,1,0:T(8,128)(2,1)}, u32[]{:S(2)}, u32[]{:S(2)}) %all-to-all-start.1) | async-done | bytes 4325408 | tf_op jit(solution)/shard_map/all_to_all | solution.py:29
  192.3 5.2 %reshape.221 = bf16[1056,2048]{1,0:T(8,128)(2,1)} reshape(bf16[8,132,2048]{2,1,0:T(8,128)(2,1)} %all-to-all-done.1) | data formatting | bytes 8650752 | tf_op jit(solution)/shard_map/reshape | solution.py:30
  197.4 9.1 %gather_fusion.1 = bf16[528,2048]{1,0:T(8,128)(2,1)S(1)} fusion(bf16[1056,2048]{1,0:T(8,128)(2,1)} %reshape.221, s32[1024]{0:T(1024)S(1)} %pad_clamp_fusion.1), kind=kCustom, calls=%fused_computation.1 | custom fusion | bytes 4327488 | tf_op jit(solution)/shard_map/gather | solution.py:30
  206.5 1.9 reshape.222
  209.5 2.4 fusion.7
  212.1 2.1 all-gather
  215.7 1.8 multiply_convert_fusion
  217.6 3.5 reduce-scatter.3.cloned.1.call-done
  222.1 2.4 pad_maximum_fusion
  224.5 1.8 reshape.255
  226.2 10.5 %scatter_custom_fusion.1 = bf16[1056,2048]{1,0:T(8,128)(2,1)} fusion(s32[528]{0:T(1024)S(1)} %fusion.26, bf16[528,2048]{1,0:T(8,128)(2,1)} %reshape.255, bf16[]{:T(256)} %constant.67.clone.1), kind=kCustom, calls=%fused_computation.12 | custom fusion | bytes 4325888 | tf_op jit(solution)/shard_map/scatter | solution.py:73
  236.8 5.1 %reshape.224 = bf16[8,132,2048]{2,1,0:T(8,128)(2,1)} reshape(bf16[1056,2048]{1,0:T(8,128)(2,1)} %scatter_custom_fusion.1) | data formatting | bytes 8650752 | tf_op jit(solution)/shard_map/reshape | solution.py:75
  241.9 4.8 %all-to-all-start.2 = ((bf16[8,132,2048]{2,1,0:T(8,128)(2,1)}), bf16[8,132,2048]{2,1,0:T(8,128)(2,1)}, u32[]{:S(2)}, u32[]{:S(2)}) async-start(bf16[8,132,2048]{2,1,0:T(8,128)(2,1)} %reshape.224), calls=%async_computation.3 | async-start | bytes 8912896 | tf_op jit(solution)/shard_map/all_to_all | solution.py:76
  247.1 98.8 %all-to-all-done.2 = bf16[8,132,2048]{2,1,0:T(8,128)(2,1)} async-done(((bf16[8,132,2048]{2,1,0:T(8,128)(2,1)}), bf16[8,132,2048]{2,1,0:T(8,128)(2,1)}, u32[]{:S(2)}, u32[]{:S(2)}) %all-to-all-start.2) | async-done | bytes 4325408 | tf_op jit(solution)/shard_map/all_to_all | solution.py:76
  346.0 6.2 %reshape.263 = f32[1056,2048]{1,0:T(8,128)} reshape(bf16[8,132,2048]{2,1,0:T(8,128)(2,1)} %all-to-all-done.2) | data formatting | bytes 12976128 | tf_op jit(solution)/shard_map/convert_element_type | solution.py:79
  352.2 24.7 %scatter_custom_fusion.2 = f32[1024,2048]{1,0:T(8,128)} fusion(s32[1056]{0:T(1024)S(1)} %fusion.18, f32[1056,2048]{1,0:T(8,128)} %reshape.263, f32[]{:T(128)} %constant.70.clone.1), kind=kCustom, calls=%fused_computation.7 | custom fusion | flops 2162688 | bytes 8389120 | tf_op jit(solution)/shard_map/scatter-add | solution.py:78
  380.0 81.9 %reduce-scatter.5.cloned.1.call-done = f32[1024,512]{1,0:T(8,128)} async-done(((f32[1024,2048]{1,0:T(8,128)}), f32[1024,512]{1,0:T(8,128)}) %reduce-scatter.5.cloned.1.call-update) | async-done | bytes 2097168 | tf_op jit(solution)/shard_map/reduce_scatter | solution.py:81
  (50 shorter events, 12.1 us)
Async XLA Ops:
  7.2 58.0 %all-gather.3.cloned.1.call-start = ((), (), s32[]{:S(2)}) async-start(), calls=%async_computation.5 | async-start | bytes 5242880 | tf_op jit(solution)/shard_map/all_gather | solution.py:26
  88.3 4.8 %copy-start.1 = (bf16[16,2048]{1,0:T(8,128)(2,1)S(1)}, bf16[16,2048]{1,0:T(8,128)(2,1)}, u32[]{:S(2)}) copy-start(bf16[16,2048]{1,0:T(8,128)(2,1)} %param.4) | copy-start | bytes 196612
  88.3 104.0 %all-to-all-start.1 = ((bf16[8,132,2048]{2,1,0:T(8,128)(2,1)}), bf16[8,132,2048]{2,1,0:T(8,128)(2,1)}, u32[]{:S(2)}, u32[]{:S(2)}) async-start(bf16[8,132,2048]{2,1,0:T(8,128)(2,1)} %broadcast_select_fusion), calls=%async_computation.1 | async-start | bytes 8912896 | tf_op jit(solution)/shard_map/all_to_all | solution.py:29
  93.0 128.0 %reduce-scatter.3.cloned.1.call-start = ((), (), s32[]{:S(2)}) async-start(), calls=%async_computation.6 | async-start | bytes 393216 | tf_op jit(solution)/shard_map/reduce_scatter | solution.py:64
  241.9 104.1 %all-to-all-start.2 = ((bf16[8,132,2048]{2,1,0:T(8,128)(2,1)}), bf16[8,132,2048]{2,1,0:T(8,128)(2,1)}, u32[]{:S(2)}, u32[]{:S(2)}) async-start(bf16[8,132,2048]{2,1,0:T(8,128)(2,1)} %reshape.224), calls=%async_computation.3 | async-start | bytes 8912896 | tf_op jit(solution)/shard_map/all_to_all | solution.py:76
  246.7 215.2 %reduce-scatter.5.cloned.1.call-start = ((), (), s32[]{:S(2)}) async-start(), calls=%async_computation.7 | async-start | bytes 10485760 | tf_op jit(solution)/shard_map/reduce_scatter | solution.py:81
  376.9 1.7 copy-start
Sparse Core Ops, SparseCore 0:
  9.8 55.2 all-gather.2
  215.8 5.2 reduce-scatter.2
  377.0 84.8 reduce-scatter.4
where the time goes:
time: 470 us; the launch traced here: 468 us
  waiting for transfers between devices  321 us (68%)
  local copies, waits for them, and re-layouts  66.2 us (14%)
  other arithmetic  38.1 us (8%)
  between operations  13.9 us (3%)
  blocking collectives  13.8 us (3%)
  starting transfers between devices  9.91 us (2%)
  matrix products  5 us (1%)
    all_to_all x1, waiting for transfers between devices, body(): lax.all_to_all(found, ('dp', 'corpus'), split_axis=0, concat_axis=0, tile...  99.1 us
    all_to_all x1, waiting for transfers between devices, body(): lax.all_to_all(grad_slots, ('dp', 'corpus'), split_axis=0, concat_axis=0,...  98.8 us
    reduce_scatter x1, waiting for transfers between devices, body(): lax.psum_scatter(accum_grad, 'tensor', scatter_dimension=1, tiled=True)  81.9 us
    all_gather x1, waiting for transfers between devices, body(): row_table = lax.all_gather(passages, 'tensor', axis=1, tiled=True)  37.4 us
    scatter-add x1, other arithmetic, body(): accum_grad.at[asked_ids.reshape(-1)]  24.7 us
    gather x2, local copies, waits for them, and re-layouts, lookup_rows(): return jnp.take(row_table, asked_ids, axis=0, mode='fill', fill_value=0)  18.4 us
    all_to_all x1, blocking collectives, body(): lax.all_to_all(send_ids, ('dp', 'corpus'), split_axis=0, concat_axis=0, t...  11.7 us
    scatter x1, local copies, waits for them, and re-layouts, body(): jnp.zeros((owners * slot_count, feat_width), jnp.bfloat16).at[slot_of]  10.5 us
  transfers between devices with their start and end apart: 5, of which 5 were waited for; matrix products, arithmetic and copies ran while one was open for 3% of the time, Pallas kernels for 0%

commit v1 on v0

v1 whole, which is shorter than its diff:
```python
import jax
import jax.numpy as jnp
from jax import lax
from jax.experimental import pallas as pl
from jax.experimental.pallas import tpu as pltpu
from jax.sharding import PartitionSpec as P

LANES = 128


def pairs(size, bit):
    return [(i, i ^ bit) for i in range(size)]


def swap(value, axis, bit):
    return lax.ppermute(value, axis, pairs(lax.axis_size(axis), bit))


def gather_pieces(pieces, axis):
    bit = 1
    while bit < lax.axis_size(axis):
        pieces = pieces + [swap(piece, axis, bit) for piece in pieces]
        bit *= 2
    return pieces


def scatter_sum(pieces, axis):
    bit = lax.axis_size(axis) // 2
    while bit:
        pieces = [
            mine + swap(theirs, axis, bit) for mine, theirs in zip(pieces[:bit], pieces[bit:])
        ]
        bit //= 2
    return pieces[0]


class Sizes:
    def __init__(self, queries, passages, neg_ids):
        self.own, self.feat = queries.shape
        self.block, self.width = passages.shape
        self.negs = neg_ids.shape[1]
        self.dp = lax.axis_size("dp")
        self.tensor = lax.axis_size("tensor")
        self.corpus = lax.axis_size("corpus")
        self.groups = self.tensor * self.corpus
        self.half = self.groups * self.own
        self.rows = self.dp * self.half
        self.columns = self.dp * self.own
        self.items = self.columns + self.negs
        self.lanes = -(-self.items // LANES) * LANES
        self.pack = max(1, LANES // self.items)
        self.packed = self.rows // self.pack
        self.part = self.packed // self.dp
        self.neg_at = self.columns % LANES
        self.pos_at = 0 if self.neg_at else self.negs
        self.chunks = self.block // LANES
        self.scale = self.feat ** (-0.5)
        self.vmem = min(60, 16 + 10 * self.rows // 1024) * 2**20


def score_kernel(z, *refs):
    arrived = refs[: z.dp]
    passage_ref = refs[z.dp]
    query_ref, index_ref = refs[z.dp + 1 : z.dp + 3]
    part_refs = refs[z.dp + 3 : 2 * z.dp + 3]
    id_ref, local_ref, logit_ref = refs[2 * z.dp + 3 :]
    d, t, c = (lax.axis_index(a) for a in ("dp", "tensor", "corpus"))
    for sd in range(z.dp):
        for sc in range(z.corpus):
            for st in range(z.tensor):
                source = pl.ds((sc * z.tensor + st) * z.own, z.own)
                place = (((d ^ sd) * z.tensor + (t ^ st)) * z.corpus + (c ^ sc)) * z.own
                place = pl.ds(pl.multiple_of(place, z.own), z.own)
                query_ref[place, :] = arrived[sd][source, : z.width]
                code = arrived[sd][source, z.width :].astype(jnp.float32)
                id_ref[place, :] = code * 256.0 + pltpu.roll(code, LANES // 2, 1)
    first = ((d * z.corpus + c) * z.block).astype(jnp.float32)
    wide = -(-z.columns // LANES) * LANES
    row = lax.broadcasted_iota(jnp.int32, (z.half, wide), 0) & (z.own - 1)
    col = lax.broadcasted_iota(jnp.int32, (z.half, wide), 1)
    group_ids = jnp.zeros((z.groups, wide), jnp.float32)
    for h in range(z.dp):
        ids = id_ref[pl.ds(h * z.half, z.half), :]
        pos = jnp.broadcast_to(ids[:, z.pos_at : z.pos_at + 1], (z.half, wide))
        kept = jnp.where(col == row + h * z.own, pos, 0.0)
        group_ids += jnp.sum(kept.reshape(z.groups, z.own, wide), axis=1)
    batch_ids = jnp.broadcast_to(group_ids[:, None, :], (z.groups, z.own, wide))
    batch_ids = batch_ids.reshape(z.half, wide)
    lane = lax.broadcasted_iota(jnp.int32, (z.half, LANES), 1)
    for h in range(z.dp):
        ids = id_ref[pl.ds(h * z.half, z.half), :]
        for base in range(0, z.lanes, LANES):
            named = ids
            if base < z.columns:
                named = jnp.where(lane + base < z.columns, batch_ids[:, base : base + LANES], ids)
            local = named - first
            inside = (local >= 0.0) & (local < float(z.block)) & (lane + base < z.items)
            local_ref[pl.ds(h * z.half, z.half), base : base + LANES] = jnp.where(
                inside, local, -float(2**20)
            ).astype(jnp.int32)
    step = min(z.rows, 256)

    def score(i, carry):
        at = pl.ds(pl.multiple_of(i * step, step), step)
        scores = lax.dot_general(
            query_ref[at, :], passage_ref[...], (((1,), (1,)), ((), ())),
            preferred_element_type=jnp.float32,
        )
        for base in range(0, z.lanes, LANES):
            local = local_ref[at, base : base + LANES]
            chunk, within = local >> 7, local & (LANES - 1)
            picked = jnp.zeros((step, LANES), jnp.float32)
            for j in range(z.chunks):
                found = jnp.take_along_axis(scores[:, j * LANES : (j + 1) * LANES], within, axis=1)
                picked = jnp.where(chunk == j, found, picked)
            logit_ref[at, base : base + LANES] = picked
        return carry

    lax.fori_loop(0, z.rows // step, score, 0)
    lane = lax.broadcasted_iota(jnp.int32, (z.packed, z.lanes), 1)
    index = local_ref[pl.ds(0, z.packed), :]
    for h in range(1, z.pack):
        other = pltpu.roll(local_ref[pl.ds(h * z.packed, z.packed), :], h * z.items, 1)
        index = jnp.where(lane < h * z.items, index, other)
    index_ref[...] = index
    for s in range(z.dp):
        at = pl.multiple_of((d ^ s) * z.part, z.part)
        total = logit_ref[pl.ds(at, z.part), :]
        for h in range(1, z.pack):
            more = logit_ref[pl.ds(pl.multiple_of(h * z.packed + at, z.part), z.part), :]
            total = total + pltpu.roll(more, h * z.items, 1)
        part_refs[s][...] = total


def weight_kernel(z, *refs):
    parts = refs[: z.dp]
    index_ref, passage_ref = refs[z.dp : z.dp + 2]
    dense_ref, loss_ref = refs[z.dp + 2 : z.dp + 4]
    grad_refs = refs[z.dp + 4 : 2 * z.dp + 4]
    logit_ref, tile_ref = refs[2 * z.dp + 4 :]
    d, t, c = (lax.axis_index(a) for a in ("dp", "tensor", "corpus"))
    for s in range(z.dp):
        at = pl.multiple_of((d ^ s) * z.part, z.part)
        logit_ref[pl.ds(at, z.part), :] = parts[s][...] * z.scale

    def softmax(logits, first_row):
        shape = logits.shape
        lane = lax.broadcasted_iota(jnp.int32, shape, 1)
        row = lax.broadcasted_iota(jnp.int32, shape, 0) + first_row
        weights = jnp.zeros(shape, jnp.float32)
        losses = []
        for h in range(z.pack):
            mask = (lane >= h * z.items) & (lane < (h + 1) * z.items)
            top = jnp.max(jnp.where(mask, logits, -jnp.inf), axis=1, keepdims=True)
            exponent = jnp.where(mask, jnp.exp(logits - top), 0.0)
            denominator = jnp.sum(exponent, axis=1, keepdims=True)
            query = row + h * z.packed
            own = (query // z.half) * z.own + (query & (z.own - 1)) + h * z.items
            target = jnp.where(lane == own, 1.0, 0.0)
            weights = jnp.where(mask, exponent / denominator - target, weights)
            chosen = jnp.sum(target * jnp.where(mask, logits, 0.0), axis=1, keepdims=True)
            losses.append(jnp.log(denominator) + top - chosen)
        return weights, losses

    mine = ((d * z.tensor + t) * z.corpus + c) * z.own
    first = pl.multiple_of(mine % z.packed, z.own)
    _, losses = softmax(logit_ref[pl.ds(first, z.own), :], first)
    loss = losses[0]
    for h in range(1, z.pack):
        loss = jnp.where(mine // z.packed == h, losses[h], loss)
    loss_ref[...] = jnp.broadcast_to(loss, (z.own, LANES))

    step = min(z.packed, 256)

    def weigh(i, carry):
        at = pl.ds(pl.multiple_of(i * step, step), step)
        weights, _ = softmax(logit_ref[at, :], i * step)
        logit_ref[at, :] = weights.astype(jnp.bfloat16).astype(jnp.float32)
        return carry

    lax.fori_loop(0, z.packed // step, weigh, 0)

    high = z.pack * z.chunks
    tall = lax.broadcasted_iota(jnp.int32, (high, z.lanes), 0)
    shift = lax.broadcasted_iota(jnp.int32, (1, z.lanes), 1) // z.items * z.chunks
    spread = lax.broadcasted_iota(jnp.int32, (LANES, z.lanes), 0).astype(jnp.bfloat16)

    def place(i, carry):
        for j in range(8):
            r = i * 8 + j
            local = index_ref[pl.ds(r, 1), :]
            chunk = (local >> 7) + shift
            within = (local & (LANES - 1)).astype(jnp.bfloat16)
            left = jnp.where(
                jnp.broadcast_to(chunk, (high, z.lanes)) == tall,
                jnp.broadcast_to(logit_ref[pl.ds(r, 1), :], (high, z.lanes)), 0.0,
            ).astype(jnp.bfloat16)
            right = jnp.where(
                jnp.broadcast_to(within, (LANES, z.lanes)) == spread,
                jnp.bfloat16(1), jnp.bfloat16(0),
            )
            tiles = lax.dot_general(
                left, right, (((1,), (1,)), ((), ())), preferred_element_type=jnp.float32
            )
            for h in range(z.pack):
                at = pl.multiple_of((h * z.packed + r) * z.chunks, z.chunks)
                tile_ref[pl.ds(at, z.chunks), :] = tiles[h * z.chunks : (h + 1) * z.chunks, :]
        return carry

    lax.fori_loop(0, z.packed // 8, place, 0)
    for j in range(z.chunks):
        dense_ref[:, j * LANES : (j + 1) * LANES] = tile_ref[
            pl.ds(j, z.rows, stride=z.chunks), :
        ].astype(jnp.bfloat16)
    for s in range(z.dp):
        at = pl.multiple_of((d ^ s) * z.half, z.half)
        grad_refs[s][...] = jnp.dot(
            dense_ref[pl.ds(at, z.half), :], passage_ref[...], preferred_element_type=jnp.float32
        )


def passage_kernel(z, dense_ref, query_ref, out_ref):
    def one(i, carry):
        at = pl.ds(pl.multiple_of(i * 256, 256), 256)
        out_ref[at, :] = z.scale * lax.dot_general(
            dense_ref[:, at], query_ref[...], (((0,), (0,)), ((), ())),
            preferred_element_type=jnp.float32,
        )
        return carry

    lax.fori_loop(0, z.block // 256, one, 0)


def query_kernel(z, arrived_ref, out_ref):
    for t in range(z.tensor):
        total = arrived_ref[t * z.corpus]
        for c in range(1, z.corpus):
            total = total + arrived_ref[t * z.corpus + c]
        out_ref[:, t * z.width : (t + 1) * z.width] = total * z.scale


def call(z, kernel, outs, scratch, args, flops):
    moved = sum(a.size * a.dtype.itemsize for a in args)
    moved += sum(o.size * jnp.dtype(o.dtype).itemsize for o in outs)
    return pl.pallas_call(
        lambda *refs: kernel(z, *refs),
        out_shape=outs,
        in_specs=[pl.BlockSpec(memory_space=pltpu.VMEM)] * len(args),
        out_specs=[pl.BlockSpec(memory_space=pltpu.VMEM)] * len(outs),
        scratch_shapes=scratch,
        compiler_params=pltpu.CompilerParams(vmem_limit_bytes=z.vmem),
        cost_estimate=pl.CostEstimate(flops=flops, bytes_accessed=moved, transcendentals=0),
    )(*args)


def body(queries, passages, pos_ids, neg_ids):
    z = Sizes(queries, passages, neg_ids)
    f32, bf16 = jnp.float32, jnp.bfloat16
    shape = jax.ShapeDtypeStruct
    t = lax.axis_index("tensor")

    pos = jnp.broadcast_to(pos_ids[:, None], (z.own, LANES // 2))
    ids = jnp.concatenate(
        [pos[:, : z.neg_at], neg_ids, pos[:, : LANES // 2 - z.neg_at - z.negs]], axis=1
    )
    code = jnp.concatenate([ids >> 8, ids & 255], axis=1).astype(bf16)
    plane = []
    for s in range(z.tensor):
        piece = lax.dynamic_slice_in_dim(queries, (t ^ s) * z.width, z.width, axis=1)
        piece = jnp.concatenate([piece, code], axis=1)
        plane.append(swap(piece, "tensor", s) if s else piece)
    plane = jnp.concatenate(plane, axis=0)
    chip = [plane] + [swap(plane, "corpus", s) for s in range(1, z.corpus)]
    arrived = gather_pieces([jnp.concatenate(chip, axis=0)], "dp")

    work = 2 * z.rows * z.block * z.width
    query_rows, index, *parts = call(
        z, score_kernel,
        [shape((z.rows, z.width), bf16), shape((z.packed, z.lanes), jnp.int32)]
        + [shape((z.part, z.lanes), f32)] * z.dp,
        [
            pltpu.VMEM((z.rows, LANES), f32),
            pltpu.VMEM((z.rows, z.lanes), jnp.int32),
            pltpu.VMEM((z.rows, z.lanes), f32),
        ],
        arrived + [passages], work,
    )
    total = scatter_sum(parts, "dp")
    bit = 1
    while bit < z.tensor:
        total = total + swap(total, "tensor", bit)
        bit *= 2
    total = sum([swap(total, "corpus", s) for s in range(1, z.corpus)], total)
    logits = gather_pieces([total], "dp")

    dense, loss, *grads = call(
        z, weight_kernel,
        [shape((z.rows, z.block), bf16), shape((z.own, LANES), f32)]
        + [shape((z.half, z.width), f32)] * z.dp,
        [
            pltpu.VMEM((z.packed, z.lanes), f32),
            pltpu.VMEM((z.rows * z.chunks, LANES), f32),
        ],
        logits + [index, passages], 2 * work,
    )
    (grad_pass,) = call(
        z, passage_kernel, [shape((z.block, z.width), f32)], [], [dense, query_rows], work
    )
    half = scatter_sum(grads, "dp")
    half = half.reshape(z.groups, z.own, z.width)
    half = lax.all_to_all(half, ("tensor", "corpus"), split_axis=0, concat_axis=0, tiled=True)
    (grad_query,) = call(
        z, query_kernel, [shape((z.own, z.feat), f32)], [], [half], half.size
    )
    return (grad_query, loss[:, 0], grad_pass)


def solution(mesh):
    spread = ("dp", "tensor", "corpus")
    in_specs = (P(spread, None), P(("dp", "corpus"), "tensor"), P(spread), P(spread, None))
    out_specs = (P(spread, None), P(spread), P(("dp", "corpus"), "tensor"))
    return jax.shard_map(body, mesh=mesh, in_specs=in_specs, out_specs=out_specs, check_vma=False)
```

time: 470 us -> 79.4 us (0.17)
  waiting for transfers between devices: 321 us -> 37 us
  local copies, waits for them, and re-layouts: 66.2 us -> 3.51 us
  other arithmetic: 38.1 us -> 1.87 us
  Pallas kernels: 0 us -> 14.9 us
  blocking collectives: 13.8 us -> 0 us
  between operations: 13.9 us -> 0.75 us
  starting transfers between devices: 9.91 us -> 21 us
  matrix products: 5 us -> 0 us
    all_to_all x2 -> x1, waiting for transfers between devices: 198 us -> 13.3 us  [body(): lax.all_to_all(half, ('tensor', 'corpus'), split_axis=0, concat_axis=0, t...]
    reduce_scatter x2 -> x0, waiting for transfers between devices: 85.4 us -> none  [the longest x1 81.9 us: body(): lax.psum_scatter(accum_grad, 'tensor', scatter_dimension=1, tiled=True)]
    all_gather x1 -> x0, waiting for transfers between devices: 37.4 us -> none  [body(): row_table = lax.all_gather(passages, 'tensor', axis=1, tiled=True)]
    gather x3 -> x0, local copies, waits for them, and re-layouts: 27.5 us -> none  [the longest x2 18.4 us: lookup_rows(): return jnp.take(row_table, asked_ids, axis=0, mode='fill', fill_value=0)]
    scatter-add x1 -> x0, other arithmetic: 24.7 us -> none  [body(): accum_grad.at[asked_ids.reshape(-1)]]
    ppermute x0 -> x15, waiting for transfers between devices: none -> 23.7 us  [swap(): return lax.ppermute(value, axis, pairs(lax.axis_size(axis), bit))]
    ppermute x0 -> x15, starting transfers between devices: none -> 16.3 us  [swap(): return lax.ppermute(value, axis, pairs(lax.axis_size(axis), bit))]
    pallas_call x0 -> x4, Pallas kernels: none -> 14.9 us  [call(): pl.pallas_call(lambda *refs: kernel(z, *refs), out_shape=outs, in_specs=[...]
  transfers between devices with their start and end apart: 5 -> 16, of which waited for: 5 -> 14; matrix products, arithmetic and copies ran while one was open for 3% -> 1% of each run, Pallas kernels for 0% -> 3%
where the time goes in v1:
time: 79.4 us; the launch traced here: 79.1 us
  waiting for transfers between devices  37 us (47%)
  starting transfers between devices  21 us (26%)
  Pallas kernels  14.9 us (19%)
  local copies, waits for them, and re-layouts  3.51 us (4%)
  other arithmetic  1.87 us (2%)
    ppermute x15, waiting for transfers between devices, swap(): return lax.ppermute(value, axis, pairs(lax.axis_size(axis), bit))  23.7 us
    ppermute x15, starting transfers between devices, swap(): return lax.ppermute(value, axis, pairs(lax.axis_size(axis), bit))  16.3 us
    pallas_call x4, Pallas kernels, call(): pl.pallas_call(lambda *refs: kernel(z, *refs), out_shape=outs, in_specs=[...  14.9 us
    all_to_all x1, waiting for transfers between devices, body(): lax.all_to_all(half, ('tensor', 'corpus'), split_axis=0, concat_axis=0, t...  13.3 us
    all_to_all x1, starting transfers between devices, body(): lax.all_to_all(half, ('tensor', 'corpus'), split_axis=0, concat_axis=0, t...  4.65 us
  transfers between devices with their start and end apart: 16, of which 14 were waited for; matrix products, arithmetic and copies ran while one was open for 1% of the time, Pallas kernels for 3%

profile of v1, /device:TPU:0, one launch (start us, length us, event | category | flops | bytes accessed | tf_op | source)
XLA Modules:
  0.0 79.1 jit_solution(10527892997951437290)
XLA Ops:
  3.1 3.9 %collective-permute-start.2 = (bf16[16,640]{1,0:T(8,128)(2,1)S(1)}, bf16[16,640]{1,0:T(8,128)(2,1)S(1)}, u32[]{:S(2)}, u32[]{:S(2)}) collective-permute-start(bf16[16,640]{1,0:T(8,128)(2,1)S(1)} %get-tuple-element.25), channel_id=1, source_target_pairs={{0,12},{4,8},{8,4},{12,0},{1,13},{5,9},{9,5},{13,1},{2,14},{6,10},... | collective-permute-start | bytes 61448 | tf_op jit(solution)/shard_map/ppermute | solution.py:16
  7.6 1.1 %collective-permute-done.2 = bf16[16,640]{1,0:T(8,128)(2,1)S(1)} collective-permute-done((bf16[16,640]{1,0:T(8,128)(2,1)S(1)}, bf16[16,640]{1,0:T(8,128)(2,1)S(1)}, u32[]{:S(2)}, u32[]{:S(2)}) %collective-permute-start.2) | collective-permute-done | bytes 20512 | tf_op jit(solution)/shard_map/ppermute | solution.py:16
  8.8 2.0 %collective-permute-done = bf16[16,640]{1,0:T(8,128)(2,1)S(1)} collective-permute-done((bf16[16,640]{1,0:T(8,128)(2,1)S(1)}, bf16[16,640]{1,0:T(8,128)(2,1)S(1)}, u32[]{:S(2)}, u32[]{:S(2)}) %collective-permute-start) | collective-permute-done | bytes 20512 | tf_op jit(solution)/shard_map/ppermute | solution.py:16
  11.4 3.6 %collective-permute-start.5 = (bf16[64,640]{1,0:T(8,128)(2,1)S(1)}, bf16[64,640]{1,0:T(8,128)(2,1)S(1)}, u32[]{:S(2)}, u32[]{:S(2)}) collective-permute-start(bf16[64,640]{1,0:T(8,128)(2,1)S(1)} %pad_maximum_fusion), channel_id=1, source_target_pairs={{0,3},{1,2},{2,1},{3,0},{4,7},{5,6},{6,5},{7,4},{8,11},{9,10},{10,... | collective-permute-start | bytes 245768 | tf_op jit(solution)/shard_map/ppermute | solution.py:16
  15.8 3.6 %collective-permute-done.3 = bf16[64,640]{1,0:T(8,128)(2,1)S(1)} collective-permute-done((bf16[64,640]{1,0:T(8,128)(2,1)S(1)}, bf16[64,640]{1,0:T(8,128)(2,1)S(1)}, u32[]{:S(2)}, u32[]{:S(2)}) %collective-permute-start.3) | collective-permute-done | bytes 81952 | tf_op jit(solution)/shard_map/ppermute | solution.py:16
  19.5 1.2 %collective-permute-done.4 = bf16[64,640]{1,0:T(8,128)(2,1)S(1)} collective-permute-done((bf16[64,640]{1,0:T(8,128)(2,1)S(1)}, bf16[64,640]{1,0:T(8,128)(2,1)S(1)}, u32[]{:S(2)}, u32[]{:S(2)}) %collective-permute-start.4) | collective-permute-done | bytes 81952 | tf_op jit(solution)/shard_map/ppermute | solution.py:16
  20.8 1.6 %collective-permute-done.6.refs_1_ = bf16[256,640]{1,0:T(8,128)(2,1)S(1)} collective-permute-done((bf16[256,640]{1,0:T(8,128)(2,1)S(1)}, bf16[256,640]{1,0:T(8,128)(2,1)S(1)}, u32[]{:S(2)}, u32[]{:S(2)}) %collective-permute-start.6) | collective-permute-done | bytes 327712 | tf_op jit(solution)/shard_map/ppermute | solution.py:16
  22.4 1.2 %copy-done = bf16[1024,512]{1,0:T(8,128)(2,1)S(1)} copy-done((bf16[1024,512]{1,0:T(8,128)(2,1)S(1)}, bf16[1024,512]{1,0:T(8,128)(2,1)}, u32[]{:S(2)}) %copy-start) | copy-done | bytes 1048600
  23.6 2.1 %shard_map.67 = (bf16[512,512]{1,0:T(8,128)(2,1)S(1)}, s32[256,128]{1,0:T(8,128)S(1)}, f32[128,128]{1,0:T(8,128)S(1)}, f32[128,128]{1,0:T(8,128)S(1)}) custom-call(bf16[256,640]{1,0:T(8,128)(2,1)S(1)} %constant_dynamic-update-slice_fusion.refs_0_, bf16[256,640]{1,0:T(8,128)(2,1)S(1)} %collective-permute-done.6.refs_1_, bf16[1024,512]{1,0:T(8,128)(2,1)S(1)} %copy-done), custom_call_target="tpu_custom_call" | custom-call | flops 536870912 | bytes 2490368 | tf_op jit(solution)/shard_map/pallas_call | solution.py:245
  25.9 1.1 %collective-permute-done.7 = f32[128,128]{1,0:T(8,128)S(1)} collective-permute-done((f32[128,128]{1,0:T(8,128)S(1)}, f32[128,128]{1,0:T(8,128)S(1)}, u32[]{:S(2)}, u32[]{:S(2)}) %collective-permute-start.7) | collective-permute-done | bytes 65568 | tf_op jit(solution)/shard_map/ppermute | solution.py:16
  27.0 1.8 %collective-permute-start.8 = (f32[128,128]{1,0:T(8,128)S(1)}, f32[128,128]{1,0:T(8,128)S(1)}, u32[]{:S(2)}, u32[]{:S(2)}) collective-permute-start(f32[128,128]{1,0:T(8,128)S(1)} %add.37), channel_id=1, source_target_pairs={{0,4},{4,0},{8,12},{12,8},{1,5},{5,1},{9,13},{13,9},{2,6},{6,2},{1... | collective-permute-start | bytes 196616 | tf_op jit(solution)/shard_map/ppermute | solution.py:16
  28.8 2.5 %collective-permute-done.8 = f32[128,128]{1,0:T(8,128)S(1)} collective-permute-done((f32[128,128]{1,0:T(8,128)S(1)}, f32[128,128]{1,0:T(8,128)S(1)}, u32[]{:S(2)}, u32[]{:S(2)}) %collective-permute-start.8) | collective-permute-done | bytes 65568 | tf_op jit(solution)/shard_map/ppermute | solution.py:16
  31.9 3.8 %collective-permute-done.9 = f32[128,128]{1,0:T(8,128)S(1)} collective-permute-done((f32[128,128]{1,0:T(8,128)S(1)}, f32[128,128]{1,0:T(8,128)S(1)}, u32[]{:S(2)}, u32[]{:S(2)}) %collective-permute-start.9) | collective-permute-done | bytes 65568 | tf_op jit(solution)/shard_map/ppermute | solution.py:16
  35.7 2.3 %collective-permute-start.12 = (f32[128,128]{1,0:T(8,128)S(1)}, f32[128,128]{1,0:T(8,128)S(1)}, u32[]{:S(2)}, u32[]{:S(2)}) collective-permute-start(f32[128,128]{1,0:T(8,128)S(1)} %add.39), channel_id=1, source_target_pairs={{0,3},{1,2},{2,1},{3,0},{4,7},{5,6},{6,5},{7,4},{8,11},{9,10},{10,... | collective-permute-start | bytes 196616 | tf_op jit(solution)/shard_map/ppermute | solution.py:16
  38.0 2.1 %collective-permute-start.10 = (f32[128,128]{1,0:T(8,128)S(1)}, f32[128,128]{1,0:T(8,128)S(1)}, u32[]{:S(2)}, u32[]{:S(2)}) collective-permute-start(f32[128,128]{1,0:T(8,128)S(1)} %add.39), channel_id=1, source_target_pairs={{0,1},{1,0},{2,3},{3,2},{4,5},{5,4},{6,7},{7,6},{8,9},{9,8},{10,11... | collective-permute-start | bytes 196616 | tf_op jit(solution)/shard_map/ppermute | solution.py:16
  40.2 1.7 %collective-permute-done.12 = f32[128,128]{1,0:T(8,128)S(1)} collective-permute-done((f32[128,128]{1,0:T(8,128)S(1)}, f32[128,128]{1,0:T(8,128)S(1)}, u32[]{:S(2)}, u32[]{:S(2)}) %collective-permute-start.12) | collective-permute-done | bytes 65568 | tf_op jit(solution)/shard_map/ppermute | solution.py:16
  41.9 1.5 %collective-permute-done.11 = f32[128,128]{1,0:T(8,128)S(1)} collective-permute-done((f32[128,128]{1,0:T(8,128)S(1)}, f32[128,128]{1,0:T(8,128)S(1)}, u32[]{:S(2)}, u32[]{:S(2)}) %collective-permute-start.11) | collective-permute-done | bytes 65568 | tf_op jit(solution)/shard_map/ppermute | solution.py:16
  43.5 1.2 %collective-permute-done.13.refs_1_ = f32[128,128]{1,0:T(8,128)S(1)} collective-permute-done((f32[128,128]{1,0:T(8,128)S(1)}, f32[128,128]{1,0:T(8,128)S(1)}, u32[]{:S(2)}, u32[]{:S(2)}) %collective-permute-start.13) | collective-permute-done | bytes 65568 | tf_op jit(solution)/shard_map/ppermute | solution.py:16
  44.8 9.5 %shard_map.68 = (bf16[512,1024]{1,0:T(8,128)(2,1)S(1)}, f32[16,128]{1,0:T(8,128)S(1)}, f32[256,512]{1,0:T(8,128)S(1)}, f32[256,512]{1,0:T(8,128)S(1)}) custom-call(f32[128,128]{1,0:T(8,128)S(1)} %add_add_fusion.refs_0_, f32[128,128]{1,0:T(8,128)S(1)} %collective-permute-done.13.refs_1_, s32[256,128]{1,0:T(8,128)S(1)} %get-tuple-element.13.refs_2_, ...), custom_call_target="tpu_custom_call" | custom-call | flops 1073741824 | bytes 3416064 | tf_op jit(solution)/shard_map/pallas_call | solution.py:245
  54.6 1.7 %collective-permute-done.14 = f32[256,512]{1,0:T(8,128)S(1)} collective-permute-done((f32[256,512]{1,0:T(8,128)S(1)}, f32[256,512]{1,0:T(8,128)S(1)}, u32[]{:S(2)}, u32[]{:S(2)}) %collective-permute-start.14) | collective-permute-done | bytes 524320 | tf_op jit(solution)/shard_map/ppermute | solution.py:16
  56.2 0.9 %add.43 = f32[256,512]{1,0:T(8,128)} add(f32[256,512]{1,0:T(8,128)S(1)} %get-tuple-element.14, f32[256,512]{1,0:T(8,128)S(1)} %collective-permute-done.14) | non-fusion elementwise | flops 131072 | bytes 1572864 | tf_op jit(solution)/shard_map/add | solution.py:31
  57.1 4.6 %all-to-all-start = ((f32[16,16,512]{2,1,0:T(8,128)}), f32[16,16,512]{2,1,0:T(8,128)S(1)}, u32[]{:S(2)}, u32[]{:S(2)}) async-start(f32[16,16,512]{2,1,0:T(8,128)} %bitcast), calls=%async_computation | async-start | bytes 1048576 | tf_op jit(solution)/shard_map/all_to_all | solution.py:311
  61.8 2.7 %shard_map.70 = f32[1024,512]{1,0:T(8,128)} custom-call(bf16[512,1024]{1,0:T(8,128)(2,1)S(1)} %get-tuple-element.17.refs_0_, bf16[512,512]{1,0:T(8,128)(2,1)S(1)} %get-tuple-element.18.refs_1_), custom_call_target="tpu_custom_call" | custom-call | flops 536870912 | bytes 3670016 | tf_op jit(solution)/shard_map/pallas_call | solution.py:245
  65.1 13.3 %all-to-all-done.refs_0_ = f32[16,16,512]{2,1,0:T(8,128)S(1)} async-done(((f32[16,16,512]{2,1,0:T(8,128)}), f32[16,16,512]{2,1,0:T(8,128)S(1)}, u32[]{:S(2)}, u32[]{:S(2)}) %all-to-all-start) | async-done | bytes 524320 | tf_op jit(solution)/shard_map/all_to_all | solution.py:311
  (33 shorter events, 7.1 us)
Async XLA Ops:
  0.6 44.1 %copy-start.1 = (bf16[1024,512]{1,0:T(8,128)(2,1)S(1)}, bf16[1024,512]{1,0:T(8,128)(2,1)}, u32[]{:S(2)}) copy-start(bf16[1024,512]{1,0:T(8,128)(2,1)} %refs_3_.1) | copy-start | bytes 3145732
  3.1 5.7 %collective-permute-start.2 = (bf16[16,640]{1,0:T(8,128)(2,1)S(1)}, bf16[16,640]{1,0:T(8,128)(2,1)S(1)}, u32[]{:S(2)}, u32[]{:S(2)}) collective-permute-start(bf16[16,640]{1,0:T(8,128)(2,1)S(1)} %get-tuple-element.25), channel_id=1, source_target_pairs={{0,12},{4,8},{8,4},{12,0},{1,13},{5,9},{9,5},{13,1},{2,14},{6,10},... | collective-permute-start | bytes 61448 | tf_op jit(solution)/shard_map/ppermute | solution.py:16
  7.0 3.8 %collective-permute-start = (bf16[16,640]{1,0:T(8,128)(2,1)S(1)}, bf16[16,640]{1,0:T(8,128)(2,1)S(1)}, u32[]{:S(2)}, u32[]{:S(2)}) collective-permute-start(bf16[16,640]{1,0:T(8,128)(2,1)S(1)} %get-tuple-element.26), channel_id=1, source_target_pairs={{0,4},{4,0},{8,12},{12,8},{1,5},{5,1},{9,13},{13,9},{2,6},{6,2},{1... | collective-permute-start | bytes 61448 | tf_op jit(solution)/shard_map/ppermute | solution.py:16
  7.5 3.8 %collective-permute-start.1 = (bf16[16,640]{1,0:T(8,128)(2,1)S(1)}, bf16[16,640]{1,0:T(8,128)(2,1)S(1)}, u32[]{:S(2)}, u32[]{:S(2)}) collective-permute-start(bf16[16,640]{1,0:T(8,128)(2,1)S(1)} %get-tuple-element.27), channel_id=1, source_target_pairs={{0,8},{4,12},{8,0},{12,4},{1,9},{5,13},{9,1},{13,5},{2,10},{6,14},... | collective-permute-start | bytes 61448 | tf_op jit(solution)/shard_map/ppermute | solution.py:16
  11.4 9.3 %collective-permute-start.5 = (bf16[64,640]{1,0:T(8,128)(2,1)S(1)}, bf16[64,640]{1,0:T(8,128)(2,1)S(1)}, u32[]{:S(2)}, u32[]{:S(2)}) collective-permute-start(bf16[64,640]{1,0:T(8,128)(2,1)S(1)} %pad_maximum_fusion), channel_id=1, source_target_pairs={{0,3},{1,2},{2,1},{3,0},{4,7},{5,6},{6,5},{7,4},{8,11},{9,10},{10,... | collective-permute-start | bytes 245768 | tf_op jit(solution)/shard_map/ppermute | solution.py:16
  15.0 5.6 %collective-permute-start.4 = (bf16[64,640]{1,0:T(8,128)(2,1)S(1)}, bf16[64,640]{1,0:T(8,128)(2,1)S(1)}, u32[]{:S(2)}, u32[]{:S(2)}) collective-permute-start(bf16[64,640]{1,0:T(8,128)(2,1)S(1)} %pad_maximum_fusion), channel_id=1, source_target_pairs={{0,2},{1,3},{2,0},{3,1},{4,6},{5,7},{6,4},{7,5},{8,10},{9,11},{10,... | collective-permute-start | bytes 245768 | tf_op jit(solution)/shard_map/ppermute | solution.py:16
  15.0 4.5 %collective-permute-start.3 = (bf16[64,640]{1,0:T(8,128)(2,1)S(1)}, bf16[64,640]{1,0:T(8,128)(2,1)S(1)}, u32[]{:S(2)}, u32[]{:S(2)}) collective-permute-start(bf16[64,640]{1,0:T(8,128)(2,1)S(1)} %pad_maximum_fusion), channel_id=1, source_target_pairs={{0,1},{1,0},{2,3},{3,2},{4,5},{5,4},{6,7},{7,6},{8,9},{9,8},{10,11... | collective-permute-start | bytes 245768 | tf_op jit(solution)/shard_map/ppermute | solution.py:16
  20.7 1.7 %collective-permute-start.6 = (bf16[256,640]{1,0:T(8,128)(2,1)S(1)}, bf16[256,640]{1,0:T(8,128)(2,1)S(1)}, u32[]{:S(2)}, u32[]{:S(2)}) collective-permute-start(bf16[256,640]{1,0:T(8,128)(2,1)S(1)} %constant_dynamic-update-slice_fusion.refs_0_), channel_id=1, source_target_pairs={{0,16},{16,0},{1,17},{17,1},{2,18},{18,2},{3,19},{19,3},{4,20},{20... | collective-permute-start | bytes 983048 | tf_op jit(solution)/shard_map/ppermute | solution.py:16
  22.4 1.2 %copy-start = (bf16[1024,512]{1,0:T(8,128)(2,1)S(1)}, bf16[1024,512]{1,0:T(8,128)(2,1)}, u32[]{:S(2)}) copy-start(bf16[1024,512]{1,0:T(8,128)(2,1)} %refs_3_.1) | copy-start | bytes 3145732
  25.7 1.3 %collective-permute-start.7 = (f32[128,128]{1,0:T(8,128)S(1)}, f32[128,128]{1,0:T(8,128)S(1)}, u32[]{:S(2)}, u32[]{:S(2)}) collective-permute-start(f32[128,128]{1,0:T(8,128)S(1)} %get-tuple-element.12), channel_id=1, source_target_pairs={{0,16},{16,0},{1,17},{17,1},{2,18},{18,2},{3,19},{19,3},{4,20},{20... | collective-permute-start | bytes 196616 | tf_op jit(solution)/shard_map/ppermute | solution.py:16
  27.0 4.3 %collective-permute-start.8 = (f32[128,128]{1,0:T(8,128)S(1)}, f32[128,128]{1,0:T(8,128)S(1)}, u32[]{:S(2)}, u32[]{:S(2)}) collective-permute-start(f32[128,128]{1,0:T(8,128)S(1)} %add.37), channel_id=1, source_target_pairs={{0,4},{4,0},{8,12},{12,8},{1,5},{5,1},{9,13},{13,9},{2,6},{6,2},{1... | collective-permute-start | bytes 196616 | tf_op jit(solution)/shard_map/ppermute | solution.py:16
  31.4 4.3 %collective-permute-start.9 = (f32[128,128]{1,0:T(8,128)S(1)}, f32[128,128]{1,0:T(8,128)S(1)}, u32[]{:S(2)}, u32[]{:S(2)}) collective-permute-start(f32[128,128]{1,0:T(8,128)S(1)} %add.38), channel_id=1, source_target_pairs={{0,8},{4,12},{8,0},{12,4},{1,9},{5,13},{9,1},{13,5},{2,10},{6,14},... | collective-permute-start | bytes 196616 | tf_op jit(solution)/shard_map/ppermute | solution.py:16
  35.7 6.1 %collective-permute-start.12 = (f32[128,128]{1,0:T(8,128)S(1)}, f32[128,128]{1,0:T(8,128)S(1)}, u32[]{:S(2)}, u32[]{:S(2)}) collective-permute-start(f32[128,128]{1,0:T(8,128)S(1)} %add.39), channel_id=1, source_target_pairs={{0,3},{1,2},{2,1},{3,0},{4,7},{5,6},{6,5},{7,4},{8,11},{9,10},{10,... | collective-permute-start | bytes 196616 | tf_op jit(solution)/shard_map/ppermute | solution.py:16
  38.0 5.4 %collective-permute-start.11 = (f32[128,128]{1,0:T(8,128)S(1)}, f32[128,128]{1,0:T(8,128)S(1)}, u32[]{:S(2)}, u32[]{:S(2)}) collective-permute-start(f32[128,128]{1,0:T(8,128)S(1)} %add.39), channel_id=1, source_target_pairs={{0,2},{1,3},{2,0},{3,1},{4,6},{5,7},{6,4},{7,5},{8,10},{9,11},{10,... | collective-permute-start | bytes 196616 | tf_op jit(solution)/shard_map/ppermute | solution.py:16
  38.0 5.4 %collective-permute-start.10 = (f32[128,128]{1,0:T(8,128)S(1)}, f32[128,128]{1,0:T(8,128)S(1)}, u32[]{:S(2)}, u32[]{:S(2)}) collective-permute-start(f32[128,128]{1,0:T(8,128)S(1)} %add.39), channel_id=1, source_target_pairs={{0,1},{1,0},{2,3},{3,2},{4,5},{5,4},{6,7},{7,6},{8,9},{9,8},{10,11... | collective-permute-start | bytes 196616 | tf_op jit(solution)/shard_map/ppermute | solution.py:16
  43.4 1.3 %collective-permute-start.13 = (f32[128,128]{1,0:T(8,128)S(1)}, f32[128,128]{1,0:T(8,128)S(1)}, u32[]{:S(2)}, u32[]{:S(2)}) collective-permute-start(f32[128,128]{1,0:T(8,128)S(1)} %add_add_fusion.refs_0_), channel_id=1, source_target_pairs={{0,16},{16,0},{1,17},{17,1},{2,18},{18,2},{3,19},{19,3},{4,20},{20... | collective-permute-start | bytes 196616 | tf_op jit(solution)/shard_map/ppermute | solution.py:16
  54.3 2.0 %collective-permute-start.14 = (f32[256,512]{1,0:T(8,128)S(1)}, f32[256,512]{1,0:T(8,128)S(1)}, u32[]{:S(2)}, u32[]{:S(2)}) collective-permute-start(f32[256,512]{1,0:T(8,128)S(1)} %get-tuple-element.15), channel_id=1, source_target_pairs={{0,16},{16,0},{1,17},{17,1},{2,18},{18,2},{3,19},{19,3},{4,20},{20... | collective-permute-start | bytes 1572872 | tf_op jit(solution)/shard_map/ppermute | solution.py:16
  57.1 21.3 %all-to-all-start = ((f32[16,16,512]{2,1,0:T(8,128)}), f32[16,16,512]{2,1,0:T(8,128)S(1)}, u32[]{:S(2)}, u32[]{:S(2)}) async-start(f32[16,16,512]{2,1,0:T(8,128)} %bitcast), calls=%async_computation | async-start | bytes 1048576 | tf_op jit(solution)/shard_map/all_to_all | solution.py:311

commit v2 on v1

--- a/solution.py
+++ b/solution.py
@@ -32,6 +32,10 @@
         ]
         bit //= 2
     return pieces[0]
+
+
+def turn_order(size):
+    return [1] + list(range(size - 1, 1, -1))
 
 
 class Sizes:
@@ -55,15 +59,71 @@
         self.pos_at = 0 if self.neg_at else self.negs
         self.chunks = self.block // LANES
         self.scale = self.feat ** (-0.5)
+        self.deep = 2 * LANES
+        self.seats = self.deep // self.negs
+        self.nrows = self.rows // self.seats
+        self.joint = max(1, self.deep // self.columns)
+        self.run = self.joint * self.own
+        self.sets = self.groups // self.joint
         self.vmem = min(60, 16 + 10 * self.rows // 1024) * 2**20
+
+
+def message_kernel(z, pos_in, neg_in, query_in, *refs):
+    piece_refs = refs[: z.tensor]
+    pos_ref, neg_ref, query_ref, sems = refs[z.tensor :]
+    t = lax.axis_index("tensor")
+    moves = [
+        pltpu.make_async_copy(source, target, sems.at[i])
+        for i, (source, target) in enumerate(
+            [(pos_in, pos_ref), (neg_in, neg_ref), (query_in, query_ref)]
+        )
+    ]
+    for move in moves:
+        move.start()
+    for move in moves:
+        move.wait()
+    half = LANES // 2
+    row = lax.broadcasted_iota(jnp.int32, (z.own, half), 0)
+    pos = jnp.zeros((z.own, half), jnp.int32)
+    for i in range(z.own):
+        pos = jnp.where(row == i, pos_ref[i], pos)
+    ids = [neg_ref[...], pos[:, : half - z.neg_at - z.negs]]
+    ids = jnp.concatenate([part for part in [pos[:, : z.neg_at]] + ids if part.shape[1]], axis=1)
+    ids = jnp.concatenate([ids >> 8, ids & 255], axis=1)
+    code = ids.astype(jnp.float32).astype(jnp.bfloat16)
+    for s in range(z.tensor):
+        at = pl.ds(pl.multiple_of((t ^ s) * z.width, LANES), z.width)
+        piece_refs[s][:, : z.width] = query_ref[:, at]
+        piece_refs[s][:, z.width :] = code
+
+
+def fetch_kernel(z, block_ref, passage_ref, sem):
+    fetch = pltpu.make_async_copy(block_ref, passage_ref, sem)
+    fetch.start()
+    fetch.wait()
+
+
+def seat_rows(z, out_ref, source):
+    lane = lax.broadcasted_iota(jnp.int32, (z.nrows, LANES), 1)
+    per = LANES // z.negs
+    for chunk in range(z.deep // LANES):
+        packed = None
+        for k in range(per):
+            ref, row, at = source(chunk * per + k)
+            base = at // LANES * LANES
+            piece = ref[pl.ds(row, z.nrows), base : base + LANES]
+            turn = (k * z.negs - at) % LANES
+            piece = pltpu.roll(piece, turn, 1) if turn else piece
+            packed = piece if packed is None else jnp.where(lane < k * z.negs, packed, piece)
+        out_ref[:, chunk * LANES : (chunk + 1) * LANES] = packed
 
 
 def score_kernel(z, *refs):
     arrived = refs[: z.dp]
     passage_ref = refs[z.dp]
-    query_ref, index_ref = refs[z.dp + 1 : z.dp + 3]
-    part_refs = refs[z.dp + 3 : 2 * z.dp + 3]
-    id_ref, local_ref, logit_ref = refs[2 * z.dp + 3 :]
+    query_ref, index_ref, pos_ref = refs[z.dp + 1 : z.dp + 4]
+    part_refs = refs[z.dp + 4 : 2 * z.dp + 4]
+    id_ref, local_ref, logit_ref = refs[2 * z.dp + 4 :]
     d, t, c = (lax.axis_index(a) for a in ("dp", "tensor", "corpus"))
     for sd in range(z.dp):
         for sc in range(z.corpus):
@@ -82,6 +142,7 @@
     for h in range(z.dp):
         ids = id_ref[pl.ds(h * z.half, z.half), :]
         pos = jnp.broadcast_to(ids[:, z.pos_at : z.pos_at + 1], (z.half, wide))
+        pos_ref[pl.ds(h * z.half, z.half), :] = (pos[:, :LANES] - first).astype(jnp.int32)
         kept = jnp.where(col == row + h * z.own, pos, 0.0)
         group_ids += jnp.sum(kept.reshape(z.groups, z.own, wide), axis=1)
     batch_ids = jnp.broadcast_to(group_ids[:, None, :], (z.groups, z.own, wide))
@@ -117,12 +178,7 @@
         return carry
 
     lax.fori_loop(0, z.rows // step, score, 0)
-    lane = lax.broadcasted_iota(jnp.int32, (z.packed, z.lanes), 1)
-    index = local_ref[pl.ds(0, z.packed), :]
-    for h in range(1, z.pack):
-        other = pltpu.roll(local_ref[pl.ds(h * z.packed, z.packed), :], h * z.items, 1)
-        index = jnp.where(lane < h * z.items, index, other)
-    index_ref[...] = index
+    seat_rows(z, index_ref, lambda j: (local_ref, j * z.nrows, z.columns))
     for s in range(z.dp):
         at = pl.multiple_of((d ^ s) * z.part, z.part)
         total = logit_ref[pl.ds(at, z.part), :]
@@ -134,10 +190,10 @@
 
 def weight_kernel(z, *refs):
     parts = refs[: z.dp]
-    index_ref, passage_ref = refs[z.dp : z.dp + 2]
-    dense_ref, loss_ref = refs[z.dp + 2 : z.dp + 4]
-    grad_refs = refs[z.dp + 4 : 2 * z.dp + 4]
-    logit_ref, tile_ref = refs[2 * z.dp + 4 :]
+    index_ref, hot_ref, passage_ref = refs[z.dp : z.dp + 3]
+    dense_ref, loss_ref = refs[z.dp + 3 : z.dp + 5]
+    grad_refs = refs[z.dp + 5 : 2 * z.dp + 5]
+    logit_ref, seat_ref, tile_ref = refs[2 * z.dp + 5 :]
     d, t, c = (lax.axis_index(a) for a in ("dp", "tensor", "corpus"))
     for s in range(z.dp):
         at = pl.multiple_of((d ^ s) * z.part, z.part)
@@ -180,43 +236,82 @@
 
     lax.fori_loop(0, z.packed // step, weigh, 0)
 
-    high = z.pack * z.chunks
-    tall = lax.broadcasted_iota(jnp.int32, (high, z.lanes), 0)
-    shift = lax.broadcasted_iota(jnp.int32, (1, z.lanes), 1) // z.items * z.chunks
-    spread = lax.broadcasted_iota(jnp.int32, (LANES, z.lanes), 0).astype(jnp.bfloat16)
+    def seat(j):
+        h, row = divmod(j * z.nrows, z.packed)
+        return logit_ref, row, h * z.items + z.columns
+
+    seat_rows(z, seat_ref, seat)
+    high = z.seats * z.chunks
+    tall = lax.broadcasted_iota(jnp.int32, (high, z.deep), 0)
+    shift = lax.broadcasted_iota(jnp.int32, (1, z.deep), 1) // z.negs * z.chunks
+    spread = lax.broadcasted_iota(jnp.int32, (LANES, z.deep), 0).astype(jnp.bfloat16)
+    turns = 16
 
     def place(i, carry):
-        for j in range(8):
-            r = i * 8 + j
+        for k in range(turns):
+            r = i * turns + k
             local = index_ref[pl.ds(r, 1), :]
             chunk = (local >> 7) + shift
             within = (local & (LANES - 1)).astype(jnp.bfloat16)
             left = jnp.where(
-                jnp.broadcast_to(chunk, (high, z.lanes)) == tall,
-                jnp.broadcast_to(logit_ref[pl.ds(r, 1), :], (high, z.lanes)), 0.0,
+                jnp.broadcast_to(chunk, (high, z.deep)) == tall,
+                jnp.broadcast_to(seat_ref[pl.ds(r, 1), :], (high, z.deep)), 0.0,
             ).astype(jnp.bfloat16)
             right = jnp.where(
-                jnp.broadcast_to(within, (LANES, z.lanes)) == spread,
+                jnp.broadcast_to(within, (LANES, z.deep)) == spread,
                 jnp.bfloat16(1), jnp.bfloat16(0),
             )
             tiles = lax.dot_general(
                 left, right, (((1,), (1,)), ((), ())), preferred_element_type=jnp.float32
             )
-            for h in range(z.pack):
-                at = pl.multiple_of((h * z.packed + r) * z.chunks, z.chunks)
-                tile_ref[pl.ds(at, z.chunks), :] = tiles[h * z.chunks : (h + 1) * z.chunks, :]
+            for j in range(z.seats):
+                at = pl.multiple_of((j * z.nrows + r) * z.chunks, z.chunks)
+                tile_ref[pl.ds(at, z.chunks), :] = tiles[j * z.chunks : (j + 1) * z.chunks, :]
         return carry
 
-    lax.fori_loop(0, z.packed // 8, place, 0)
-    for j in range(z.chunks):
-        dense_ref[:, j * LANES : (j + 1) * LANES] = tile_ref[
-            pl.ds(j, z.rows, stride=z.chunks), :
-        ].astype(jnp.bfloat16)
+    lax.fori_loop(0, z.nrows // turns, place, 0)
+    lane = lax.broadcasted_iota(jnp.int32, (z.run, LANES), 1)
+    group = lax.broadcasted_iota(jnp.int32, (z.run, LANES), 0) // z.own
+    for n in range(z.sets):
+        spans = [pl.ds(h * z.half + n * z.run, z.run) for h in range(z.dp)]
+        hot = jnp.concatenate([hot_ref[span, :] for span in spans], axis=0)
+        for h in range(z.dp):
+            first_row = h * z.half + n * z.run
+            side, row = divmod(first_row, z.packed)
+            left = []
+            for chunk in range(z.deep // LANES):
+                if z.joint == 1:
+                    part = logit_ref[pl.ds(row, z.run), chunk * LANES : (chunk + 1) * LANES]
+                else:
+                    at = chunk * LANES + lane
+                    from_lane = side * z.items + at // z.run * z.own + at % z.own
+                    part = jnp.take_along_axis(
+                        logit_ref[pl.ds(row, z.run), :LANES], from_lane, axis=1
+                    )
+                    part = jnp.where(at // z.own % z.joint == group, part, 0.0)
+                left.append(part.astype(jnp.bfloat16))
+            shared = jnp.dot(
+                jnp.concatenate(left, axis=1), hot, preferred_element_type=jnp.float32
+            )
+            for j in range(z.chunks):
+                alone = tile_ref[pl.ds(first_row * z.chunks + j, z.run, stride=z.chunks), :]
+                dense_ref[spans[h], j * LANES : (j + 1) * LANES] = (
+                    alone + shared[:, j * LANES : (j + 1) * LANES]
+                ).astype(jnp.bfloat16)
     for s in range(z.dp):
         at = pl.multiple_of((d ^ s) * z.half, z.half)
         grad_refs[s][...] = jnp.dot(
             dense_ref[pl.ds(at, z.half), :], passage_ref[...], preferred_element_type=jnp.float32
         )
+
+
+def hot_kernel(z, pos_ref, hot_ref):
+    lane = lax.broadcasted_iota(jnp.int32, (z.half, LANES), 1)
+    for h in range(z.dp):
+        at = pl.ds(h * z.half, z.half)
+        for j in range(z.chunks):
+            same = pos_ref[at, :] == lane + j * LANES
+            hot_ref[at, j * LANES : (j + 1) * LANES] = jnp.where(same, 1.0, 0.0).astype(jnp.bfloat16)
 
 
 def passage_kernel(z, dense_ref, query_ref, out_ref):
@@ -239,16 +334,17 @@
         out_ref[:, t * z.width : (t + 1) * z.width] = total * z.scale
 
 
-def call(z, kernel, outs, scratch, args, flops):
+def call(z, kernel, outs, scratch, args, flops, spaces=None, vmem=None):
+    spaces = spaces or [pltpu.VMEM] * len(args)
     moved = sum(a.size * a.dtype.itemsize for a in args)
     moved += sum(o.size * jnp.dtype(o.dtype).itemsize for o in outs)
     return pl.pallas_call(
         lambda *refs: kernel(z, *refs),
         out_shape=outs,
-        in_specs=[pl.BlockSpec(memory_space=pltpu.VMEM)] * len(args),
+        in_specs=[pl.BlockSpec(memory_space=space) for space in spaces],
         out_specs=[pl.BlockSpec(memory_space=pltpu.VMEM)] * len(outs),
         scratch_shapes=scratch,
-        compiler_params=pltpu.CompilerParams(vmem_limit_bytes=z.vmem),
+        compiler_params=pltpu.CompilerParams(vmem_limit_bytes=vmem or z.vmem),
         cost_estimate=pl.CostEstimate(flops=flops, bytes_accessed=moved, transcendentals=0),
     )(*args)
 
@@ -257,26 +353,37 @@
     z = Sizes(queries, passages, neg_ids)
     f32, bf16 = jnp.float32, jnp.bfloat16
     shape = jax.ShapeDtypeStruct
-    t = lax.axis_index("tensor")
-
-    pos = jnp.broadcast_to(pos_ids[:, None], (z.own, LANES // 2))
-    ids = jnp.concatenate(
-        [pos[:, : z.neg_at], neg_ids, pos[:, : LANES // 2 - z.neg_at - z.negs]], axis=1
-    )
-    code = jnp.concatenate([ids >> 8, ids & 255], axis=1).astype(bf16)
-    plane = []
-    for s in range(z.tensor):
-        piece = lax.dynamic_slice_in_dim(queries, (t ^ s) * z.width, z.width, axis=1)
-        piece = jnp.concatenate([piece, code], axis=1)
-        plane.append(swap(piece, "tensor", s) if s else piece)
+
+    pieces = call(
+        z, message_kernel, [shape((z.own, z.width + LANES), bf16)] * z.tensor,
+        [
+            pltpu.SMEM(pos_ids.shape, jnp.int32), pltpu.VMEM(neg_ids.shape, jnp.int32),
+            pltpu.VMEM(queries.shape, bf16), pltpu.SemaphoreType.DMA((3,)),
+        ],
+        [pos_ids, neg_ids, queries], 0, [pltpu.HBM] * 3, 60 * 2**20,
+    )
+    passages, pieces = lax.optimization_barrier((passages, pieces))
+    (passages,) = call(
+        z, fetch_kernel, [shape(passages.shape, bf16)], [pltpu.SemaphoreType.DMA],
+        [passages], 0, [pltpu.HBM],
+    )
+    plane = [None] * z.tensor
+    for s in range(1, z.tensor):
+        plane[s] = swap(pieces[s], "tensor", s)
+    plane[0] = pieces[0]
     plane = jnp.concatenate(plane, axis=0)
-    chip = [plane] + [swap(plane, "corpus", s) for s in range(1, z.corpus)]
+    chip = [plane] * z.corpus
+    for s in range(1, z.corpus):
+        chip[s] = swap(plane, "corpus", s)
     arrived = gather_pieces([jnp.concatenate(chip, axis=0)], "dp")
 
     work = 2 * z.rows * z.block * z.width
-    query_rows, index, *parts = call(
+    query_rows, index, pos_rows, *parts = call(
         z, score_kernel,
-        [shape((z.rows, z.width), bf16), shape((z.packed, z.lanes), jnp.int32)]
+        [
+            shape((z.rows, z.width), bf16), shape((z.nrows, z.deep), jnp.int32),
+            shape((z.rows, LANES), jnp.int32),
+        ]
         + [shape((z.part, z.lanes), f32)] * z.dp,
         [
             pltpu.VMEM((z.rows, LANES), f32),
@@ -285,12 +392,13 @@
         ],
         arrived + [passages], work,
     )
+    (hot,) = call(z, hot_kernel, [shape((z.rows, z.block), bf16)], [], [pos_rows], z.rows * z.block)
     total = scatter_sum(parts, "dp")
     bit = 1
     while bit < z.tensor:
         total = total + swap(total, "tensor", bit)
         bit *= 2
-    total = sum([swap(total, "corpus", s) for s in range(1, z.corpus)], total)
+    total = sum([swap(total, "corpus", s) for s in turn_order(z.corpus)], total)
     logits = gather_pieces([total], "dp")
 
     dense, loss, *grads = call(
@@ -299,9 +407,10 @@
         + [shape((z.half, z.width), f32)] * z.dp,
         [
             pltpu.VMEM((z.packed, z.lanes), f32),
+            pltpu.VMEM((z.nrows, z.deep), f32),
             pltpu.VMEM((z.rows * z.chunks, LANES), f32),
         ],
-        logits + [index, passages], 2 * work,
+        logits + [index, hot, passages], 2 * work,
     )
     (grad_pass,) = call(
         z, passage_kernel, [shape((z.block, z.width), f32)], [], [dense, query_rows], work

time: 79.4 us -> 72.4 us (0.912)
  Pallas kernels: 14.9 us -> 11.1 us
  starting transfers between devices: 21 us -> 17.6 us
  waiting for transfers between devices: 37 us -> 38.9 us
  other arithmetic: 1.87 us -> 0.93 us
  local copies, waits for them, and re-layouts: 3.51 us -> 2.65 us
    pallas_call x4 -> x7, Pallas kernels: 14.9 us -> 11.1 us  [call(): pl.pallas_call(lambda *refs: kernel(z, *refs), out_shape=outs, in_specs=[...]
    ppermute x15, starting transfers between devices: 16.3 us -> 14.1 us  [swap(): return lax.ppermute(value, axis, pairs(lax.axis_size(axis), bit))]
    ppermute x15, waiting for transfers between devices: 23.7 us -> 25.5 us  [swap(): return lax.ppermute(value, axis, pairs(lax.axis_size(axis), bit))]
    all_to_all x1, starting transfers between devices: 4.65 us -> 3.57 us  [body(): lax.all_to_all(half, ('tensor', 'corpus'), split_axis=0, concat_axis=0, t...]
    slice x1 -> x0, local copies, waits for them, and re-layouts: 0.81 us -> none  [body(): pos[:, :z.neg_at]]
    unnamed x9 -> x7, local copies, waits for them, and re-layouts: 1.28 us -> 2 us
  transfers between devices with their start and end apart: 16 -> 16, of which waited for: 14 -> 14; matrix products, arithmetic and copies ran while one was open for 1% -> 2% of each run, Pallas kernels for 3% -> 4%
where the time goes in v2:
time: 72.4 us; the launch traced here: 72 us
  waiting for transfers between devices  38.9 us (54%)
  starting transfers between devices  17.6 us (24%)
  Pallas kernels  11.1 us (15%)
  local copies, waits for them, and re-layouts  2.65 us (4%)
  other arithmetic  0.93 us (1%)
  between operations  0.75 us (1%)
    ppermute x15, waiting for transfers between devices, swap(): return lax.ppermute(value, axis, pairs(lax.axis_size(axis), bit))  25.5 us
    ppermute x15, starting transfers between devices, swap(): return lax.ppermute(value, axis, pairs(lax.axis_size(axis), bit))  14.1 us
    all_to_all x1, waiting for transfers between devices, body(): lax.all_to_all(half, ('tensor', 'corpus'), split_axis=0, concat_axis=0, t...  13.4 us
    pallas_call x7, Pallas kernels, call(): pl.pallas_call(lambda *refs: kernel(z, *refs), out_shape=outs, in_specs=[...  11.1 us
    all_to_all x1, starting transfers between devices, body(): lax.all_to_all(half, ('tensor', 'corpus'), split_axis=0, concat_axis=0, t...  3.57 us
    unnamed x7, local copies, waits for them, and re-layouts  2 us
  transfers between devices with their start and end apart: 16, of which 14 were waited for; matrix products, arithmetic and copies ran while one was open for 2% of the time, Pallas kernels for 4%

profile of v2, /device:TPU:0, one launch (start us, length us, event | category | flops | bytes accessed | tf_op | source)
XLA Modules:
  0.0 72.0 jit_solution(5050453145387164973)
XLA Ops:
  0.6 1.6 %shard_map.67 = (bf16[16,640]{1,0:T(8,128)(2,1)}, bf16[16,640]{1,0:T(8,128)(2,1)}, bf16[16,640]{1,0:T(8,128)(2,1)}, bf16[16,640]{1,0:T(8,128)(2,1)}) custom-call(s32[16]{0:T(128)} %refs_0_.1, s32[16,32]{1,0:T(8,128)} %refs_1_.1, bf16[16,2048]{1,0:T(8,128)(2,1)} %refs_2_.1), custom_call_target="tpu_custom_call" | custom-call | bytes 149568 | tf_op jit(solution)/shard_map/pallas_call | solution.py:341
  2.3 3.0 %collective-permute-start = (bf16[16,640]{1,0:T(8,128)(2,1)}, bf16[16,640]{1,0:T(8,128)(2,1)S(1)}, u32[]{:S(2)}, u32[]{:S(2)}) collective-permute-start(bf16[16,640]{1,0:T(8,128)(2,1)} %get-tuple-element.26), channel_id=1, source_target_pairs={{0,4},{4,0},{8,12},{12,8},{1,5},{5,1},{9,13},{13,9},{2,6},{6,2},{1... | collective-permute-start | bytes 61448 | tf_op jit(solution)/shard_map/ppermute | solution.py:16
  5.3 1.5 %collective-permute-start.1 = (bf16[16,640]{1,0:T(8,128)(2,1)}, bf16[16,640]{1,0:T(8,128)(2,1)S(1)}, u32[]{:S(2)}, u32[]{:S(2)}) collective-permute-start(bf16[16,640]{1,0:T(8,128)(2,1)} %get-tuple-element.27), channel_id=1, source_target_pairs={{0,8},{4,12},{8,0},{12,4},{1,9},{5,13},{9,1},{13,5},{2,10},{6,14},... | collective-permute-start | bytes 61448 | tf_op jit(solution)/shard_map/ppermute | solution.py:16
  7.6 1.7 %collective-permute-done.1 = bf16[16,640]{1,0:T(8,128)(2,1)S(1)} collective-permute-done((bf16[16,640]{1,0:T(8,128)(2,1)}, bf16[16,640]{1,0:T(8,128)(2,1)S(1)}, u32[]{:S(2)}, u32[]{:S(2)}) %collective-permute-start.1) | collective-permute-done | bytes 20512 | tf_op jit(solution)/shard_map/ppermute | solution.py:16
  9.3 2.4 %collective-permute-done.2 = bf16[16,640]{1,0:T(8,128)(2,1)S(1)} collective-permute-done((bf16[16,640]{1,0:T(8,128)(2,1)}, bf16[16,640]{1,0:T(8,128)(2,1)S(1)}, u32[]{:S(2)}, u32[]{:S(2)}) %collective-permute-start.2) | collective-permute-done | bytes 20512 | tf_op jit(solution)/shard_map/ppermute | solution.py:16
  11.7 1.6 %collective-permute-start.3 = (bf16[64,640]{1,0:T(8,128)(2,1)S(1)}, bf16[64,640]{1,0:T(8,128)(2,1)S(1)}, u32[]{:S(2)}, u32[]{:S(2)}) collective-permute-start(bf16[64,640]{1,0:T(8,128)(2,1)S(1)} %get-tuple-element.39), channel_id=1, source_target_pairs={{0,1},{1,0},{2,3},{3,2},{4,5},{5,4},{6,7},{7,6},{8,9},{9,8},{10,11... | collective-permute-start | bytes 245768 | tf_op jit(solution)/shard_map/ppermute | solution.py:16
  13.3 2.5 %collective-permute-start.5 = (bf16[64,640]{1,0:T(8,128)(2,1)S(1)}, bf16[64,640]{1,0:T(8,128)(2,1)S(1)}, u32[]{:S(2)}, u32[]{:S(2)}) collective-permute-start(bf16[64,640]{1,0:T(8,128)(2,1)S(1)} %get-tuple-element.39), channel_id=1, source_target_pairs={{0,3},{1,2},{2,1},{3,0},{4,7},{5,6},{6,5},{7,4},{8,11},{9,10},{10,... | collective-permute-start | bytes 245768 | tf_op jit(solution)/shard_map/ppermute | solution.py:16
  15.9 1.4 %collective-permute-done.3 = bf16[64,640]{1,0:T(8,128)(2,1)S(1)} collective-permute-done((bf16[64,640]{1,0:T(8,128)(2,1)S(1)}, bf16[64,640]{1,0:T(8,128)(2,1)S(1)}, u32[]{:S(2)}, u32[]{:S(2)}) %collective-permute-start.3) | collective-permute-done | bytes 81952 | tf_op jit(solution)/shard_map/ppermute | solution.py:16
  17.3 4.8 %collective-permute-done.4 = bf16[64,640]{1,0:T(8,128)(2,1)S(1)} collective-permute-done((bf16[64,640]{1,0:T(8,128)(2,1)S(1)}, bf16[64,640]{1,0:T(8,128)(2,1)S(1)}, u32[]{:S(2)}, u32[]{:S(2)}) %collective-permute-start.4) | collective-permute-done | bytes 81952 | tf_op jit(solution)/shard_map/ppermute | solution.py:16
  22.2 1.2 %copy-done = bf16[1024,512]{1,0:T(8,128)(2,1)S(1)} copy-done((bf16[1024,512]{1,0:T(8,128)(2,1)S(1)}, bf16[1024,512]{1,0:T(8,128)(2,1)}, u32[]{:S(2)}) %copy-start) | copy-done | bytes 1048600
  23.8 2.1 %shard_map.69 = (bf16[512,512]{1,0:T(8,128)(2,1)S(1)}, s32[64,256]{1,0:T(8,128)S(1)}, s32[512,128]{1,0:T(8,128)S(1)}, f32[128,128]{1,0:T(8,128)S(1)}, f32[128,128]{1,0:T(8,128)S(1)}) custom-call(bf16[256,640]{1,0:T(8,128)(2,1)S(1)} %constant_dynamic-update-slice_fusion.4.refs_0_, bf16[256,640]{1,0:T(8,128)(2,1)S(1)} %collective-permute-done.6.refs_1_, ...), custom_call_target="tpu_custom_call" | custom-call | flops 536870912 | bytes 2686976 | tf_op jit(solution)/shard_map/pallas_call | solution.py:341
  26.2 1.0 %collective-permute-done.7 = f32[128,128]{1,0:T(8,128)S(1)} collective-permute-done((f32[128,128]{1,0:T(8,128)S(1)}, f32[128,128]{1,0:T(8,128)S(1)}, u32[]{:S(2)}, u32[]{:S(2)}) %collective-permute-start.7) | collective-permute-done | bytes 65568 | tf_op jit(solution)/shard_map/ppermute | solution.py:16
  27.9 3.7 %collective-permute-done.8 = f32[128,128]{1,0:T(8,128)S(1)} collective-permute-done((f32[128,128]{1,0:T(8,128)S(1)}, f32[128,128]{1,0:T(8,128)S(1)}, u32[]{:S(2)}, u32[]{:S(2)}) %collective-permute-start.8) | collective-permute-done | bytes 65568 | tf_op jit(solution)/shard_map/ppermute | solution.py:16
  32.2 3.8 %collective-permute-done.9 = f32[128,128]{1,0:T(8,128)S(1)} collective-permute-done((f32[128,128]{1,0:T(8,128)S(1)}, f32[128,128]{1,0:T(8,128)S(1)}, u32[]{:S(2)}, u32[]{:S(2)}) %collective-permute-start.9) | collective-permute-done | bytes 65568 | tf_op jit(solution)/shard_map/ppermute | solution.py:16
  36.4 1.9 %collective-permute-start.11 = (f32[128,128]{1,0:T(8,128)S(1)}, f32[128,128]{1,0:T(8,128)S(1)}, u32[]{:S(2)}, u32[]{:S(2)}) collective-permute-start(f32[128,128]{1,0:T(8,128)S(1)} %add.23), channel_id=1, source_target_pairs={{0,3},{1,2},{2,1},{3,0},{4,7},{5,6},{6,5},{7,4},{8,11},{9,10},{10,... | collective-permute-start | bytes 196616 | tf_op jit(solution)/shard_map/ppermute | solution.py:16
  38.3 1.3 %collective-permute-start.10 = (f32[128,128]{1,0:T(8,128)S(1)}, f32[128,128]{1,0:T(8,128)S(1)}, u32[]{:S(2)}, u32[]{:S(2)}) collective-permute-start(f32[128,128]{1,0:T(8,128)S(1)} %add.23), channel_id=1, source_target_pairs={{0,1},{1,0},{2,3},{3,2},{4,5},{5,4},{6,7},{7,6},{8,9},{9,8},{10,11... | collective-permute-start | bytes 196616 | tf_op jit(solution)/shard_map/ppermute | solution.py:16
  39.5 2.0 %collective-permute-done.12 = f32[128,128]{1,0:T(8,128)S(1)} collective-permute-done((f32[128,128]{1,0:T(8,128)S(1)}, f32[128,128]{1,0:T(8,128)S(1)}, u32[]{:S(2)}, u32[]{:S(2)}) %collective-permute-start.12) | collective-permute-done | bytes 65568 | tf_op jit(solution)/shard_map/ppermute | solution.py:16
  41.5 1.0 %collective-permute-done.11 = f32[128,128]{1,0:T(8,128)S(1)} collective-permute-done((f32[128,128]{1,0:T(8,128)S(1)}, f32[128,128]{1,0:T(8,128)S(1)}, u32[]{:S(2)}, u32[]{:S(2)}) %collective-permute-start.11) | collective-permute-done | bytes 65568 | tf_op jit(solution)/shard_map/ppermute | solution.py:16
  43.5 1.0 %collective-permute-done.13.refs_1_ = f32[128,128]{1,0:T(8,128)S(1)} collective-permute-done((f32[128,128]{1,0:T(8,128)S(1)}, f32[128,128]{1,0:T(8,128)S(1)}, u32[]{:S(2)}, u32[]{:S(2)}) %collective-permute-start.13) | collective-permute-done | bytes 65568 | tf_op jit(solution)/shard_map/ppermute | solution.py:16
  44.5 3.7 %shard_map.71 = (bf16[512,1024]{1,0:T(8,128)(2,1)S(1)}, f32[16,128]{1,0:T(8,128)S(1)}, f32[256,512]{1,0:T(8,128)S(1)}, f32[256,512]{1,0:T(8,128)S(1)}) custom-call(f32[128,128]{1,0:T(8,128)S(1)} %add_add_fusion.refs_0_, f32[128,128]{1,0:T(8,128)S(1)} %collective-permute-done.13.refs_1_, s32[64,256]{1,0:T(8,128)S(1)} %get-tuple-element.32.refs_2_, ...), custom_call_target="tpu_custom_call" | custom-call | flops 1073741824 | bytes 4399104 | tf_op jit(solution)/shard_map/pallas_call | solution.py:341
  48.4 1.8 %collective-permute-done.14 = f32[256,512]{1,0:T(8,128)S(1)} collective-permute-done((f32[256,512]{1,0:T(8,128)S(1)}, f32[256,512]{1,0:T(8,128)S(1)}, u32[]{:S(2)}, u32[]{:S(2)}) %collective-permute-start.14) | collective-permute-done | bytes 524320 | tf_op jit(solution)/shard_map/ppermute | solution.py:16
  51.0 3.6 %all-to-all-start = ((f32[16,16,512]{2,1,0:T(8,128)}), f32[16,16,512]{2,1,0:T(8,128)S(1)}, u32[]{:S(2)}, u32[]{:S(2)}) async-start(f32[16,16,512]{2,1,0:T(8,128)} %bitcast), calls=%async_computation | async-start | bytes 1048576 | tf_op jit(solution)/shard_map/all_to_all | solution.py:420
  54.6 2.7 %shard_map.73 = f32[1024,512]{1,0:T(8,128)} custom-call(bf16[512,1024]{1,0:T(8,128)(2,1)S(1)} %get-tuple-element.37.refs_0_, bf16[512,512]{1,0:T(8,128)(2,1)S(1)} %get-tuple-element.38.refs_1_), custom_call_target="tpu_custom_call" | custom-call | flops 536870912 | bytes 3670016 | tf_op jit(solution)/shard_map/pallas_call | solution.py:341
  57.9 13.4 %all-to-all-done.refs_0_ = f32[16,16,512]{2,1,0:T(8,128)S(1)} async-done(((f32[16,16,512]{2,1,0:T(8,128)}), f32[16,16,512]{2,1,0:T(8,128)S(1)}, u32[]{:S(2)}, u32[]{:S(2)}) %all-to-all-start) | async-done | bytes 524320 | tf_op jit(solution)/shard_map/all_to_all | solution.py:420
  (30 shorter events, 6.7 us)
Async XLA Ops:
  2.3 5.3 %collective-permute-start = (bf16[16,640]{1,0:T(8,128)(2,1)}, bf16[16,640]{1,0:T(8,128)(2,1)S(1)}, u32[]{:S(2)}, u32[]{:S(2)}) collective-permute-start(bf16[16,640]{1,0:T(8,128)(2,1)} %get-tuple-element.26), channel_id=1, source_target_pairs={{0,4},{4,0},{8,12},{12,8},{1,5},{5,1},{9,13},{13,9},{2,6},{6,2},{1... | collective-permute-start | bytes 61448 | tf_op jit(solution)/shard_map/ppermute | solution.py:16
  5.3 4.0 %collective-permute-start.1 = (bf16[16,640]{1,0:T(8,128)(2,1)}, bf16[16,640]{1,0:T(8,128)(2,1)S(1)}, u32[]{:S(2)}, u32[]{:S(2)}) collective-permute-start(bf16[16,640]{1,0:T(8,128)(2,1)} %get-tuple-element.27), channel_id=1, source_target_pairs={{0,8},{4,12},{8,0},{12,4},{1,9},{5,13},{9,1},{13,5},{2,10},{6,14},... | collective-permute-start | bytes 61448 | tf_op jit(solution)/shard_map/ppermute | solution.py:16
  6.8 4.9 %collective-permute-start.2 = (bf16[16,640]{1,0:T(8,128)(2,1)}, bf16[16,640]{1,0:T(8,128)(2,1)S(1)}, u32[]{:S(2)}, u32[]{:S(2)}) collective-permute-start(bf16[16,640]{1,0:T(8,128)(2,1)} %get-tuple-element.28), channel_id=1, source_target_pairs={{0,12},{4,8},{8,4},{12,0},{1,13},{5,9},{9,5},{13,1},{2,14},{6,10},... | collective-permute-start | bytes 61448 | tf_op jit(solution)/shard_map/ppermute | solution.py:16
  11.7 5.5 %collective-permute-start.3 = (bf16[64,640]{1,0:T(8,128)(2,1)S(1)}, bf16[64,640]{1,0:T(8,128)(2,1)S(1)}, u32[]{:S(2)}, u32[]{:S(2)}) collective-permute-start(bf16[64,640]{1,0:T(8,128)(2,1)S(1)} %get-tuple-element.39), channel_id=1, source_target_pairs={{0,1},{1,0},{2,3},{3,2},{4,5},{5,4},{6,7},{7,6},{8,9},{9,8},{10,11... | collective-permute-start | bytes 245768 | tf_op jit(solution)/shard_map/ppermute | solution.py:16
  13.3 8.8 %collective-permute-start.5 = (bf16[64,640]{1,0:T(8,128)(2,1)S(1)}, bf16[64,640]{1,0:T(8,128)(2,1)S(1)}, u32[]{:S(2)}, u32[]{:S(2)}) collective-permute-start(bf16[64,640]{1,0:T(8,128)(2,1)S(1)} %get-tuple-element.39), channel_id=1, source_target_pairs={{0,3},{1,2},{2,1},{3,0},{4,7},{5,6},{6,5},{7,4},{8,11},{9,10},{10,... | collective-permute-start | bytes 245768 | tf_op jit(solution)/shard_map/ppermute | solution.py:16
  15.8 6.3 %collective-permute-start.4 = (bf16[64,640]{1,0:T(8,128)(2,1)S(1)}, bf16[64,640]{1,0:T(8,128)(2,1)S(1)}, u32[]{:S(2)}, u32[]{:S(2)}) collective-permute-start(bf16[64,640]{1,0:T(8,128)(2,1)S(1)} %get-tuple-element.39), channel_id=1, source_target_pairs={{0,2},{1,3},{2,0},{3,1},{4,6},{5,7},{6,4},{7,5},{8,10},{9,11},{10,... | collective-permute-start | bytes 245768 | tf_op jit(solution)/shard_map/ppermute | solution.py:16
  22.1 1.7 %collective-permute-start.6 = (bf16[256,640]{1,0:T(8,128)(2,1)S(1)}, bf16[256,640]{1,0:T(8,128)(2,1)S(1)}, u32[]{:S(2)}, u32[]{:S(2)}) collective-permute-start(bf16[256,640]{1,0:T(8,128)(2,1)S(1)} %constant_dynamic-update-slice_fusion.4.refs_0_), channel_id=1, source_target_pairs={{0,16},{16,0},{1,17},{17,1},{2,18},{18,2},{3,19},{19,3},{4,20},{20... | collective-permute-start | bytes 983048 | tf_op jit(solution)/shard_map/ppermute | solution.py:16
  22.2 1.2 %copy-start = (bf16[1024,512]{1,0:T(8,128)(2,1)S(1)}, bf16[1024,512]{1,0:T(8,128)(2,1)}, u32[]{:S(2)}) copy-start(bf16[1024,512]{1,0:T(8,128)(2,1)} %refs_0_.2) | copy-start | bytes 3145732
  26.0 1.3 %collective-permute-start.7 = (f32[128,128]{1,0:T(8,128)S(1)}, f32[128,128]{1,0:T(8,128)S(1)}, u32[]{:S(2)}, u32[]{:S(2)}) collective-permute-start(f32[128,128]{1,0:T(8,128)S(1)} %get-tuple-element.31), channel_id=1, source_target_pairs={{0,16},{16,0},{1,17},{17,1},{2,18},{18,2},{3,19},{19,3},{4,20},{20... | collective-permute-start | bytes 196616 | tf_op jit(solution)/shard_map/ppermute | solution.py:16
  27.3 4.3 %collective-permute-start.8 = (f32[128,128]{1,0:T(8,128)S(1)}, f32[128,128]{1,0:T(8,128)S(1)}, u32[]{:S(2)}, u32[]{:S(2)}) collective-permute-start(f32[128,128]{1,0:T(8,128)S(1)} %add.21), channel_id=1, source_target_pairs={{0,4},{4,0},{8,12},{12,8},{1,5},{5,1},{9,13},{13,9},{2,6},{6,2},{1... | collective-permute-start | bytes 196616 | tf_op jit(solution)/shard_map/ppermute | solution.py:16
  31.6 4.3 %collective-permute-start.9 = (f32[128,128]{1,0:T(8,128)S(1)}, f32[128,128]{1,0:T(8,128)S(1)}, u32[]{:S(2)}, u32[]{:S(2)}) collective-permute-start(f32[128,128]{1,0:T(8,128)S(1)} %add.22), channel_id=1, source_target_pairs={{0,8},{4,12},{8,0},{12,4},{1,9},{5,13},{9,1},{13,5},{2,10},{6,14},... | collective-permute-start | bytes 196616 | tf_op jit(solution)/shard_map/ppermute | solution.py:16
  36.0 5.5 %collective-permute-start.12 = (f32[128,128]{1,0:T(8,128)S(1)}, f32[128,128]{1,0:T(8,128)S(1)}, u32[]{:S(2)}, u32[]{:S(2)}) collective-permute-start(f32[128,128]{1,0:T(8,128)S(1)} %add.23), channel_id=1, source_target_pairs={{0,2},{1,3},{2,0},{3,1},{4,6},{5,7},{6,4},{7,5},{8,10},{9,11},{10,... | collective-permute-start | bytes 196616 | tf_op jit(solution)/shard_map/ppermute | solution.py:16
  36.4 6.1 %collective-permute-start.11 = (f32[128,128]{1,0:T(8,128)S(1)}, f32[128,128]{1,0:T(8,128)S(1)}, u32[]{:S(2)}, u32[]{:S(2)}) collective-permute-start(f32[128,128]{1,0:T(8,128)S(1)} %add.23), channel_id=1, source_target_pairs={{0,3},{1,2},{2,1},{3,0},{4,7},{5,6},{6,5},{7,4},{8,11},{9,10},{10,... | collective-permute-start | bytes 196616 | tf_op jit(solution)/shard_map/ppermute | solution.py:16
  38.3 4.9 %collective-permute-start.10 = (f32[128,128]{1,0:T(8,128)S(1)}, f32[128,128]{1,0:T(8,128)S(1)}, u32[]{:S(2)}, u32[]{:S(2)}) collective-permute-start(f32[128,128]{1,0:T(8,128)S(1)} %add.23), channel_id=1, source_target_pairs={{0,1},{1,0},{2,3},{3,2},{4,5},{5,4},{6,7},{7,6},{8,9},{9,8},{10,11... | collective-permute-start | bytes 196616 | tf_op jit(solution)/shard_map/ppermute | solution.py:16
  43.2 1.3 %collective-permute-start.13 = (f32[128,128]{1,0:T(8,128)S(1)}, f32[128,128]{1,0:T(8,128)S(1)}, u32[]{:S(2)}, u32[]{:S(2)}) collective-permute-start(f32[128,128]{1,0:T(8,128)S(1)} %add_add_fusion.refs_0_), channel_id=1, source_target_pairs={{0,16},{16,0},{1,17},{17,1},{2,18},{18,2},{3,19},{19,3},{4,20},{20... | collective-permute-start | bytes 196616 | tf_op jit(solution)/shard_map/ppermute | solution.py:16
  48.2 2.0 %collective-permute-start.14 = (f32[256,512]{1,0:T(8,128)S(1)}, f32[256,512]{1,0:T(8,128)S(1)}, u32[]{:S(2)}, u32[]{:S(2)}) collective-permute-start(f32[256,512]{1,0:T(8,128)S(1)} %get-tuple-element.35), channel_id=1, source_target_pairs={{0,16},{16,0},{1,17},{17,1},{2,18},{18,2},{3,19},{19,3},{4,20},{20... | collective-permute-start | bytes 1572872 | tf_op jit(solution)/shard_map/ppermute | solution.py:16
  51.0 20.3 %all-to-all-start = ((f32[16,16,512]{2,1,0:T(8,128)}), f32[16,16,512]{2,1,0:T(8,128)S(1)}, u32[]{:S(2)}, u32[]{:S(2)}) async-start(f32[16,16,512]{2,1,0:T(8,128)} %bitcast), calls=%async_computation | async-start | bytes 1048576 | tf_op jit(solution)/shard_map/all_to_all | solution.py:420

commit v3 on v2

--- a/solution.py
+++ b/solution.py
@@ -36,6 +36,9 @@
 
 def turn_order(size):
     return [1] + list(range(size - 1, 1, -1))
+
+
+PLANE, ZED = [0, 1, 2, 3], [0, 3, 2, 1]
 
 
 class Sizes:
@@ -59,13 +62,15 @@
         self.pos_at = 0 if self.neg_at else self.negs
         self.chunks = self.block // LANES
         self.scale = self.feat ** (-0.5)
+        self.tensor_order = PLANE if self.tensor == 4 else list(range(self.tensor))
+        self.corpus_order = ZED if self.corpus == 4 else list(range(self.corpus))
         self.deep = 2 * LANES
         self.seats = self.deep // self.negs
         self.nrows = self.rows // self.seats
         self.joint = max(1, self.deep // self.columns)
         self.run = self.joint * self.own
         self.sets = self.groups // self.joint
-        self.vmem = min(60, 16 + 10 * self.rows // 1024) * 2**20
+        self.vmem = min(60, 20 + 10 * self.rows // 1024) * 2**20
 
 
 def message_kernel(z, pos_in, neg_in, query_in, *refs):
@@ -119,20 +124,22 @@
 
 
 def score_kernel(z, *refs):
-    arrived = refs[: z.dp]
-    passage_ref = refs[z.dp]
-    query_ref, index_ref, pos_ref = refs[z.dp + 1 : z.dp + 4]
-    part_refs = refs[z.dp + 4 : 2 * z.dp + 4]
-    id_ref, local_ref, logit_ref = refs[2 * z.dp + 4 :]
+    cuts = z.corpus if z.dp == 2 else 1
+    arrived, refs = refs[: cuts * z.dp], refs[cuts * z.dp :]
+    passage_ref, query_ref, index_ref, pos_ref = refs[:4]
+    part_refs = refs[4 : z.dp + 4]
+    id_ref, local_ref, logit_ref = refs[z.dp + 4 :]
     d, t, c = (lax.axis_index(a) for a in ("dp", "tensor", "corpus"))
     for sd in range(z.dp):
         for sc in range(z.corpus):
             for st in range(z.tensor):
-                source = pl.ds((sc * z.tensor + st) * z.own, z.own)
-                place = (((d ^ sd) * z.tensor + (t ^ st)) * z.corpus + (c ^ sc)) * z.own
+                piece_ref = arrived[sd * cuts + sc % cuts]
+                source = pl.ds((sc // cuts * z.tensor + st) * z.own, z.own)
+                place = (d ^ sd) * z.tensor + (t ^ z.tensor_order[st])
+                place = (place * z.corpus + (c ^ z.corpus_order[sc])) * z.own
                 place = pl.ds(pl.multiple_of(place, z.own), z.own)
-                query_ref[place, :] = arrived[sd][source, : z.width]
-                code = arrived[sd][source, z.width :].astype(jnp.float32)
+                query_ref[place, :] = piece_ref[source, : z.width]
+                code = piece_ref[source, z.width :].astype(jnp.float32)
                 id_ref[place, :] = code * 256.0 + pltpu.roll(code, LANES // 2, 1)
     first = ((d * z.corpus + c) * z.block).astype(jnp.float32)
     wide = -(-z.columns // LANES) * LANES
@@ -191,9 +198,10 @@
 def weight_kernel(z, *refs):
     parts = refs[: z.dp]
     index_ref, hot_ref, passage_ref = refs[z.dp : z.dp + 3]
-    dense_ref, loss_ref = refs[z.dp + 3 : z.dp + 5]
-    grad_refs = refs[z.dp + 5 : 2 * z.dp + 5]
-    logit_ref, seat_ref, tile_ref = refs[2 * z.dp + 5 :]
+    dense_ref, loss_ref, size_ref = refs[z.dp + 3 : z.dp + 6]
+    sizes_ref = refs[z.dp + 6]
+    grad_refs = refs[z.dp + 7 : 2 * z.dp + 6]
+    logit_ref, seat_ref, tile_ref = refs[2 * z.dp + 6 :]
     d, t, c = (lax.axis_index(a) for a in ("dp", "tensor", "corpus"))
     for s in range(z.dp):
         at = pl.multiple_of((d ^ s) * z.part, z.part)
@@ -204,7 +212,7 @@
         lane = lax.broadcasted_iota(jnp.int32, shape, 1)
         row = lax.broadcasted_iota(jnp.int32, shape, 0) + first_row
         weights = jnp.zeros(shape, jnp.float32)
-        losses = []
+        losses, sizes = [], []
         for h in range(z.pack):
             mask = (lane >= h * z.items) & (lane < (h + 1) * z.items)
             top = jnp.max(jnp.where(mask, logits, -jnp.inf), axis=1, keepdims=True)
@@ -214,13 +222,15 @@
             own = (query // z.half) * z.own + (query & (z.own - 1)) + h * z.items
             target = jnp.where(lane == own, 1.0, 0.0)
             weights = jnp.where(mask, exponent / denominator - target, weights)
+            size = jnp.max(jnp.where(mask, jnp.abs(weights), 0.0), axis=1, keepdims=True)
+            sizes.append(jnp.maximum(size, 1e-30))
             chosen = jnp.sum(target * jnp.where(mask, logits, 0.0), axis=1, keepdims=True)
             losses.append(jnp.log(denominator) + top - chosen)
-        return weights, losses
+        return weights, losses, sizes
 
     mine = ((d * z.tensor + t) * z.corpus + c) * z.own
     first = pl.multiple_of(mine % z.packed, z.own)
-    _, losses = softmax(logit_ref[pl.ds(first, z.own), :], first)
+    _, losses, _ = softmax(logit_ref[pl.ds(first, z.own), :], first)
     loss = losses[0]
     for h in range(1, z.pack):
         loss = jnp.where(mine // z.packed == h, losses[h], loss)
@@ -230,11 +240,15 @@
 
     def weigh(i, carry):
         at = pl.ds(pl.multiple_of(i * step, step), step)
-        weights, _ = softmax(logit_ref[at, :], i * step)
+        weights, _, sizes = softmax(logit_ref[at, :], i * step)
         logit_ref[at, :] = weights.astype(jnp.bfloat16).astype(jnp.float32)
+        for h in range(z.pack):
+            place = pl.ds(pl.multiple_of(h * z.packed + i * step, step), step)
+            sizes_ref[place, :] = jnp.broadcast_to(sizes[h], (step, LANES))
         return carry
 
     lax.fori_loop(0, z.packed // step, weigh, 0)
+    size_ref[...] = sizes_ref[pl.ds(pl.multiple_of(mine, z.own), z.own), :]
 
     def seat(j):
         h, row = divmod(j * z.nrows, z.packed)
@@ -298,11 +312,18 @@
                 dense_ref[spans[h], j * LANES : (j + 1) * LANES] = (
                     alone + shared[:, j * LANES : (j + 1) * LANES]
                 ).astype(jnp.bfloat16)
-    for s in range(z.dp):
-        at = pl.multiple_of((d ^ s) * z.half, z.half)
-        grad_refs[s][...] = jnp.dot(
-            dense_ref[pl.ds(at, z.half), :], passage_ref[...], preferred_element_type=jnp.float32
-        )
+    for s in range(1, z.dp):
+        query_grads(z, s, dense_ref, sizes_ref, passage_ref, grad_refs[s - 1])
+
+
+def query_grads(z, s, dense_ref, sizes_ref, passage_ref, grad_ref):
+    at = pl.ds(pl.multiple_of((lax.axis_index("dp") ^ s) * z.half, z.half), z.half)
+    grads = jnp.dot(dense_ref[at, :], passage_ref[...], preferred_element_type=jnp.float32)
+    grad_ref[...] = grads / sizes_ref[at, :1]
+
+
+def own_kernel(z, dense_ref, sizes_ref, passage_ref, grad_ref):
+    query_grads(z, 0, dense_ref, sizes_ref, passage_ref, grad_ref)
 
 
 def hot_kernel(z, pos_ref, hot_ref):
@@ -324,14 +345,6 @@
         return carry
 
     lax.fori_loop(0, z.block // 256, one, 0)
-
-
-def query_kernel(z, arrived_ref, out_ref):
-    for t in range(z.tensor):
-        total = arrived_ref[t * z.corpus]
-        for c in range(1, z.corpus):
-            total = total + arrived_ref[t * z.corpus + c]
-        out_ref[:, t * z.width : (t + 1) * z.width] = total * z.scale
 
 
 def call(z, kernel, outs, scratch, args, flops, spaces=None, vmem=None):
@@ -367,15 +380,13 @@
         z, fetch_kernel, [shape(passages.shape, bf16)], [pltpu.SemaphoreType.DMA],
         [passages], 0, [pltpu.HBM],
     )
-    plane = [None] * z.tensor
-    for s in range(1, z.tensor):
-        plane[s] = swap(pieces[s], "tensor", s)
-    plane[0] = pieces[0]
+    plane = [swap(pieces[s], "tensor", s) if s else pieces[s] for s in z.tensor_order]
     plane = jnp.concatenate(plane, axis=0)
-    chip = [plane] * z.corpus
-    for s in range(1, z.corpus):
-        chip[s] = swap(plane, "corpus", s)
-    arrived = gather_pieces([jnp.concatenate(chip, axis=0)], "dp")
+    plane, passages = lax.optimization_barrier((plane, passages))
+    chip = [swap(plane, "corpus", s) if s else plane for s in z.corpus_order]
+    if z.dp > 2:
+        chip = [jnp.concatenate(chip, axis=0)]
+    arrived = gather_pieces(chip, "dp")
 
     work = 2 * z.rows * z.block * z.width
     query_rows, index, pos_rows, *parts = call(
@@ -394,17 +405,14 @@
     )
     (hot,) = call(z, hot_kernel, [shape((z.rows, z.block), bf16)], [], [pos_rows], z.rows * z.block)
     total = scatter_sum(parts, "dp")
-    bit = 1
-    while bit < z.tensor:
-        total = total + swap(total, "tensor", bit)
-        bit *= 2
+    total = sum([swap(total, "tensor", s) for s in range(1, z.tensor)], total)
     total = sum([swap(total, "corpus", s) for s in turn_order(z.corpus)], total)
     logits = gather_pieces([total], "dp")
 
-    dense, loss, *grads = call(
+    dense, loss, size, sizes, *grads = call(
         z, weight_kernel,
-        [shape((z.rows, z.block), bf16), shape((z.own, LANES), f32)]
-        + [shape((z.half, z.width), f32)] * z.dp,
+        [shape((z.rows, z.block), bf16)] + [shape((z.own, LANES), f32)] * 2
+        + [shape((z.rows, LANES), f32)] + [shape((z.half, z.width), f32)] * (z.dp - 1),
         [
             pltpu.VMEM((z.packed, z.lanes), f32),
             pltpu.VMEM((z.nrows, z.deep), f32),
@@ -415,12 +423,14 @@
     (grad_pass,) = call(
         z, passage_kernel, [shape((z.block, z.width), f32)], [], [dense, query_rows], work
     )
-    half = scatter_sum(grads, "dp")
-    half = half.reshape(z.groups, z.own, z.width)
+    (own_grad,) = call(
+        z, own_kernel, [shape((z.half, z.width), f32)], [], [dense, sizes, passages], work // 2
+    )
+    half = scatter_sum([own_grad] + grads, "dp")
+    half = half.astype(jnp.float16).reshape(z.groups, z.own, z.width)
     half = lax.all_to_all(half, ("tensor", "corpus"), split_axis=0, concat_axis=0, tiled=True)
-    (grad_query,) = call(
-        z, query_kernel, [shape((z.own, z.feat), f32)], [], [half], half.size
-    )
+    half = half.astype(f32).reshape(z.tensor, z.corpus, z.own, z.width).sum(axis=1)
+    grad_query = half.swapaxes(0, 1).reshape(z.own, z.feat) * (size[:, :1] * z.scale)
     return (grad_query, loss[:, 0], grad_pass)
 
 

time: 72.4 us -> 64.8 us (0.90)
  waiting for transfers between devices: 38.9 us -> 27.1 us
  starting transfers between devices: 17.6 us -> 22.4 us
  local copies, waits for them, and re-layouts: 2.65 us -> 1.24 us
  other arithmetic: 0.93 us -> 2.27 us
    ppermute x15 -> x19, waiting for transfers between devices: 25.5 us -> 19.5 us  [swap(): return lax.ppermute(value, axis, pairs(lax.axis_size(axis), bit))]
    all_to_all x1, waiting for transfers between devices: 13.4 us -> 7.59 us  [body(): lax.all_to_all(half, ('tensor', 'corpus'), split_axis=0, concat_axis=0, t...]
    ppermute x15 -> x19, starting transfers between devices: 14.1 us -> 17.4 us  [swap(): return lax.ppermute(value, axis, pairs(lax.axis_size(axis), bit))]
    all_to_all x1, starting transfers between devices: 3.57 us -> 4.96 us  [body(): lax.all_to_all(half, ('tensor', 'corpus'), split_axis=0, concat_axis=0, t...]
    add x2 -> x1, other arithmetic: 0.9 us -> 0.01 us  [scatter_sum(): mine + swap(theirs, axis, bit)]
    convert_element_type x0 -> x1, other arithmetic: none -> 0.82 us  [body(): half = half.astype(jnp.float16).reshape(z.groups, z.own, z.width)]
    unnamed x7 -> x4, local copies, waits for them, and re-layouts: 2 us -> 1.23 us
    mul x0 -> x1, other arithmetic: none -> 0.73 us  [body(): half.swapaxes(0, 1).reshape(z.own, z.feat) * (size[:, :1] * z.scale)]
  transfers between devices with their start and end apart: 16 -> 20, of which waited for: 14 -> 15; matrix products, arithmetic and copies ran while one was open for 2% -> 1% of each run, Pallas kernels for 4% -> 5%
where the time goes in v3:
time: 64.8 us; the launch traced here: 64.5 us
  waiting for transfers between devices  27.1 us (42%)
  starting transfers between devices  22.4 us (35%)
  Pallas kernels  10.8 us (17%)
  other arithmetic  2.27 us (4%)
  local copies, waits for them, and re-layouts  1.24 us (2%)
  between operations  0.74 us (1%)
    ppermute x19, waiting for transfers between devices, swap(): return lax.ppermute(value, axis, pairs(lax.axis_size(axis), bit))  19.5 us
    ppermute x19, starting transfers between devices, swap(): return lax.ppermute(value, axis, pairs(lax.axis_size(axis), bit))  17.4 us
    pallas_call x7, Pallas kernels, call(): pl.pallas_call(lambda *refs: kernel(z, *refs), out_shape=outs, in_specs=[...  10.8 us
    all_to_all x1, waiting for transfers between devices, body(): lax.all_to_all(half, ('tensor', 'corpus'), split_axis=0, concat_axis=0, t...  7.59 us
    all_to_all x1, starting transfers between devices, body(): lax.all_to_all(half, ('tensor', 'corpus'), split_axis=0, concat_axis=0, t...  4.96 us
  transfers between devices with their start and end apart: 20, of which 15 were waited for; matrix products, arithmetic and copies ran while one was open for 1% of the time, Pallas kernels for 5%

profile of v3, /device:TPU:0, one launch (start us, length us, event | category | flops | bytes accessed | tf_op | source)
XLA Modules:
  0.0 64.5 jit_solution(15515405045594443300)
XLA Ops:
  0.6 1.7 %shard_map.67 = (bf16[16,640]{1,0:T(8,128)(2,1)}, bf16[16,640]{1,0:T(8,128)(2,1)}, bf16[16,640]{1,0:T(8,128)(2,1)}, bf16[16,640]{1,0:T(8,128)(2,1)}) custom-call(s32[16]{0:T(128)} %refs_0_.1, s32[16,32]{1,0:T(8,128)} %refs_1_.1, bf16[16,2048]{1,0:T(8,128)(2,1)} %refs_2_.1), custom_call_target="tpu_custom_call" | custom-call | bytes 149568 | tf_op jit(solution)/shard_map/pallas_call | solution.py:354
  2.3 4.0 %collective-permute-start.2 = (bf16[16,640]{1,0:T(8,128)(2,1)}, bf16[16,640]{1,0:T(8,128)(2,1)S(1)}, u32[]{:S(2)}, u32[]{:S(2)}) collective-permute-start(bf16[16,640]{1,0:T(8,128)(2,1)} %get-tuple-element.31), channel_id=1, source_target_pairs={{0,12},{4,8},{8,4},{12,0},{1,13},{5,9},{9,5},{13,1},{2,14},{6,10},... | collective-permute-start | bytes 61448 | tf_op jit(solution)/shard_map/ppermute | solution.py:16
  6.9 1.2 %copy-done = bf16[1024,512]{1,0:T(8,128)(2,1)S(1)} copy-done((bf16[1024,512]{1,0:T(8,128)(2,1)S(1)}, bf16[1024,512]{1,0:T(8,128)(2,1)}, u32[]{:S(2)}) %copy-start) | copy-done | bytes 1048600
  8.2 2.0 %collective-permute-done.1 = bf16[16,640]{1,0:T(8,128)(2,1)S(1)} collective-permute-done((bf16[16,640]{1,0:T(8,128)(2,1)}, bf16[16,640]{1,0:T(8,128)(2,1)S(1)}, u32[]{:S(2)}, u32[]{:S(2)}) %collective-permute-start.1) | collective-permute-done | bytes 20512 | tf_op jit(solution)/shard_map/ppermute | solution.py:16
  10.8 3.7 %collective-permute-start.3 = (bf16[64,640]{1,0:T(8,128)(2,1)S(1)}, bf16[64,640]{1,0:T(8,128)(2,1)S(1)}, u32[]{:S(2)}, u32[]{:S(2)}) collective-permute-start(bf16[64,640]{1,0:T(8,128)(2,1)S(1)} %pad_maximum_fusion.refs_0_), channel_id=1, source_target_pairs={{0,3},{1,2},{2,1},{3,0},{4,7},{5,6},{6,5},{7,4},{8,11},{9,10},{10,... | collective-permute-start | bytes 245768 | tf_op jit(solution)/shard_map/ppermute | solution.py:16
  15.2 2.0 %collective-permute-done.3.refs_1_ = bf16[64,640]{1,0:T(8,128)(2,1)S(1)} collective-permute-done((bf16[64,640]{1,0:T(8,128)(2,1)S(1)}, bf16[64,640]{1,0:T(8,128)(2,1)S(1)}, u32[]{:S(2)}, u32[]{:S(2)}) %collective-permute-start.3) | collective-permute-done | bytes 81952 | tf_op jit(solution)/shard_map/ppermute | solution.py:16
  17.2 2.8 %collective-permute-done.4.refs_2_ = bf16[64,640]{1,0:T(8,128)(2,1)S(1)} collective-permute-done((bf16[64,640]{1,0:T(8,128)(2,1)S(1)}, bf16[64,640]{1,0:T(8,128)(2,1)S(1)}, u32[]{:S(2)}, u32[]{:S(2)}) %collective-permute-start.4) | collective-permute-done | bytes 81952 | tf_op jit(solution)/shard_map/ppermute | solution.py:16
  21.5 2.1 %shard_map.69 = (bf16[512,512]{1,0:T(8,128)(2,1)S(1)}, s32[64,256]{1,0:T(8,128)S(1)}, s32[512,128]{1,0:T(8,128)S(1)}, f32[128,128]{1,0:T(8,128)S(1)}, f32[128,128]{1,0:T(8,128)S(1)}) custom-call(bf16[64,640]{1,0:T(8,128)(2,1)S(1)} %pad_maximum_fusion.refs_0_, bf16[64,640]{1,0:T(8,128)(2,1)S(1)} %collective-permute-done.3.refs_1_, ...), custom_call_target="tpu_custom_call" | custom-call | flops 536870912 | bytes 2686976 | tf_op jit(solution)/shard_map/pallas_call | solution.py:354
  24.0 0.9 %collective-permute-done.10 = f32[128,128]{1,0:T(8,128)S(1)} collective-permute-done((f32[128,128]{1,0:T(8,128)S(1)}, f32[128,128]{1,0:T(8,128)S(1)}, u32[]{:S(2)}, u32[]{:S(2)}) %collective-permute-start.10) | collective-permute-done | bytes 65568 | tf_op jit(solution)/shard_map/ppermute | solution.py:16
  24.9 1.9 %collective-permute-start.13 = (f32[128,128]{1,0:T(8,128)S(1)}, f32[128,128]{1,0:T(8,128)S(1)}, u32[]{:S(2)}, u32[]{:S(2)}) collective-permute-start(f32[128,128]{1,0:T(8,128)S(1)} %add.24), channel_id=1, source_target_pairs={{0,12},{4,8},{8,4},{12,0},{1,13},{5,9},{9,5},{13,1},{2,14},{6,10},... | collective-permute-start | bytes 196616 | tf_op jit(solution)/shard_map/ppermute | solution.py:16
  27.3 1.2 %collective-permute-start.11 = (f32[128,128]{1,0:T(8,128)S(1)}, f32[128,128]{1,0:T(8,128)S(1)}, u32[]{:S(2)}, u32[]{:S(2)}) collective-permute-start(f32[128,128]{1,0:T(8,128)S(1)} %add.24), channel_id=1, source_target_pairs={{0,4},{4,0},{8,12},{12,8},{1,5},{5,1},{9,13},{13,9},{2,6},{6,2},{1... | collective-permute-start | bytes 196616 | tf_op jit(solution)/shard_map/ppermute | solution.py:16
  28.5 1.8 %collective-permute-done.13 = f32[128,128]{1,0:T(8,128)S(1)} collective-permute-done((f32[128,128]{1,0:T(8,128)S(1)}, f32[128,128]{1,0:T(8,128)S(1)}, u32[]{:S(2)}, u32[]{:S(2)}) %collective-permute-start.13) | collective-permute-done | bytes 65568 | tf_op jit(solution)/shard_map/ppermute | solution.py:16
  30.3 1.3 %collective-permute-done.12 = f32[128,128]{1,0:T(8,128)S(1)} collective-permute-done((f32[128,128]{1,0:T(8,128)S(1)}, f32[128,128]{1,0:T(8,128)S(1)}, u32[]{:S(2)}, u32[]{:S(2)}) %collective-permute-start.12) | collective-permute-done | bytes 65568 | tf_op jit(solution)/shard_map/ppermute | solution.py:16
  32.0 1.2 %collective-permute-start.16 = (f32[128,128]{1,0:T(8,128)S(1)}, f32[128,128]{1,0:T(8,128)S(1)}, u32[]{:S(2)}, u32[]{:S(2)}) collective-permute-start(f32[128,128]{1,0:T(8,128)S(1)} %add_add_fusion.1), channel_id=1, source_target_pairs={{0,2},{1,3},{2,0},{3,1},{4,6},{5,7},{6,4},{7,5},{8,10},{9,11},{10,... | collective-permute-start | bytes 196616 | tf_op jit(solution)/shard_map/ppermute | solution.py:16
  33.2 1.3 %collective-permute-start.15 = (f32[128,128]{1,0:T(8,128)S(1)}, f32[128,128]{1,0:T(8,128)S(1)}, u32[]{:S(2)}, u32[]{:S(2)}) collective-permute-start(f32[128,128]{1,0:T(8,128)S(1)} %add_add_fusion.1), channel_id=1, source_target_pairs={{0,3},{1,2},{2,1},{3,0},{4,7},{5,6},{6,5},{7,4},{8,11},{9,10},{10,... | collective-permute-start | bytes 196616 | tf_op jit(solution)/shard_map/ppermute | solution.py:16
  34.5 1.0 %collective-permute-start.14 = (f32[128,128]{1,0:T(8,128)S(1)}, f32[128,128]{1,0:T(8,128)S(1)}, u32[]{:S(2)}, u32[]{:S(2)}) collective-permute-start(f32[128,128]{1,0:T(8,128)S(1)} %add_add_fusion.1), channel_id=1, source_target_pairs={{0,1},{1,0},{2,3},{3,2},{4,5},{5,4},{6,7},{7,6},{8,9},{9,8},{10,11... | collective-permute-start | bytes 196616 | tf_op jit(solution)/shard_map/ppermute | solution.py:16
  35.6 4.1 %collective-permute-done.16 = f32[128,128]{1,0:T(8,128)S(1)} collective-permute-done((f32[128,128]{1,0:T(8,128)S(1)}, f32[128,128]{1,0:T(8,128)S(1)}, u32[]{:S(2)}, u32[]{:S(2)}) %collective-permute-start.16) | collective-permute-done | bytes 65568 | tf_op jit(solution)/shard_map/ppermute | solution.py:16
  40.5 1.0 %collective-permute-done.17.refs_1_ = f32[128,128]{1,0:T(8,128)S(1)} collective-permute-done((f32[128,128]{1,0:T(8,128)S(1)}, f32[128,128]{1,0:T(8,128)S(1)}, u32[]{:S(2)}, u32[]{:S(2)}) %collective-permute-start.17) | collective-permute-done | bytes 65568 | tf_op jit(solution)/shard_map/ppermute | solution.py:16
  41.4 3.5 %shard_map.71 = (bf16[512,1024]{1,0:T(8,128)(2,1)S(1)}, f32[16,128]{1,0:T(8,128)S(1)}, f32[16,128]{1,0:T(8,128)S(1)}, f32[512,128]{1,0:T(8,128)S(1)}, f32[256,512]{1,0:T(8,128)S(1)}) custom-call(f32[128,128]{1,0:T(8,128)S(1)} %add_add_fusion.refs_0_, f32[128,128]{1,0:T(8,128)S(1)} %collective-permute-done.17.refs_1_, ...), custom_call_target="tpu_custom_call" | custom-call | flops 1073741824 | bytes 4145152 | tf_op jit(solution)/shard_map/pallas_call | solution.py:354
  45.7 1.3 %collective-permute-done.18 = f32[256,512]{1,0:T(8,128)S(1)} collective-permute-done((f32[256,512]{1,0:T(8,128)S(1)}, f32[256,512]{1,0:T(8,128)S(1)}, u32[]{:S(2)}, u32[]{:S(2)}) %collective-permute-start.18) | collective-permute-done | bytes 524320 | tf_op jit(solution)/shard_map/ppermute | solution.py:16
  47.0 0.8 %add_convert_fusion = f16[256,512]{1,0:T(8,128)(2,1)} fusion(f32[256,512]{1,0:T(8,128)S(1)} %shard_map.72, f32[256,512]{1,0:T(8,128)S(1)} %collective-permute-done.18), kind=kLoop, calls=%fused_computation.1 | loop fusion | flops 262144 | bytes 1310720 | tf_op jit(solution)/shard_map/convert_element_type | solution.py:430
  47.8 5.0 %all-to-all-start = ((f16[16,16,512]{2,1,0:T(8,128)(2,1)}), f16[16,16,512]{2,1,0:T(8,128)(2,1)S(1)}, u32[]{:S(2)}, u32[]{:S(2)}) async-start(f16[16,16,512]{2,1,0:T(8,128)(2,1)} %bitcast), calls=%async_computation | async-start | bytes 524288 | tf_op jit(solution)/shard_map/all_to_all | solution.py:431
  52.8 2.7 %shard_map.73 = f32[1024,512]{1,0:T(8,128)} custom-call(bf16[512,1024]{1,0:T(8,128)(2,1)S(1)} %get-tuple-element.39.refs_0_, bf16[512,512]{1,0:T(8,128)(2,1)S(1)} %get-tuple-element.44.refs_1_), custom_call_target="tpu_custom_call" | custom-call | flops 536870912 | bytes 3670016 | tf_op jit(solution)/shard_map/pallas_call | solution.py:354
  56.1 7.6 %all-to-all-done = f16[16,16,512]{2,1,0:T(8,128)(2,1)S(1)} async-done(((f16[16,16,512]{2,1,0:T(8,128)(2,1)}), f16[16,16,512]{2,1,0:T(8,128)(2,1)S(1)}, u32[]{:S(2)}, u32[]{:S(2)}) %all-to-all-start) | async-done | bytes 262176 | tf_op jit(solution)/shard_map/all_to_all | solution.py:431
  (36 shorter events, 7.6 us)
Async XLA Ops:
  2.3 5.9 %collective-permute-start.2 = (bf16[16,640]{1,0:T(8,128)(2,1)}, bf16[16,640]{1,0:T(8,128)(2,1)S(1)}, u32[]{:S(2)}, u32[]{:S(2)}) collective-permute-start(bf16[16,640]{1,0:T(8,128)(2,1)} %get-tuple-element.31), channel_id=1, source_target_pairs={{0,12},{4,8},{8,4},{12,0},{1,13},{5,9},{9,5},{13,1},{2,14},{6,10},... | collective-permute-start | bytes 61448 | tf_op jit(solution)/shard_map/ppermute | solution.py:16
  6.3 4.0 %collective-permute-start.1 = (bf16[16,640]{1,0:T(8,128)(2,1)}, bf16[16,640]{1,0:T(8,128)(2,1)S(1)}, u32[]{:S(2)}, u32[]{:S(2)}) collective-permute-start(bf16[16,640]{1,0:T(8,128)(2,1)} %get-tuple-element.30), channel_id=1, source_target_pairs={{0,8},{4,12},{8,0},{12,4},{1,9},{5,13},{9,1},{13,5},{2,10},{6,14},... | collective-permute-start | bytes 61448 | tf_op jit(solution)/shard_map/ppermute | solution.py:16
  6.8 4.0 %collective-permute-start = (bf16[16,640]{1,0:T(8,128)(2,1)}, bf16[16,640]{1,0:T(8,128)(2,1)S(1)}, u32[]{:S(2)}, u32[]{:S(2)}) collective-permute-start(bf16[16,640]{1,0:T(8,128)(2,1)} %get-tuple-element.29), channel_id=1, source_target_pairs={{0,4},{4,0},{8,12},{12,8},{1,5},{5,1},{9,13},{13,9},{2,6},{6,2},{1... | collective-permute-start | bytes 61448 | tf_op jit(solution)/shard_map/ppermute | solution.py:16
  6.9 1.2 %copy-start = (bf16[1024,512]{1,0:T(8,128)(2,1)S(1)}, bf16[1024,512]{1,0:T(8,128)(2,1)}, u32[]{:S(2)}) copy-start(bf16[1024,512]{1,0:T(8,128)(2,1)} %refs_0_.2) | copy-start | bytes 3145732
  8.1 2.6 %copy-start.1 = (bf16[16,640]{1,0:T(8,128)(2,1)S(1)}, bf16[16,640]{1,0:T(8,128)(2,1)}, u32[]{:S(2)}) copy-start(bf16[16,640]{1,0:T(8,128)(2,1)} %get-tuple-element.28) | copy-start | bytes 61444
  10.8 6.5 %collective-permute-start.3 = (bf16[64,640]{1,0:T(8,128)(2,1)S(1)}, bf16[64,640]{1,0:T(8,128)(2,1)S(1)}, u32[]{:S(2)}, u32[]{:S(2)}) collective-permute-start(bf16[64,640]{1,0:T(8,128)(2,1)S(1)} %pad_maximum_fusion.refs_0_), channel_id=1, source_target_pairs={{0,3},{1,2},{2,1},{3,0},{4,7},{5,6},{6,5},{7,4},{8,11},{9,10},{10,... | collective-permute-start | bytes 245768 | tf_op jit(solution)/shard_map/ppermute | solution.py:16
  14.4 5.6 %collective-permute-start.4 = (bf16[64,640]{1,0:T(8,128)(2,1)S(1)}, bf16[64,640]{1,0:T(8,128)(2,1)S(1)}, u32[]{:S(2)}, u32[]{:S(2)}) collective-permute-start(bf16[64,640]{1,0:T(8,128)(2,1)S(1)} %pad_maximum_fusion.refs_0_), channel_id=1, source_target_pairs={{0,2},{1,3},{2,0},{3,1},{4,6},{5,7},{6,4},{7,5},{8,10},{9,11},{10,... | collective-permute-start | bytes 245768 | tf_op jit(solution)/shard_map/ppermute | solution.py:16
  14.4 5.6 %collective-permute-start.5 = (bf16[64,640]{1,0:T(8,128)(2,1)S(1)}, bf16[64,640]{1,0:T(8,128)(2,1)S(1)}, u32[]{:S(2)}, u32[]{:S(2)}) collective-permute-start(bf16[64,640]{1,0:T(8,128)(2,1)S(1)} %pad_maximum_fusion.refs_0_), channel_id=1, source_target_pairs={{0,1},{1,0},{2,3},{3,2},{4,5},{5,4},{6,7},{7,6},{8,9},{9,8},{10,11... | collective-permute-start | bytes 245768 | tf_op jit(solution)/shard_map/ppermute | solution.py:16
  15.2 5.3 %collective-permute-start.6 = (bf16[64,640]{1,0:T(8,128)(2,1)S(1)}, bf16[64,640]{1,0:T(8,128)(2,1)S(1)}, u32[]{:S(2)}, u32[]{:S(2)}) collective-permute-start(bf16[64,640]{1,0:T(8,128)(2,1)S(1)} %pad_maximum_fusion.refs_0_), channel_id=1, source_target_pairs={{0,16},{16,0},{1,17},{17,1},{2,18},{18,2},{3,19},{19,3},{4,20},{20... | collective-permute-start | bytes 245768 | tf_op jit(solution)/shard_map/ppermute | solution.py:16
  17.2 3.3 %collective-permute-start.7 = (bf16[64,640]{1,0:T(8,128)(2,1)S(1)}, bf16[64,640]{1,0:T(8,128)(2,1)S(1)}, u32[]{:S(2)}, u32[]{:S(2)}) collective-permute-start(bf16[64,640]{1,0:T(8,128)(2,1)S(1)} %collective-permute-done.3.refs_1_), channel_id=1, source_target_pairs={{0,16},{16,0},{1,17},{17,1},{2,18},{18,2},{3,19},{19,3},{4,20},{20... | collective-permute-start | bytes 245768 | tf_op jit(solution)/shard_map/ppermute | solution.py:16
  20.0 1.3 %collective-permute-start.8 = (bf16[64,640]{1,0:T(8,128)(2,1)S(1)}, bf16[64,640]{1,0:T(8,128)(2,1)S(1)}, u32[]{:S(2)}, u32[]{:S(2)}) collective-permute-start(bf16[64,640]{1,0:T(8,128)(2,1)S(1)} %collective-permute-done.4.refs_2_), channel_id=1, source_target_pairs={{0,16},{16,0},{1,17},{17,1},{2,18},{18,2},{3,19},{19,3},{4,20},{20... | collective-permute-start | bytes 245768 | tf_op jit(solution)/shard_map/ppermute | solution.py:16
  20.0 1.4 %collective-permute-start.9 = (bf16[64,640]{1,0:T(8,128)(2,1)S(1)}, bf16[64,640]{1,0:T(8,128)(2,1)S(1)}, u32[]{:S(2)}, u32[]{:S(2)}) collective-permute-start(bf16[64,640]{1,0:T(8,128)(2,1)S(1)} %collective-permute-done.5.refs_3_), channel_id=1, source_target_pairs={{0,16},{16,0},{1,17},{17,1},{2,18},{18,2},{3,19},{19,3},{4,20},{20... | collective-permute-start | bytes 245768 | tf_op jit(solution)/shard_map/ppermute | solution.py:16
  23.6 1.3 %collective-permute-start.10 = (f32[128,128]{1,0:T(8,128)S(1)}, f32[128,128]{1,0:T(8,128)S(1)}, u32[]{:S(2)}, u32[]{:S(2)}) collective-permute-start(f32[128,128]{1,0:T(8,128)S(1)} %get-tuple-element.36), channel_id=1, source_target_pairs={{0,16},{16,0},{1,17},{17,1},{2,18},{18,2},{3,19},{19,3},{4,20},{20... | collective-permute-start | bytes 196616 | tf_op jit(solution)/shard_map/ppermute | solution.py:16
  24.9 5.4 %collective-permute-start.13 = (f32[128,128]{1,0:T(8,128)S(1)}, f32[128,128]{1,0:T(8,128)S(1)}, u32[]{:S(2)}, u32[]{:S(2)}) collective-permute-start(f32[128,128]{1,0:T(8,128)S(1)} %add.24), channel_id=1, source_target_pairs={{0,12},{4,8},{8,4},{12,0},{1,13},{5,9},{9,5},{13,1},{2,14},{6,10},... | collective-permute-start | bytes 196616 | tf_op jit(solution)/shard_map/ppermute | solution.py:16
  26.8 4.8 %collective-permute-start.12 = (f32[128,128]{1,0:T(8,128)S(1)}, f32[128,128]{1,0:T(8,128)S(1)}, u32[]{:S(2)}, u32[]{:S(2)}) collective-permute-start(f32[128,128]{1,0:T(8,128)S(1)} %add.24), channel_id=1, source_target_pairs={{0,8},{4,12},{8,0},{12,4},{1,9},{5,13},{9,1},{13,5},{2,10},{6,14},... | collective-permute-start | bytes 196616 | tf_op jit(solution)/shard_map/ppermute | solution.py:16
  27.3 4.7 %collective-permute-start.11 = (f32[128,128]{1,0:T(8,128)S(1)}, f32[128,128]{1,0:T(8,128)S(1)}, u32[]{:S(2)}, u32[]{:S(2)}) collective-permute-start(f32[128,128]{1,0:T(8,128)S(1)} %add.24), channel_id=1, source_target_pairs={{0,4},{4,0},{8,12},{12,8},{1,5},{5,1},{9,13},{13,9},{2,6},{6,2},{1... | collective-permute-start | bytes 196616 | tf_op jit(solution)/shard_map/ppermute | solution.py:16
  32.0 7.7 %collective-permute-start.16 = (f32[128,128]{1,0:T(8,128)S(1)}, f32[128,128]{1,0:T(8,128)S(1)}, u32[]{:S(2)}, u32[]{:S(2)}) collective-permute-start(f32[128,128]{1,0:T(8,128)S(1)} %add_add_fusion.1), channel_id=1, source_target_pairs={{0,2},{1,3},{2,0},{3,1},{4,6},{5,7},{6,4},{7,5},{8,10},{9,11},{10,... | collective-permute-start | bytes 196616 | tf_op jit(solution)/shard_map/ppermute | solution.py:16
  33.2 6.5 %collective-permute-start.15 = (f32[128,128]{1,0:T(8,128)S(1)}, f32[128,128]{1,0:T(8,128)S(1)}, u32[]{:S(2)}, u32[]{:S(2)}) collective-permute-start(f32[128,128]{1,0:T(8,128)S(1)} %add_add_fusion.1), channel_id=1, source_target_pairs={{0,3},{1,2},{2,1},{3,0},{4,7},{5,6},{6,5},{7,4},{8,11},{9,10},{10,... | collective-permute-start | bytes 196616 | tf_op jit(solution)/shard_map/ppermute | solution.py:16
  34.5 5.6 %collective-permute-start.14 = (f32[128,128]{1,0:T(8,128)S(1)}, f32[128,128]{1,0:T(8,128)S(1)}, u32[]{:S(2)}, u32[]{:S(2)}) collective-permute-start(f32[128,128]{1,0:T(8,128)S(1)} %add_add_fusion.1), channel_id=1, source_target_pairs={{0,1},{1,0},{2,3},{3,2},{4,5},{5,4},{6,7},{7,6},{8,9},{9,8},{10,11... | collective-permute-start | bytes 196616 | tf_op jit(solution)/shard_map/ppermute | solution.py:16
  40.1 1.3 %collective-permute-start.17 = (f32[128,128]{1,0:T(8,128)S(1)}, f32[128,128]{1,0:T(8,128)S(1)}, u32[]{:S(2)}, u32[]{:S(2)}) collective-permute-start(f32[128,128]{1,0:T(8,128)S(1)} %add_add_fusion.refs_0_), channel_id=1, source_target_pairs={{0,16},{16,0},{1,17},{17,1},{2,18},{18,2},{3,19},{19,3},{4,20},{20... | collective-permute-start | bytes 196616 | tf_op jit(solution)/shard_map/ppermute | solution.py:16
  45.0 2.0 %collective-permute-start.18 = (f32[256,512]{1,0:T(8,128)S(1)}, f32[256,512]{1,0:T(8,128)S(1)}, u32[]{:S(2)}, u32[]{:S(2)}) collective-permute-start(f32[256,512]{1,0:T(8,128)S(1)} %get-tuple-element.41), channel_id=1, source_target_pairs={{0,16},{16,0},{1,17},{17,1},{2,18},{18,2},{3,19},{19,3},{4,20},{20... | collective-permute-start | bytes 1572872 | tf_op jit(solution)/shard_map/ppermute | solution.py:16
  47.8 15.9 %all-to-all-start = ((f16[16,16,512]{2,1,0:T(8,128)(2,1)}), f16[16,16,512]{2,1,0:T(8,128)(2,1)S(1)}, u32[]{:S(2)}, u32[]{:S(2)}) async-start(f16[16,16,512]{2,1,0:T(8,128)(2,1)} %bitcast), calls=%async_computation | async-start | bytes 524288 | tf_op jit(solution)/shard_map/all_to_all | solution.py:431

commit v4 on v3

v4 whole, which is shorter than its diff:
```python
import jax
import jax.numpy as jnp
from jax import lax
from jax.experimental import pallas as pl
from jax.experimental.pallas import tpu as pltpu
from jax.sharding import PartitionSpec as P

LANES = 128
FAR = -(2**20)
LOW = -1e30
PLANE, ZED = [0, 1, 2, 3], [0, 3, 2, 1]


def swap(value, axis, bit):
    size = lax.axis_size(axis)
    return lax.ppermute(value, axis, [(i, i ^ bit) for i in range(size)])


def gather_pairs(pieces):
    bit = 2
    while bit < lax.axis_size("dp"):
        pieces = pieces + [swap(piece, "dp", bit) for piece in pieces]
        bit *= 2
    return pieces


def scatter_pairs(pieces):
    while len(pieces) > 1:
        n = len(pieces) // 2
        pieces = [
            mine + swap(theirs, "dp", 2 * n) for mine, theirs in zip(pieces[:n], pieces[n:])
        ]
    return pieces[0]


class Sizes:
    def __init__(self, queries, passages, neg_ids):
        self.own, self.feat = queries.shape
        self.block, self.width = passages.shape
        self.negs = neg_ids.shape[1]
        self.dp = lax.axis_size("dp")
        self.tensor = lax.axis_size("tensor")
        self.corpus = lax.axis_size("corpus")
        self.side = self.dp // 2
        self.groups = self.tensor * self.corpus
        self.half = self.groups * self.own
        self.rows = self.side * self.half
        self.named = self.dp * self.half
        self.columns = self.dp * self.own
        self.items = self.columns + self.negs
        self.lanes = -(-self.items // LANES) * LANES
        self.pack = max(1, LANES // self.items)
        self.packed = self.rows // self.pack
        self.neg_at = self.columns % LANES
        self.pos_at = 0 if self.neg_at else self.negs
        self.wide = 2 * self.block
        self.chunks = self.wide // LANES
        self.scale = self.feat ** (-0.5)
        self.tensor_order = PLANE if self.tensor == 4 else list(range(self.tensor))
        self.corpus_order = ZED if self.corpus == 4 else list(range(self.corpus))
        self.cuts = self.corpus if self.side == 1 else 1
        self.deep = 2 * LANES
        self.seats = self.deep // self.negs
        self.nrows = self.rows // self.seats
        self.joint = max(1, self.deep // self.columns)
        self.run = self.joint * self.own
        self.sets = self.groups // self.joint
        self.high = -(-3 * self.pack // 8) * 8
        self.vmem = min(61, 20 + 20 * self.rows // 1024) * 2**20


def places():
    return [lax.axis_index(axis) for axis in ("dp", "tensor", "corpus")]


def rows_at(start, size):
    return pl.ds(pl.multiple_of(start, size), size)


def message_kernel(z, pos_in, neg_in, query_in, *refs):
    piece_refs = refs[: z.tensor]
    pos_ref, neg_ref, query_ref, sems = refs[z.tensor :]
    t = lax.axis_index("tensor")
    moves = [
        pltpu.make_async_copy(source, target, sems.at[i])
        for i, (source, target) in enumerate(
            [(pos_in, pos_ref), (neg_in, neg_ref), (query_in, query_ref)]
        )
    ]
    for move in moves:
        move.start()
    for move in moves:
        move.wait()
    half = LANES // 2
    row = lax.broadcasted_iota(jnp.int32, (z.own, half), 0)
    pos = jnp.zeros((z.own, half), jnp.int32)
    for i in range(z.own):
        pos = jnp.where(row == i, pos_ref[i], pos)
    ids = [neg_ref[...], pos[:, : half - z.neg_at - z.negs]]
    ids = jnp.concatenate([part for part in [pos[:, : z.neg_at]] + ids if part.shape[1]], axis=1)
    ids = jnp.concatenate([ids >> 8, ids & 255], axis=1)
    code = ids.astype(jnp.float32).astype(jnp.bfloat16)
    for s in range(z.tensor):
        at = pl.ds(pl.multiple_of((t ^ s) * z.width, LANES), z.width)
        piece_refs[s][:, : z.width] = query_ref[:, at]
        piece_refs[s][:, z.width :] = code


def fetch_kernel(z, block_ref, passage_ref, sem):
    fetch = pltpu.make_async_copy(block_ref, passage_ref, sem)
    fetch.start()
    fetch.wait()


def seat_rows(z, out_ref, source):
    lane = lax.broadcasted_iota(jnp.int32, (z.nrows, LANES), 1)
    per = LANES // z.negs
    for chunk in range(z.deep // LANES):
        packed = None
        for k in range(per):
            ref, row, at = source(chunk * per + k)
            base = at // LANES * LANES
            piece = ref[pl.ds(row, z.nrows), base : base + LANES]
            turn = (k * z.negs - at) % LANES
            piece = pltpu.roll(piece, turn, 1) if turn else piece
            packed = piece if packed is None else jnp.where(lane < k * z.negs, packed, piece)
        out_ref[:, chunk * LANES : (chunk + 1) * LANES] = packed


def score_kernel(z, *refs):
    count = z.side * z.cuts
    arrived, others, refs = refs[:count], refs[count : 2 * count], refs[2 * count :]
    block_refs, (query_ref, index_ref, pos_ref, inside_ref, part_ref) = refs[:2], refs[2:7]
    id_ref, local_ref, logit_ref = refs[7:]
    d, t, c = places()
    for su in range(z.side):
        for sc in range(z.corpus):
            for st in range(z.tensor):
                piece = su * z.cuts + sc % z.cuts
                source = pl.ds((sc // z.cuts * z.tensor + st) * z.own, z.own)
                from_d = d ^ (2 * su)
                place = (t ^ z.tensor_order[st]) * z.corpus + (c ^ z.corpus_order[sc])
                row = rows_at(((from_d >> 1) * z.groups + place) * z.own, z.own)
                query_ref[row, :] = arrived[piece][source, : z.width]
                codes = [arrived[piece][source, z.width :], others[piece][source, :]]
                for side, code in enumerate(codes):
                    code = code.astype(jnp.float32)
                    row = rows_at(((from_d ^ side) * z.groups + place) * z.own, z.own)
                    id_ref[row, :] = code * 256.0 + pltpu.roll(code, LANES // 2, 1)

    def localize(ids):
        found = jnp.full(ids.shape, float(FAR), jnp.float32)
        for side in range(2):
            local = ids - (((d ^ side) * z.corpus + c) * z.block).astype(jnp.float32)
            inside = (local >= 0.0) & (local < float(z.block))
            found = jnp.where(inside, local + float(side * z.block), found)
        return found

    wide = -(-z.columns // LANES) * LANES
    row = lax.broadcasted_iota(jnp.int32, (z.half, wide), 0) & (z.own - 1)
    col = lax.broadcasted_iota(jnp.int32, (z.half, wide), 1)
    group_ids = jnp.zeros((z.groups, wide), jnp.float32)
    for h in range(z.dp):
        at = pl.ds(h * z.half, z.half)
        pos = jnp.broadcast_to(id_ref[at, z.pos_at : z.pos_at + 1], (z.half, wide))
        pos_ref[at, :] = localize(pos[:, :LANES]).astype(jnp.int32)
        kept = jnp.where(col == row + h * z.own, pos, 0.0)
        group_ids += jnp.sum(kept.reshape(z.groups, z.own, wide), axis=1)
    batch_ids = jnp.broadcast_to(group_ids[:, None, :], (z.groups, z.own, wide))
    batch_ids = batch_ids.reshape(z.half, wide)
    lane = lax.broadcasted_iota(jnp.int32, (z.half, LANES), 1)
    for u in range(z.side):
        ids = id_ref[rows_at((2 * u + (d & 1)) * z.half, z.half), :]
        for base in range(0, z.lanes, LANES):
            named = ids
            if base < z.columns:
                named = jnp.where(lane + base < z.columns, batch_ids[:, base : base + LANES], ids)
            local = jnp.where(lane + base < z.items, localize(named), float(FAR))
            local_ref[pl.ds(u * z.half, z.half), base : base + LANES] = local.astype(jnp.int32)
    step = min(z.rows, 128)

    def score(i, carry):
        at = rows_at(i * step, step)
        scores = [
            lax.dot_general(
                query_ref[at, :], block_ref[...], (((1,), (1,)), ((), ())),
                preferred_element_type=jnp.float32,
            )
            for block_ref in block_refs
        ]
        each = z.block // LANES
        for base in range(0, z.lanes, LANES):
            local = local_ref[at, base : base + LANES]
            chunk, within = local >> 7, local & (LANES - 1)
            picked = jnp.zeros((step, LANES), jnp.float32)
            for j in range(z.chunks):
                k = j % each * LANES
                found = jnp.take_along_axis(scores[j // each][:, k : k + LANES], within, axis=1)
                picked = jnp.where(chunk == j, found, picked)
            logit_ref[at, base : base + LANES] = picked
        return carry

    lax.fori_loop(0, z.rows // step, score, 0)
    seat_rows(z, index_ref, lambda j: (local_ref, j * z.nrows, z.columns))
    for source_ref, target_ref in [(logit_ref, part_ref), (local_ref, inside_ref)]:
        lane = lax.broadcasted_iota(jnp.int32, (z.packed, z.lanes), 1)
        packed = source_ref[pl.ds(0, z.packed), :]
        for h in range(1, z.pack):
            other = pltpu.roll(source_ref[pl.ds(h * z.packed, z.packed), :], h * z.items, 1)
            packed = jnp.where(lane < h * z.items, packed, other)
        target_ref[...] = packed


def hot_kernel(z, pos_ref, hot_ref):
    lane = lax.broadcasted_iota(jnp.int32, (z.half, LANES), 1)
    for h in range(z.dp):
        at = pl.ds(h * z.half, z.half)
        for j in range(z.chunks):
            same = pos_ref[at, :] == lane + j * LANES
            hot_ref[at, j * LANES : (j + 1) * LANES] = jnp.where(same, 1.0, 0.0).astype(jnp.bfloat16)


def stat_kernel(z, total_ref, inside_ref, exponent_ref, stat_ref):
    step = min(z.packed, 256)
    side = lax.axis_index("dp") & 1

    def one(i, carry):
        at = rows_at(i * step, step)
        logits = total_ref[at, :] * z.scale
        lane = lax.broadcasted_iota(jnp.int32, logits.shape, 1)
        row = lax.broadcasted_iota(jnp.int32, logits.shape, 0) + i * step
        short = lax.broadcasted_iota(jnp.int32, (step, LANES), 1)
        named = inside_ref[at, :] >= 0
        exponents = jnp.zeros(logits.shape, jnp.float32)
        stats = jnp.zeros((step, LANES), jnp.float32)
        for h in range(z.pack):
            mask = named & (lane >= h * z.items) & (lane < (h + 1) * z.items)
            top = jnp.max(jnp.where(mask, logits, LOW), axis=1, keepdims=True)
            exponent = jnp.where(mask, jnp.exp(logits - top), 0.0)
            query = row + h * z.packed
            own = (2 * (query // z.half) + side) * z.own + (query & (z.own - 1)) + h * z.items
            chosen = jnp.where(mask & (lane == own), logits, 0.0)
            values = (
                top,
                jnp.sum(exponent, axis=1, keepdims=True),
                jnp.sum(chosen, axis=1, keepdims=True),
            )
            for k, value in enumerate(values):
                stats = jnp.where(short == 3 * h + k, value, stats)
            exponents = exponents + exponent
        exponent_ref[at, :] = exponents
        stat_ref[:, at] = stats.T[: z.high, :]
        return carry

    lax.fori_loop(0, z.packed // step, one, 0, unroll=z.packed == step)


def split(values):
    parts = []
    for _ in range(3):
        part = values.astype(jnp.bfloat16)
        parts.append(part)
        values = values - part.astype(jnp.float32)
    return parts


def join(tiles):
    n = tiles.shape[0] // 3
    return tiles[:n] + (tiles[n : 2 * n] + tiles[2 * n :])


def place_kernel(z, exponent_ref, index_ref, hot_ref, raw_ref, seat_ref, part_ref, tile_ref):
    def seat(j):
        h, row = divmod(j * z.nrows, z.packed)
        return exponent_ref, row, h * z.items + z.columns

    seat_rows(z, seat_ref, seat)
    for k, part in enumerate(split(seat_ref[...])):
        part_ref[k] = part.astype(jnp.float32)
    high = z.seats * z.chunks
    shape = (high, z.deep)
    tall = lax.broadcasted_iota(jnp.int32, shape, 0).astype(jnp.bfloat16)
    shift = lax.broadcasted_iota(jnp.int32, (1, z.deep), 1) // z.negs * z.chunks
    spread = lax.broadcasted_iota(jnp.int32, (LANES, z.deep), 0).astype(jnp.bfloat16)
    turns = min(16, z.nrows)
    none, unit = jnp.bfloat16(0), jnp.bfloat16(1)

    def place(i, carry):
        for k in range(turns):
            r = i * turns + k
            local = index_ref[pl.ds(r, 1), :]
            chunk = ((local >> 7) + shift).astype(jnp.bfloat16)
            within = (local & (LANES - 1)).astype(jnp.bfloat16)
            here = jnp.broadcast_to(chunk, shape) == tall
            left = [
                jnp.where(
                    here,
                    jnp.broadcast_to(part_ref[p, pl.ds(r, 1), :].astype(jnp.bfloat16), shape), none,
                )
                for p in range(3)
            ]
            right = jnp.where(jnp.broadcast_to(within, (LANES, z.deep)) == spread, unit, none)
            tiles = join(lax.dot_general(
                jnp.concatenate(left, axis=0), right, (((1,), (1,)), ((), ())),
                preferred_element_type=jnp.float32,
            ))
            for j in range(z.seats):
                at = rows_at((j * z.nrows + r) * z.chunks, z.chunks)
                tile_ref[at, :] = tiles[j * z.chunks : (j + 1) * z.chunks, :]
        return carry

    lax.fori_loop(0, z.nrows // turns, place, 0)
    lane = lax.broadcasted_iota(jnp.int32, (z.run, LANES), 1)
    group = lax.broadcasted_iota(jnp.int32, (z.run, LANES), 0) // z.own
    for n in range(z.sets):
        hot = [hot_ref[pl.ds(h * z.half + n * z.run, z.run), :] for h in range(z.dp)]
        hot = jnp.concatenate(hot, axis=0)
        for u in range(z.side):
            first_row = u * z.half + n * z.run
            side, row = divmod(first_row, z.packed)
            left = []
            for chunk in range(z.deep // LANES):
                if z.joint == 1:
                    part = exponent_ref[pl.ds(row, z.run), chunk * LANES : (chunk + 1) * LANES]
                else:
                    at = chunk * LANES + lane
                    from_lane = side * z.items + at // z.run * z.own + at % z.own
                    part = jnp.take_along_axis(
                        exponent_ref[pl.ds(row, z.run), :LANES], from_lane, axis=1
                    )
                    part = jnp.where(at // z.own % z.joint == group, part, 0.0)
                left.append(part)
            left = jnp.concatenate(split(jnp.concatenate(left, axis=1)), axis=0)
            shared = join(jnp.dot(left, hot, preferred_element_type=jnp.float32))
            for j in range(z.chunks):
                alone = tile_ref[pl.ds(first_row * z.chunks + j, z.run, stride=z.chunks), :]
                raw_ref[pl.ds(first_row, z.run), j * LANES : (j + 1) * LANES] = (
                    alone + shared[:, j * LANES : (j + 1) * LANES]
                )


def weight_kernel(z, *refs):
    count = z.side * z.cuts
    parts, refs = refs[:count], refs[count:]
    raw_ref, hot_ref, own_ref, other_ref = refs[:4]
    dense_refs, (loss_ref, size_ref) = refs[4:6], refs[6:8]
    grad_refs = refs[8 : 8 + z.side]
    stat_ref, row_ref, back_ref, sizes_ref = refs[8 + z.side :]
    d, t, c = places()
    for su in range(z.side):
        for sc in range(z.corpus):
            part = parts[su * z.cuts + sc % z.cuts][pl.ds(sc // z.cuts * z.high, z.high), :]
            stat_ref[((d >> 1) ^ su) * z.corpus + (c ^ z.corpus_order[sc])] = part
    planes = z.side * z.corpus
    row_ref[...] = jnp.zeros_like(row_ref)
    for h in range(z.pack):
        tops = [stat_ref[b, 3 * h : 3 * h + 1, :] for b in range(planes)]
        top = tops[0]
        for other in tops[1:]:
            top = jnp.maximum(top, other)
        total, chosen = jnp.zeros_like(top), jnp.zeros_like(top)
        for b in range(planes):
            total += stat_ref[b, 3 * h + 1 : 3 * h + 2, :] * jnp.exp(tops[b] - top)
            chosen += stat_ref[b, 3 * h + 2 : 3 * h + 3, :]
        mine = stat_ref[(d >> 1) * z.corpus + c, 3 * h : 3 * h + 1, :]
        rest = 1.0 - jnp.exp(chosen - top) / total
        row_ref[h : h + 1, :] = jnp.exp(mine - top) / total
        row_ref[z.pack + h : z.pack + h + 1, :] = jnp.maximum(rest, 2.0**-24)
        row_ref[2 * z.pack + h : 2 * z.pack + h + 1, :] = jnp.log(total) + top - chosen
    back_ref[...] = row_ref[...].T
    mine = (((d >> 1) * z.tensor + t) * z.corpus + c) * z.own
    place = rows_at(mine % z.packed, z.own)
    for k, target_ref in [(1, size_ref), (2, loss_ref)]:
        value = back_ref[place, k * z.pack : k * z.pack + 1]
        for h in range(1, z.pack):
            other = back_ref[place, k * z.pack + h : k * z.pack + h + 1]
            value = jnp.where(mine // z.packed == h, other, value)
        target_ref[...] = jnp.broadcast_to(value, (z.own, LANES))
    step = min(z.packed, 128)
    for h in range(z.pack):

        def one(i, carry):
            row = i * step
            query = h * z.packed + row
            at = rows_at(query, step)
            named = rows_at((2 * (query // z.half) + (d & 1)) * z.half + query % z.half, step)
            ratio = back_ref[rows_at(row, step), h : h + 1]
            weights = raw_ref[at, :] * ratio - hot_ref[named, :].astype(jnp.float32)
            weights = weights.astype(jnp.bfloat16)
            dense_refs[0][at, :] = weights[:, : z.block]
            dense_refs[1][at, :] = weights[:, z.block :]
            size = back_ref[rows_at(row, step), z.pack + h : z.pack + h + 1]
            sizes_ref[at, :] = jnp.broadcast_to(size, (step, LANES))
            return carry

        lax.fori_loop(0, z.packed // step, one, 0, unroll=z.packed == step)
    for s in range(z.side):
        at = rows_at(((d >> 1) ^ s) * z.half, z.half)
        grads = sum(
            jnp.dot(dense_ref[at, :], block_ref[...], preferred_element_type=jnp.float32)
            for dense_ref, block_ref in zip(dense_refs, (own_ref, other_ref))
        )
        grad_refs[s][...] = grads / sizes_ref[at, :1]


def passage_kernel(z, own_ref, query_ref, other_ref, other_query_ref, out_ref):
    def one(i, carry):
        at = rows_at(i * 256, 256)
        grads = [
            lax.dot_general(
                dense_ref[:, at], rows_ref[...], (((0,), (0,)), ((), ())),
                preferred_element_type=jnp.float32,
            )
            for dense_ref, rows_ref in [(own_ref, query_ref), (other_ref, other_query_ref)]
        ]
        out_ref[at, :] = z.scale * (grads[0] + grads[1])
        return carry

    lax.fori_loop(0, z.block // 256, one, 0)


def call(z, kernel, outs, scratch, args, flops, spaces=None, vmem=None):
    spaces = spaces or [pltpu.VMEM] * len(args)
    moved = sum(a.size * a.dtype.itemsize for a in args)
    moved += sum(o.size * jnp.dtype(o.dtype).itemsize for o in outs)
    return pl.pallas_call(
        lambda *refs: kernel(z, *refs),
        out_shape=outs,
        in_specs=[pl.BlockSpec(memory_space=space) for space in spaces],
        out_specs=[pl.BlockSpec(memory_space=pltpu.VMEM)] * len(outs),
        scratch_shapes=scratch,
        compiler_params=pltpu.CompilerParams(vmem_limit_bytes=vmem or z.vmem),
        cost_estimate=pl.CostEstimate(flops=flops, bytes_accessed=moved, transcendentals=0),
    )(*args)


def body(queries, passages, pos_ids, neg_ids):
    z = Sizes(queries, passages, neg_ids)
    f32, bf16, i32 = jnp.float32, jnp.bfloat16, jnp.int32
    shape = jax.ShapeDtypeStruct

    pieces = call(
        z, message_kernel, [shape((z.own, z.width + LANES), bf16)] * z.tensor,
        [
            pltpu.SMEM(pos_ids.shape, i32), pltpu.VMEM(neg_ids.shape, i32),
            pltpu.VMEM(queries.shape, bf16), pltpu.SemaphoreType.DMA((3,)),
        ],
        [pos_ids, neg_ids, queries], 0, [pltpu.HBM] * 3, 60 * 2**20,
    )
    passages, pieces = lax.optimization_barrier((passages, pieces))
    other_block = swap(passages, "dp", 1)
    (own_block,) = call(
        z, fetch_kernel, [shape(passages.shape, bf16)], [pltpu.SemaphoreType.DMA],
        [passages], 0, [pltpu.HBM],
    )
    plane = [swap(pieces[s], "tensor", s) if s else pieces[s] for s in z.tensor_order]
    plane = jnp.concatenate(plane, axis=0)
    plane, own_block, other_block = lax.optimization_barrier((plane, own_block, other_block))
    chip = [swap(plane, "corpus", s) if s else plane for s in z.corpus_order]
    if z.cuts == 1:
        chip = [jnp.concatenate(chip, axis=0)]
    arrived = gather_pairs(chip)
    others = [swap(piece[:, z.width :], "dp", 1) for piece in arrived]
    blocks = [own_block, other_block]

    work = 2 * z.rows * z.wide * z.width
    query_rows, index, pos_rows, inside, part = call(
        z, score_kernel,
        [
            shape((z.rows, z.width), bf16), shape((z.nrows, z.deep), i32),
            shape((z.named, LANES), i32), shape((z.packed, z.lanes), i32),
            shape((z.packed, z.lanes), f32),
        ],
        [
            pltpu.VMEM((z.named, LANES), f32), pltpu.VMEM((z.rows, z.lanes), i32),
            pltpu.VMEM((z.rows, z.lanes), f32),
        ],
        arrived + others + blocks, work,
    )
    (hot,) = call(z, hot_kernel, [shape((z.named, z.wide), bf16)], [], [pos_rows], work // 64)
    total = sum([swap(part, "tensor", s) for s in range(1, z.tensor)], part)
    exponent, stat = call(
        z, stat_kernel, [shape((z.packed, z.lanes), f32), shape((z.high, z.packed), f32)], [],
        [total, inside], total.size,
    )
    stats = [swap(stat, "corpus", s) if s else stat for s in z.corpus_order]
    (raw,) = call(
        z, place_kernel, [shape((z.rows, z.wide), f32)],
        [
            pltpu.VMEM((z.nrows, z.deep), f32), pltpu.VMEM((3, z.nrows, z.deep), f32),
            pltpu.VMEM((z.rows * z.chunks, LANES), f32),
        ],
        [exponent, index, hot], 3 * work,
    )
    if z.cuts == 1:
        stats = [jnp.concatenate(stats, axis=0)]
    stats = gather_pairs(stats)
    dense, other_dense, loss, size, *grads = call(
        z, weight_kernel,
        [shape((z.rows, z.block), bf16)] * 2 + [shape((z.own, LANES), f32)] * 2
        + [shape((z.half, z.width), f32)] * z.side,
        [
            pltpu.VMEM((z.side * z.corpus, z.high, z.packed), f32),
            pltpu.VMEM((LANES, z.packed), f32), pltpu.VMEM((z.packed, LANES), f32),
            pltpu.VMEM((z.rows, LANES), f32),
        ],
        stats + [raw, hot] + blocks, work,
    )
    half = scatter_pairs(grads).astype(jnp.float16).reshape(z.groups, z.own, z.width)
    half = lax.all_to_all(half, ("tensor", "corpus"), split_axis=0, concat_axis=0, tiled=True)
    (grad_pass,) = call(
        z, passage_kernel, [shape((z.block, z.width), f32)], [],
        [dense, query_rows, swap(other_dense, "dp", 1), swap(query_rows, "dp", 1)], work,
    )
    half, grad_pass = lax.optimization_barrier((half, grad_pass))
    half = half.astype(f32).reshape(z.tensor, z.corpus, z.own, z.width).sum(axis=1)
    grad_query = half.swapaxes(0, 1).reshape(z.own, z.feat) * (size[:, :1] * z.scale)
    return (grad_query, loss[:, 0], grad_pass)


def solution(mesh):
    spread = ("dp", "tensor", "corpus")
    in_specs = (P(spread, None), P(("dp", "corpus"), "tensor"), P(spread), P(spread, None))
    out_specs = (P(spread, None), P(spread), P(("dp", "corpus"), "tensor"))
    return jax.shard_map(body, mesh=mesh, in_specs=in_specs, out_specs=out_specs, check_vma=False)
```

time: 64.8 us -> 60.6 us (0.935)
  waiting for transfers between devices: 27.1 us -> 21.1 us
  Pallas kernels: 10.8 us -> 12.2 us
    ppermute x19, waiting for transfers between devices: 19.5 us -> 14.2 us  [swap(): return lax.ppermute(value, axis, [(i, i ^ bit) for i in range(size)])]
    pallas_call x7 -> x8, Pallas kernels: 10.8 us -> 12.2 us  [call(): pl.pallas_call(lambda *refs: kernel(z, *refs), out_shape=outs, in_specs=[...]
  transfers between devices with their start and end apart: 20 -> 20, of which waited for: 15 -> 11; matrix products, arithmetic and copies ran while one was open for 1% -> 2% of each run, Pallas kernels for 5% -> 11%
where the time goes in v4:
time: 60.6 us; the launch traced here: 60.3 us
  starting transfers between devices  22.8 us (38%)
  waiting for transfers between devices  21.1 us (35%)
  Pallas kernels  12.2 us (20%)
  other arithmetic  2.14 us (4%)
  local copies, waits for them, and re-layouts  1.25 us (2%)
  between operations  0.79 us (1%)
    ppermute x19, starting transfers between devices, swap(): return lax.ppermute(value, axis, [(i, i ^ bit) for i in range(size)])  17.4 us
    ppermute x19, waiting for transfers between devices, swap(): return lax.ppermute(value, axis, [(i, i ^ bit) for i in range(size)])  14.2 us
    pallas_call x8, Pallas kernels, call(): pl.pallas_call(lambda *refs: kernel(z, *refs), out_shape=outs, in_specs=[...  12.2 us
    all_to_all x1, waiting for transfers between devices, body(): lax.all_to_all(half, ('tensor', 'corpus'), split_axis=0, concat_axis=0, t...  6.95 us
    all_to_all x1, starting transfers between devices, body(): lax.all_to_all(half, ('tensor', 'corpus'), split_axis=0, concat_axis=0, t...  5.38 us
    unnamed x4, local copies, waits for them, and re-layouts  1.23 us
  transfers between devices with their start and end apart: 20, of which 11 were waited for; matrix products, arithmetic and copies ran while one was open for 2% of the time, Pallas kernels for 11%

profile of v4, /device:TPU:0, one launch (start us, length us, event | category | flops | bytes accessed | tf_op | source)
XLA Modules:
  0.0 60.3 jit_solution(17049422647154839006)
XLA Ops:
  0.6 1.7 %shard_map.67 = (bf16[16,640]{1,0:T(8,128)(2,1)}, bf16[16,640]{1,0:T(8,128)(2,1)}, bf16[16,640]{1,0:T(8,128)(2,1)}, bf16[16,640]{1,0:T(8,128)(2,1)}) custom-call(s32[16]{0:T(128)} %refs_0_.1, s32[16,32]{1,0:T(8,128)} %refs_1_.1, bf16[16,2048]{1,0:T(8,128)(2,1)} %refs_2_.1), custom_call_target="tpu_custom_call" | custom-call | bytes 149568 | tf_op jit(solution)/shard_map/pallas_call | solution.py:426
  2.8 2.6 %collective-permute-start = (bf16[16,640]{1,0:T(8,128)(2,1)}, bf16[16,640]{1,0:T(8,128)(2,1)S(1)}, u32[]{:S(2)}, u32[]{:S(2)}) collective-permute-start(bf16[16,640]{1,0:T(8,128)(2,1)} %get-tuple-element.34), channel_id=1, source_target_pairs={{0,4},{4,0},{8,12},{12,8},{1,5},{5,1},{9,13},{13,9},{2,6},{6,2},{1... | collective-permute-start | bytes 61448 | tf_op jit(solution)/shard_map/ppermute | solution.py:16
  5.4 1.5 %collective-permute-start.1 = (bf16[16,640]{1,0:T(8,128)(2,1)}, bf16[16,640]{1,0:T(8,128)(2,1)S(1)}, u32[]{:S(2)}, u32[]{:S(2)}) collective-permute-start(bf16[16,640]{1,0:T(8,128)(2,1)} %get-tuple-element.35), channel_id=1, source_target_pairs={{0,8},{4,12},{8,0},{12,4},{1,9},{5,13},{9,1},{13,5},{2,10},{6,14},... | collective-permute-start | bytes 61448 | tf_op jit(solution)/shard_map/ppermute | solution.py:16
  6.9 1.2 %copy-done = bf16[1024,512]{1,0:T(8,128)(2,1)S(1)} copy-done((bf16[1024,512]{1,0:T(8,128)(2,1)S(1)}, bf16[1024,512]{1,0:T(8,128)(2,1)}, u32[]{:S(2)}) %copy-start) | copy-done | bytes 1048600
  8.2 1.1 %collective-permute-done.1 = bf16[16,640]{1,0:T(8,128)(2,1)S(1)} collective-permute-done((bf16[16,640]{1,0:T(8,128)(2,1)}, bf16[16,640]{1,0:T(8,128)(2,1)S(1)}, u32[]{:S(2)}, u32[]{:S(2)}) %collective-permute-start.1) | collective-permute-done | bytes 20512 | tf_op jit(solution)/shard_map/ppermute | solution.py:16
  9.4 2.4 %collective-permute-done.2 = bf16[16,640]{1,0:T(8,128)(2,1)S(1)} collective-permute-done((bf16[16,640]{1,0:T(8,128)(2,1)}, bf16[16,640]{1,0:T(8,128)(2,1)S(1)}, u32[]{:S(2)}, u32[]{:S(2)}) %collective-permute-start.2) | collective-permute-done | bytes 20512 | tf_op jit(solution)/shard_map/ppermute | solution.py:16
  11.8 1.6 %collective-permute-start.6 = (bf16[64,640]{1,0:T(8,128)(2,1)S(1)}, bf16[64,640]{1,0:T(8,128)(2,1)S(1)}, u32[]{:S(2)}, u32[]{:S(2)}) collective-permute-start(bf16[64,640]{1,0:T(8,128)(2,1)S(1)} %pad_maximum_fusion.refs_0_), channel_id=1, source_target_pairs={{0,1},{1,0},{2,3},{3,2},{4,5},{5,4},{6,7},{7,6},{8,9},{9,8},{10,11... | collective-permute-start | bytes 245768 | tf_op jit(solution)/shard_map/ppermute | solution.py:16
  13.5 2.5 %collective-permute-start.4 = (bf16[64,640]{1,0:T(8,128)(2,1)S(1)}, bf16[64,640]{1,0:T(8,128)(2,1)S(1)}, u32[]{:S(2)}, u32[]{:S(2)}) collective-permute-start(bf16[64,640]{1,0:T(8,128)(2,1)S(1)} %pad_maximum_fusion.refs_0_), channel_id=1, source_target_pairs={{0,3},{1,2},{2,1},{3,0},{4,7},{5,6},{6,5},{7,4},{8,11},{9,10},{10,... | collective-permute-start | bytes 245768 | tf_op jit(solution)/shard_map/ppermute | solution.py:16
  16.6 3.6 %collective-permute-done.4.refs_1_ = bf16[64,640]{1,0:T(8,128)(2,1)S(1)} collective-permute-done((bf16[64,640]{1,0:T(8,128)(2,1)S(1)}, bf16[64,640]{1,0:T(8,128)(2,1)S(1)}, u32[]{:S(2)}, u32[]{:S(2)}) %collective-permute-start.4) | collective-permute-done | bytes 81952 | tf_op jit(solution)/shard_map/ppermute | solution.py:16
  20.2 2.6 %collective-permute-done.5.refs_2_ = bf16[64,640]{1,0:T(8,128)(2,1)S(1)} collective-permute-done((bf16[64,640]{1,0:T(8,128)(2,1)S(1)}, bf16[64,640]{1,0:T(8,128)(2,1)S(1)}, u32[]{:S(2)}, u32[]{:S(2)}) %collective-permute-start.5) | collective-permute-done | bytes 81952 | tf_op jit(solution)/shard_map/ppermute | solution.py:16
  22.9 1.2 %collective-permute-done.9.refs_6_ = bf16[64,128]{1,0:T(8,128)(2,1)S(1)} collective-permute-done((bf16[64,128]{1,0:T(8,128)(2,1)S(1)}, bf16[64,128]{1,0:T(8,128)(2,1)S(1)}, u32[]{:S(2)}, u32[]{:S(2)}) %collective-permute-start.9) | collective-permute-done | bytes 16416 | tf_op jit(solution)/shard_map/ppermute | solution.py:16
  24.0 2.5 %shard_map.69 = (bf16[256,512]{1,0:T(8,128)(2,1)S(1)}, s32[32,256]{1,0:T(8,128)S(1)}, s32[512,128]{1,0:T(8,128)S(1)}, s32[128,128]{1,0:T(8,128)S(1)}, f32[128,128]{1,0:T(8,128)S(1)}) custom-call(bf16[64,640]{1,0:T(8,128)(2,1)S(1)} %pad_maximum_fusion.refs_0_, bf16[64,640]{1,0:T(8,128)(2,1)S(1)} %collective-permute-done.4.refs_1_, ...), custom_call_target="tpu_custom_call" | custom-call | flops 536870912 | bytes 3178496 | tf_op jit(solution)/shard_map/pallas_call | solution.py:426
  27.7 2.4 %collective-permute-start.13 = (f32[128,128]{1,0:T(8,128)S(1)}, f32[128,128]{1,0:T(8,128)S(1)}, u32[]{:S(2)}, u32[]{:S(2)}) collective-permute-start(f32[128,128]{1,0:T(8,128)S(1)} %get-tuple-element.41), channel_id=1, source_target_pairs={{0,12},{4,8},{8,4},{12,0},{1,13},{5,9},{9,5},{13,1},{2,14},{6,10},... | collective-permute-start | bytes 196616 | tf_op jit(solution)/shard_map/ppermute | solution.py:16
  31.0 1.1 %collective-permute-done.12 = f32[128,128]{1,0:T(8,128)S(1)} collective-permute-done((f32[128,128]{1,0:T(8,128)S(1)}, f32[128,128]{1,0:T(8,128)S(1)}, u32[]{:S(2)}, u32[]{:S(2)}) %collective-permute-start.12) | collective-permute-done | bytes 65568 | tf_op jit(solution)/shard_map/ppermute | solution.py:16
  32.1 0.8 %collective-permute-done.13 = f32[128,128]{1,0:T(8,128)S(1)} collective-permute-done((f32[128,128]{1,0:T(8,128)S(1)}, f32[128,128]{1,0:T(8,128)S(1)}, u32[]{:S(2)}, u32[]{:S(2)}) %collective-permute-start.13) | collective-permute-done | bytes 65568 | tf_op jit(solution)/shard_map/ppermute | solution.py:16
  33.1 2.6 %collective-permute-start.14 = (f32[8,128]{1,0:T(8,128)S(1)}, f32[8,128]{1,0:T(8,128)S(1)}, u32[]{:S(2)}, u32[]{:S(2)}) collective-permute-start(f32[8,128]{1,0:T(8,128)S(1)} %get-tuple-element.43.refs_0_), channel_id=1, source_target_pairs={{0,3},{1,2},{2,1},{3,0},{4,7},{5,6},{6,5},{7,4},{8,11},{9,10},{10,... | collective-permute-start | bytes 12296 | tf_op jit(solution)/shard_map/ppermute | solution.py:16
  35.7 1.9 %collective-permute-start.16 = (f32[8,128]{1,0:T(8,128)S(1)}, f32[8,128]{1,0:T(8,128)S(1)}, u32[]{:S(2)}, u32[]{:S(2)}) collective-permute-start(f32[8,128]{1,0:T(8,128)S(1)} %get-tuple-element.43.refs_0_), channel_id=1, source_target_pairs={{0,1},{1,0},{2,3},{3,2},{4,5},{5,4},{6,7},{7,6},{8,9},{9,8},{10,11... | collective-permute-start | bytes 12296 | tf_op jit(solution)/shard_map/ppermute | solution.py:16
  37.6 3.4 %shard_map.72.refs_4_ = f32[256,2048]{1,0:T(8,128)S(1)} custom-call(f32[128,128]{1,0:T(8,128)S(1)} %get-tuple-element.44.refs_0_, s32[32,256]{1,0:T(8,128)S(1)} %get-tuple-element.45.refs_1_, bf16[512,2048]{1,0:T(8,128)(2,1)S(1)} %shard_map.71.refs_2_.refs_5_), custom_call_target="tpu_custom_call" | custom-call | flops 1610612736 | bytes 4292608 | tf_op jit(solution)/shard_map/pallas_call | solution.py:426
  41.0 1.1 %shard_map.73 = (bf16[256,1024]{1,0:T(8,128)(2,1)S(1)}, bf16[256,1024]{1,0:T(8,128)(2,1)S(1)}, f32[16,128]{1,0:T(8,128)S(1)}, f32[16,128]{1,0:T(8,128)S(1)}, f32[256,512]{1,0:T(8,128)S(1)}) custom-call(f32[8,128]{1,0:T(8,128)S(1)} %get-tuple-element.43.refs_0_, f32[8,128]{1,0:T(8,128)S(1)} %collective-permute-done.14.refs_1_, ...), custom_call_target="tpu_custom_call" | custom-call | flops 536870912 | bytes 7897088 | tf_op jit(solution)/shard_map/pallas_call | solution.py:426
  42.1 0.7 %convert_element_type.4 = f16[256,512]{1,0:T(8,128)(2,1)} convert(f32[256,512]{1,0:T(8,128)S(1)} %get-tuple-element.47) | non-fusion elementwise | flops 131072 | bytes 786432 | tf_op jit(solution)/shard_map/convert_element_type | solution.py:509
  42.9 5.4 %all-to-all-start = ((f16[16,16,512]{2,1,0:T(8,128)(2,1)}), f16[16,16,512]{2,1,0:T(8,128)(2,1)S(1)}, u32[]{:S(2)}, u32[]{:S(2)}) async-start(f16[16,16,512]{2,1,0:T(8,128)(2,1)} %bitcast), calls=%async_computation | async-start | bytes 524288 | tf_op jit(solution)/shard_map/all_to_all | solution.py:510
  49.9 2.7 %shard_map.74 = f32[1024,512]{1,0:T(8,128)} custom-call(bf16[256,1024]{1,0:T(8,128)(2,1)S(1)} %get-tuple-element.48.refs_0_, bf16[256,512]{1,0:T(8,128)(2,1)S(1)} %get-tuple-element.49.refs_1_, bf16[256,1024]{1,0:T(8,128)(2,1)S(1)} %collective-permute-done.17.refs_2_, bf16[256,512]{1,0:T(8,128)(2,1)S(1)} %collective-permute-done.18.refs_3_), custom_call_target="tpu_custom_call" | custom-call | flops 536870912 | bytes 3670016 | tf_op jit(solution)/shard_map/pallas_call | solution.py:426
  52.5 6.9 %all-to-all-done = f16[16,16,512]{2,1,0:T(8,128)(2,1)S(1)} async-done(((f16[16,16,512]{2,1,0:T(8,128)(2,1)}), f16[16,16,512]{2,1,0:T(8,128)(2,1)S(1)}, u32[]{:S(2)}, u32[]{:S(2)}) %all-to-all-start) | async-done | bytes 262176 | tf_op jit(solution)/shard_map/all_to_all | solution.py:510
  59.5 0.7 %broadcast_multiply_fusion = f32[16,2048]{1,0:T(8,128)} fusion(f32[16,2048]{1,0:T(8,128)S(1)} %bitcast.8, f32[16]{0:T(128)S(1)} %get-tuple-element.56), kind=kLoop, calls=%fused_computation.2 | loop fusion | flops 32768 | bytes 262208 | tf_op jit(solution)/shard_map/mul | solution.py:517
  (39 shorter events, 5.3 us)
Async XLA Ops:
  2.3 9.5 %collective-permute-start.3 = (bf16[1024,512]{1,0:T(8,128)(2,1)}, bf16[1024,512]{1,0:T(8,128)(2,1)S(1)}, u32[]{:S(2)}, u32[]{:S(2)}) collective-permute-start(bf16[1024,512]{1,0:T(8,128)(2,1)} %refs_0_.2), channel_id=1, source_target_pairs={{0,16},{16,0},{1,17},{17,1},{2,18},{18,2},{3,19},{19,3},{4,20},{20... | collective-permute-start | bytes 3145736 | tf_op jit(solution)/shard_map/ppermute | solution.py:16
  2.8 5.4 %collective-permute-start = (bf16[16,640]{1,0:T(8,128)(2,1)}, bf16[16,640]{1,0:T(8,128)(2,1)S(1)}, u32[]{:S(2)}, u32[]{:S(2)}) collective-permute-start(bf16[16,640]{1,0:T(8,128)(2,1)} %get-tuple-element.34), channel_id=1, source_target_pairs={{0,4},{4,0},{8,12},{12,8},{1,5},{5,1},{9,13},{13,9},{2,6},{6,2},{1... | collective-permute-start | bytes 61448 | tf_op jit(solution)/shard_map/ppermute | solution.py:16
  5.4 4.0 %collective-permute-start.1 = (bf16[16,640]{1,0:T(8,128)(2,1)}, bf16[16,640]{1,0:T(8,128)(2,1)S(1)}, u32[]{:S(2)}, u32[]{:S(2)}) collective-permute-start(bf16[16,640]{1,0:T(8,128)(2,1)} %get-tuple-element.35), channel_id=1, source_target_pairs={{0,8},{4,12},{8,0},{12,4},{1,9},{5,13},{9,1},{13,5},{2,10},{6,14},... | collective-permute-start | bytes 61448 | tf_op jit(solution)/shard_map/ppermute | solution.py:16
  6.9 4.9 %collective-permute-start.2 = (bf16[16,640]{1,0:T(8,128)(2,1)}, bf16[16,640]{1,0:T(8,128)(2,1)S(1)}, u32[]{:S(2)}, u32[]{:S(2)}) collective-permute-start(bf16[16,640]{1,0:T(8,128)(2,1)} %get-tuple-element.36), channel_id=1, source_target_pairs={{0,12},{4,8},{8,4},{12,0},{1,13},{5,9},{9,5},{13,1},{2,14},{6,10},... | collective-permute-start | bytes 61448 | tf_op jit(solution)/shard_map/ppermute | solution.py:16
  6.9 1.2 %copy-start = (bf16[1024,512]{1,0:T(8,128)(2,1)S(1)}, bf16[1024,512]{1,0:T(8,128)(2,1)}, u32[]{:S(2)}) copy-start(bf16[1024,512]{1,0:T(8,128)(2,1)} %refs_0_.2) | copy-start | bytes 3145732
  8.1 3.6 %copy-start.1 = (bf16[16,640]{1,0:T(8,128)(2,1)S(1)}, bf16[16,640]{1,0:T(8,128)(2,1)}, u32[]{:S(2)}) copy-start(bf16[16,640]{1,0:T(8,128)(2,1)} %get-tuple-element.33) | copy-start | bytes 61444
  11.8 4.5 %collective-permute-start.6 = (bf16[64,640]{1,0:T(8,128)(2,1)S(1)}, bf16[64,640]{1,0:T(8,128)(2,1)S(1)}, u32[]{:S(2)}, u32[]{:S(2)}) collective-permute-start(bf16[64,640]{1,0:T(8,128)(2,1)S(1)} %pad_maximum_fusion.refs_0_), channel_id=1, source_target_pairs={{0,1},{1,0},{2,3},{3,2},{4,5},{5,4},{6,7},{7,6},{8,9},{9,8},{10,11... | collective-permute-start | bytes 245768 | tf_op jit(solution)/shard_map/ppermute | solution.py:16
  13.5 6.7 %collective-permute-start.4 = (bf16[64,640]{1,0:T(8,128)(2,1)S(1)}, bf16[64,640]{1,0:T(8,128)(2,1)S(1)}, u32[]{:S(2)}, u32[]{:S(2)}) collective-permute-start(bf16[64,640]{1,0:T(8,128)(2,1)S(1)} %pad_maximum_fusion.refs_0_), channel_id=1, source_target_pairs={{0,3},{1,2},{2,1},{3,0},{4,7},{5,6},{6,5},{7,4},{8,11},{9,10},{10,... | collective-permute-start | bytes 245768 | tf_op jit(solution)/shard_map/ppermute | solution.py:16
  15.9 6.9 %collective-permute-start.5 = (bf16[64,640]{1,0:T(8,128)(2,1)S(1)}, bf16[64,640]{1,0:T(8,128)(2,1)S(1)}, u32[]{:S(2)}, u32[]{:S(2)}) collective-permute-start(bf16[64,640]{1,0:T(8,128)(2,1)S(1)} %pad_maximum_fusion.refs_0_), channel_id=1, source_target_pairs={{0,2},{1,3},{2,0},{3,1},{4,6},{5,7},{6,4},{7,5},{8,10},{9,11},{10,... | collective-permute-start | bytes 245768 | tf_op jit(solution)/shard_map/ppermute | solution.py:16
  16.0 6.8 %collective-permute-start.7 = (bf16[64,128]{1,0:T(8,128)(2,1)S(1)}, bf16[64,128]{1,0:T(8,128)(2,1)S(1)}, u32[]{:S(2)}, u32[]{:S(2)}) collective-permute-start(bf16[64,128]{1,0:T(8,128)(2,1)S(1)} %slice.18), channel_id=1, source_target_pairs={{0,16},{16,0},{1,17},{17,1},{2,18},{18,2},{3,19},{19,3},{4,20},{20... | collective-permute-start | bytes 49160 | tf_op jit(solution)/shard_map/ppermute | solution.py:16
  16.3 6.5 %collective-permute-start.10 = (bf16[64,128]{1,0:T(8,128)(2,1)S(1)}, bf16[64,128]{1,0:T(8,128)(2,1)S(1)}, u32[]{:S(2)}, u32[]{:S(2)}) collective-permute-start(bf16[64,128]{1,0:T(8,128)(2,1)S(1)} %slice.26), channel_id=1, source_target_pairs={{0,16},{16,0},{1,17},{17,1},{2,18},{18,2},{3,19},{19,3},{4,20},{20... | collective-permute-start | bytes 49160 | tf_op jit(solution)/shard_map/ppermute | solution.py:16
  20.2 2.7 %collective-permute-start.8 = (bf16[64,128]{1,0:T(8,128)(2,1)S(1)}, bf16[64,128]{1,0:T(8,128)(2,1)S(1)}, u32[]{:S(2)}, u32[]{:S(2)}) collective-permute-start(bf16[64,128]{1,0:T(8,128)(2,1)S(1)} %slice.24), channel_id=1, source_target_pairs={{0,16},{16,0},{1,17},{17,1},{2,18},{18,2},{3,19},{19,3},{4,20},{20... | collective-permute-start | bytes 49160 | tf_op jit(solution)/shard_map/ppermute | solution.py:16
  22.9 1.2 %collective-permute-start.9 = (bf16[64,128]{1,0:T(8,128)(2,1)S(1)}, bf16[64,128]{1,0:T(8,128)(2,1)S(1)}, u32[]{:S(2)}, u32[]{:S(2)}) collective-permute-start(bf16[64,128]{1,0:T(8,128)(2,1)S(1)} %slice.25), channel_id=1, source_target_pairs={{0,16},{16,0},{1,17},{17,1},{2,18},{18,2},{3,19},{19,3},{4,20},{20... | collective-permute-start | bytes 49160 | tf_op jit(solution)/shard_map/ppermute | solution.py:16
  26.5 4.4 %collective-permute-start.11 = (f32[128,128]{1,0:T(8,128)S(1)}, f32[128,128]{1,0:T(8,128)S(1)}, u32[]{:S(2)}, u32[]{:S(2)}) collective-permute-start(f32[128,128]{1,0:T(8,128)S(1)} %get-tuple-element.41), channel_id=1, source_target_pairs={{0,4},{4,0},{8,12},{12,8},{1,5},{5,1},{9,13},{13,9},{2,6},{6,2},{1... | collective-permute-start | bytes 196616 | tf_op jit(solution)/shard_map/ppermute | solution.py:16
  27.1 5.0 %collective-permute-start.12 = (f32[128,128]{1,0:T(8,128)S(1)}, f32[128,128]{1,0:T(8,128)S(1)}, u32[]{:S(2)}, u32[]{:S(2)}) collective-permute-start(f32[128,128]{1,0:T(8,128)S(1)} %get-tuple-element.41), channel_id=1, source_target_pairs={{0,8},{4,12},{8,0},{12,4},{1,9},{5,13},{9,1},{13,5},{2,10},{6,14},... | collective-permute-start | bytes 196616 | tf_op jit(solution)/shard_map/ppermute | solution.py:16
  27.7 5.2 %collective-permute-start.13 = (f32[128,128]{1,0:T(8,128)S(1)}, f32[128,128]{1,0:T(8,128)S(1)}, u32[]{:S(2)}, u32[]{:S(2)}) collective-permute-start(f32[128,128]{1,0:T(8,128)S(1)} %get-tuple-element.41), channel_id=1, source_target_pairs={{0,12},{4,8},{8,4},{12,0},{1,13},{5,9},{9,5},{13,1},{2,14},{6,10},... | collective-permute-start | bytes 196616 | tf_op jit(solution)/shard_map/ppermute | solution.py:16
  33.1 7.8 %collective-permute-start.14 = (f32[8,128]{1,0:T(8,128)S(1)}, f32[8,128]{1,0:T(8,128)S(1)}, u32[]{:S(2)}, u32[]{:S(2)}) collective-permute-start(f32[8,128]{1,0:T(8,128)S(1)} %get-tuple-element.43.refs_0_), channel_id=1, source_target_pairs={{0,3},{1,2},{2,1},{3,0},{4,7},{5,6},{6,5},{7,4},{8,11},{9,10},{10,... | collective-permute-start | bytes 12296 | tf_op jit(solution)/shard_map/ppermute | solution.py:16
  35.7 5.3 %collective-permute-start.15 = (f32[8,128]{1,0:T(8,128)S(1)}, f32[8,128]{1,0:T(8,128)S(1)}, u32[]{:S(2)}, u32[]{:S(2)}) collective-permute-start(f32[8,128]{1,0:T(8,128)S(1)} %get-tuple-element.43.refs_0_), channel_id=1, source_target_pairs={{0,2},{1,3},{2,0},{3,1},{4,6},{5,7},{6,4},{7,5},{8,10},{9,11},{10,... | collective-permute-start | bytes 12296 | tf_op jit(solution)/shard_map/ppermute | solution.py:16
  35.7 5.3 %collective-permute-start.16 = (f32[8,128]{1,0:T(8,128)S(1)}, f32[8,128]{1,0:T(8,128)S(1)}, u32[]{:S(2)}, u32[]{:S(2)}) collective-permute-start(f32[8,128]{1,0:T(8,128)S(1)} %get-tuple-element.43.refs_0_), channel_id=1, source_target_pairs={{0,1},{1,0},{2,3},{3,2},{4,5},{5,4},{6,7},{7,6},{8,9},{9,8},{10,11... | collective-permute-start | bytes 12296 | tf_op jit(solution)/shard_map/ppermute | solution.py:16
  42.1 7.8 %collective-permute-start.17 = (bf16[256,1024]{1,0:T(8,128)(2,1)S(1)}, bf16[256,1024]{1,0:T(8,128)(2,1)S(1)}, u32[]{:S(2)}, u32[]{:S(2)}) collective-permute-start(bf16[256,1024]{1,0:T(8,128)(2,1)S(1)} %get-tuple-element.50), channel_id=1, source_target_pairs={{0,16},{16,0},{1,17},{17,1},{2,18},{18,2},{3,19},{19,3},{4,20},{20... | collective-permute-start | bytes 1572872 | tf_op jit(solution)/shard_map/ppermute | solution.py:16
  42.9 16.6 %all-to-all-start = ((f16[16,16,512]{2,1,0:T(8,128)(2,1)}), f16[16,16,512]{2,1,0:T(8,128)(2,1)S(1)}, u32[]{:S(2)}, u32[]{:S(2)}) async-start(f16[16,16,512]{2,1,0:T(8,128)(2,1)} %bitcast), calls=%async_computation | async-start | bytes 524288 | tf_op jit(solution)/shard_map/all_to_all | solution.py:510
  48.3 1.6 %collective-permute-start.18 = (bf16[256,512]{1,0:T(8,128)(2,1)S(1)}, bf16[256,512]{1,0:T(8,128)(2,1)S(1)}, u32[]{:S(2)}, u32[]{:S(2)}) collective-permute-start(bf16[256,512]{1,0:T(8,128)(2,1)S(1)} %get-tuple-element.49.refs_1_), channel_id=1, source_target_pairs={{0,16},{16,0},{1,17},{17,1},{2,18},{18,2},{3,19},{19,3},{4,20},{20... | collective-permute-start | bytes 786440 | tf_op jit(solution)/shard_map/ppermute | solution.py:16

commit v5 on v4

--- a/solution.py
+++ b/solution.py
@@ -8,7 +8,7 @@
 LANES = 128
 FAR = -(2**20)
 LOW = -1e30
-PLANE, ZED = [0, 1, 2, 3], [0, 3, 2, 1]
+SUM, ZED = [3, 2, 1], [0, 2, 3, 1]
 
 
 def swap(value, axis, bit):
@@ -56,7 +56,7 @@
         self.wide = 2 * self.block
         self.chunks = self.wide // LANES
         self.scale = self.feat ** (-0.5)
-        self.tensor_order = PLANE if self.tensor == 4 else list(range(self.tensor))
+        self.tensor_order = SUM if self.tensor == 4 else list(range(1, self.tensor))
         self.corpus_order = ZED if self.corpus == 4 else list(range(self.corpus))
         self.cuts = self.corpus if self.side == 1 else 1
         self.deep = 2 * LANES
@@ -77,10 +77,7 @@
     return pl.ds(pl.multiple_of(start, size), size)
 
 
-def message_kernel(z, pos_in, neg_in, query_in, *refs):
-    piece_refs = refs[: z.tensor]
-    pos_ref, neg_ref, query_ref, sems = refs[z.tensor :]
-    t = lax.axis_index("tensor")
+def message_kernel(z, pos_in, neg_in, query_in, out_ref, pos_ref, neg_ref, query_ref, sems):
     moves = [
         pltpu.make_async_copy(source, target, sems.at[i])
         for i, (source, target) in enumerate(
@@ -100,10 +97,10 @@
     ids = jnp.concatenate([part for part in [pos[:, : z.neg_at]] + ids if part.shape[1]], axis=1)
     ids = jnp.concatenate([ids >> 8, ids & 255], axis=1)
     code = ids.astype(jnp.float32).astype(jnp.bfloat16)
-    for s in range(z.tensor):
-        at = pl.ds(pl.multiple_of((t ^ s) * z.width, LANES), z.width)
-        piece_refs[s][:, : z.width] = query_ref[:, at]
-        piece_refs[s][:, z.width :] = code
+    for k in range(z.groups):
+        t = k // z.corpus
+        out_ref[k, :, : z.width] = query_ref[:, t * z.width : (t + 1) * z.width]
+        out_ref[k, :, z.width :] = code
 
 
 def fetch_kernel(z, block_ref, passage_ref, sem):
@@ -128,25 +125,28 @@
 
 
 def score_kernel(z, *refs):
-    count = z.side * z.cuts
-    arrived, others, refs = refs[:count], refs[count : 2 * count], refs[2 * count :]
-    block_refs, (query_ref, index_ref, pos_ref, inside_ref, part_ref) = refs[:2], refs[2:7]
-    id_ref, local_ref, logit_ref = refs[7:]
-    d, t, c = places()
+    arrived, block_refs = refs[: z.side], refs[z.side : z.side + 2]
+    query_ref, score_ref = refs[z.side + 2 :]
+    d = lax.axis_index("dp")
     for su in range(z.side):
-        for sc in range(z.corpus):
-            for st in range(z.tensor):
-                piece = su * z.cuts + sc % z.cuts
-                source = pl.ds((sc // z.cuts * z.tensor + st) * z.own, z.own)
-                from_d = d ^ (2 * su)
-                place = (t ^ z.tensor_order[st]) * z.corpus + (c ^ z.corpus_order[sc])
-                row = rows_at(((from_d >> 1) * z.groups + place) * z.own, z.own)
-                query_ref[row, :] = arrived[piece][source, : z.width]
-                codes = [arrived[piece][source, z.width :], others[piece][source, :]]
-                for side, code in enumerate(codes):
-                    code = code.astype(jnp.float32)
-                    row = rows_at(((from_d ^ side) * z.groups + place) * z.own, z.own)
-                    id_ref[row, :] = code * 256.0 + pltpu.roll(code, LANES // 2, 1)
+        at = rows_at(((d ^ (2 * su)) >> 1) * z.half, z.half)
+        query_ref[at, :] = arrived[su][:, : z.width]
+    step = min(z.rows, 256)
+
+    def score(i, carry):
+        at = rows_at(i * step, step)
+        for side, block_ref in enumerate(block_refs):
+            score_ref[at, side * z.block : (side + 1) * z.block] = lax.dot_general(
+                query_ref[at, :], block_ref[...], (((1,), (1,)), ((), ())),
+                preferred_element_type=jnp.float32,
+            )
+        return carry
+
+    lax.fori_loop(0, z.rows // step, score, 0, unroll=z.rows == step)
+
+
+def localizer(z):
+    d, _, c = places()
 
     def localize(ids):
         found = jnp.full(ids.shape, float(FAR), jnp.float32)
@@ -156,6 +156,20 @@
             found = jnp.where(inside, local + float(side * z.block), found)
         return found
 
+    return localize
+
+
+def pick_kernel(z, *refs):
+    arrived, others, score_ref = refs[: z.side], refs[z.side : 2 * z.side], refs[2 * z.side]
+    part_ref, local_ref, id_ref, logit_ref = refs[2 * z.side + 1 :]
+    d = lax.axis_index("dp")
+    localize = localizer(z)
+    for su in range(z.side):
+        from_d = d ^ (2 * su)
+        for side, code in enumerate([arrived[su][:, z.width :], others[su][...]]):
+            code = code.astype(jnp.float32)
+            at = rows_at((from_d ^ side) * z.half, z.half)
+            id_ref[at, :] = code * 256.0 + pltpu.roll(code, LANES // 2, 1)
     wide = -(-z.columns // LANES) * LANES
     row = lax.broadcasted_iota(jnp.int32, (z.half, wide), 0) & (z.own - 1)
     col = lax.broadcasted_iota(jnp.int32, (z.half, wide), 1)
@@ -163,7 +177,6 @@
     for h in range(z.dp):
         at = pl.ds(h * z.half, z.half)
         pos = jnp.broadcast_to(id_ref[at, z.pos_at : z.pos_at + 1], (z.half, wide))
-        pos_ref[at, :] = localize(pos[:, :LANES]).astype(jnp.int32)
         kept = jnp.where(col == row + h * z.own, pos, 0.0)
         group_ids += jnp.sum(kept.reshape(z.groups, z.own, wide), axis=1)
     batch_ids = jnp.broadcast_to(group_ids[:, None, :], (z.groups, z.own, wide))
@@ -177,47 +190,47 @@
                 named = jnp.where(lane + base < z.columns, batch_ids[:, base : base + LANES], ids)
             local = jnp.where(lane + base < z.items, localize(named), float(FAR))
             local_ref[pl.ds(u * z.half, z.half), base : base + LANES] = local.astype(jnp.int32)
-    step = min(z.rows, 128)
-
-    def score(i, carry):
+    step = min(z.rows, 256)
+
+    def pick(i, carry):
         at = rows_at(i * step, step)
-        scores = [
-            lax.dot_general(
-                query_ref[at, :], block_ref[...], (((1,), (1,)), ((), ())),
-                preferred_element_type=jnp.float32,
-            )
-            for block_ref in block_refs
-        ]
-        each = z.block // LANES
         for base in range(0, z.lanes, LANES):
             local = local_ref[at, base : base + LANES]
             chunk, within = local >> 7, local & (LANES - 1)
             picked = jnp.zeros((step, LANES), jnp.float32)
             for j in range(z.chunks):
-                k = j % each * LANES
-                found = jnp.take_along_axis(scores[j // each][:, k : k + LANES], within, axis=1)
+                found = jnp.take_along_axis(
+                    score_ref[at, j * LANES : (j + 1) * LANES], within, axis=1
+                )
                 picked = jnp.where(chunk == j, found, picked)
             logit_ref[at, base : base + LANES] = picked
         return carry
 
-    lax.fori_loop(0, z.rows // step, score, 0)
+    lax.fori_loop(0, z.rows // step, pick, 0, unroll=z.rows == step)
+    pack_rows(z, logit_ref, part_ref)
+
+
+def pack_rows(z, source_ref, target_ref):
+    lane = lax.broadcasted_iota(jnp.int32, (z.packed, z.lanes), 1)
+    packed = source_ref[pl.ds(0, z.packed), :]
+    for h in range(1, z.pack):
+        other = pltpu.roll(source_ref[pl.ds(h * z.packed, z.packed), :], h * z.items, 1)
+        packed = jnp.where(lane < h * z.items, packed, other)
+    target_ref[...] = packed
+
+
+def index_kernel(z, local_ref, id_ref, index_ref, inside_ref, hot_ref):
     seat_rows(z, index_ref, lambda j: (local_ref, j * z.nrows, z.columns))
-    for source_ref, target_ref in [(logit_ref, part_ref), (local_ref, inside_ref)]:
-        lane = lax.broadcasted_iota(jnp.int32, (z.packed, z.lanes), 1)
-        packed = source_ref[pl.ds(0, z.packed), :]
-        for h in range(1, z.pack):
-            other = pltpu.roll(source_ref[pl.ds(h * z.packed, z.packed), :], h * z.items, 1)
-            packed = jnp.where(lane < h * z.items, packed, other)
-        target_ref[...] = packed
-
-
-def hot_kernel(z, pos_ref, hot_ref):
+    pack_rows(z, local_ref, inside_ref)
+    localize = localizer(z)
     lane = lax.broadcasted_iota(jnp.int32, (z.half, LANES), 1)
     for h in range(z.dp):
         at = pl.ds(h * z.half, z.half)
+        pos = localize(jnp.broadcast_to(id_ref[at, z.pos_at : z.pos_at + 1], (z.half, LANES)))
+        pos = pos.astype(jnp.int32)
         for j in range(z.chunks):
-            same = pos_ref[at, :] == lane + j * LANES
-            hot_ref[at, j * LANES : (j + 1) * LANES] = jnp.where(same, 1.0, 0.0).astype(jnp.bfloat16)
+            same = jnp.where(pos == lane + j * LANES, 1.0, 0.0).astype(jnp.bfloat16)
+            hot_ref[at, j * LANES : (j + 1) * LANES] = same
 
 
 def stat_kernel(z, total_ref, inside_ref, exponent_ref, stat_ref):
@@ -282,7 +295,7 @@
     tall = lax.broadcasted_iota(jnp.int32, shape, 0).astype(jnp.bfloat16)
     shift = lax.broadcasted_iota(jnp.int32, (1, z.deep), 1) // z.negs * z.chunks
     spread = lax.broadcasted_iota(jnp.int32, (LANES, z.deep), 0).astype(jnp.bfloat16)
-    turns = min(16, z.nrows)
+    turns = min(32, z.nrows)
     none, unit = jnp.bfloat16(0), jnp.bfloat16(1)
 
     def place(i, carry):
@@ -309,7 +322,7 @@
                 tile_ref[at, :] = tiles[j * z.chunks : (j + 1) * z.chunks, :]
         return carry
 
-    lax.fori_loop(0, z.nrows // turns, place, 0)
+    lax.fori_loop(0, z.nrows // turns, place, 0, unroll=z.nrows == turns)
     lane = lax.broadcasted_iota(jnp.int32, (z.run, LANES), 1)
     group = lax.broadcasted_iota(jnp.int32, (z.run, LANES), 0) // z.own
     for n in range(z.sets):
@@ -440,7 +453,7 @@
     shape = jax.ShapeDtypeStruct
 
     pieces = call(
-        z, message_kernel, [shape((z.own, z.width + LANES), bf16)] * z.tensor,
+        z, message_kernel, [shape((z.groups, z.own, z.width + LANES), bf16)],
         [
             pltpu.SMEM(pos_ids.shape, i32), pltpu.VMEM(neg_ids.shape, i32),
             pltpu.VMEM(queries.shape, bf16), pltpu.SemaphoreType.DMA((3,)),
@@ -448,37 +461,39 @@
         [pos_ids, neg_ids, queries], 0, [pltpu.HBM] * 3, 60 * 2**20,
     )
     passages, pieces = lax.optimization_barrier((passages, pieces))
-    other_block = swap(passages, "dp", 1)
     (own_block,) = call(
         z, fetch_kernel, [shape(passages.shape, bf16)], [pltpu.SemaphoreType.DMA],
         [passages], 0, [pltpu.HBM],
     )
-    plane = [swap(pieces[s], "tensor", s) if s else pieces[s] for s in z.tensor_order]
-    plane = jnp.concatenate(plane, axis=0)
-    plane, own_block, other_block = lax.optimization_barrier((plane, own_block, other_block))
-    chip = [swap(plane, "corpus", s) if s else plane for s in z.corpus_order]
-    if z.cuts == 1:
-        chip = [jnp.concatenate(chip, axis=0)]
-    arrived = gather_pairs(chip)
+    other_block = swap(passages, "dp", 1)
+    chip = lax.all_to_all(pieces[0], ("tensor", "corpus"), split_axis=0, concat_axis=0, tiled=True)
+    chip, own_block, other_block = lax.optimization_barrier((chip, own_block, other_block))
+    arrived = gather_pairs([chip.reshape(z.half, z.width + LANES)])
     others = [swap(piece[:, z.width :], "dp", 1) for piece in arrived]
     blocks = [own_block, other_block]
 
     work = 2 * z.rows * z.wide * z.width
-    query_rows, index, pos_rows, inside, part = call(
-        z, score_kernel,
+    query_rows, scores = call(
+        z, score_kernel, [shape((z.rows, z.width), bf16), shape((z.rows, z.wide), f32)], [],
+        arrived + blocks, work,
+    )
+    part, local, ids = call(
+        z, pick_kernel,
         [
-            shape((z.rows, z.width), bf16), shape((z.nrows, z.deep), i32),
-            shape((z.named, LANES), i32), shape((z.packed, z.lanes), i32),
-            shape((z.packed, z.lanes), f32),
+            shape((z.packed, z.lanes), f32), shape((z.rows, z.lanes), i32),
+            shape((z.named, LANES), f32),
         ],
+        [pltpu.VMEM((z.rows, z.lanes), f32)], arrived + others + [scores], work // 16,
+    )
+    index, inside, hot = call(
+        z, index_kernel,
         [
-            pltpu.VMEM((z.named, LANES), f32), pltpu.VMEM((z.rows, z.lanes), i32),
-            pltpu.VMEM((z.rows, z.lanes), f32),
+            shape((z.nrows, z.deep), i32), shape((z.packed, z.lanes), i32),
+            shape((z.named, z.wide), bf16),
         ],
-        arrived + others + blocks, work,
-    )
-    (hot,) = call(z, hot_kernel, [shape((z.named, z.wide), bf16)], [], [pos_rows], work // 64)
-    total = sum([swap(part, "tensor", s) for s in range(1, z.tensor)], part)
+        [], [local, ids], work // 64,
+    )
+    total = sum([swap(part, "tensor", s) for s in z.tensor_order], part)
     exponent, stat = call(
         z, stat_kernel, [shape((z.packed, z.lanes), f32), shape((z.high, z.packed), f32)], [],
         [total, inside], total.size,

time: 60.6 us -> 57.6 us (0.950)
  starting transfers between devices: 22.8 us -> 20 us
    all_to_all x0 -> x1, waiting for transfers between devices: none -> 11.3 us  [body(): lax.all_to_all(pieces[0], ('tensor', 'corpus'), split_axis=0, concat_axis...]
    ppermute x19 -> x10, waiting for transfers between devices: 14.2 us -> 3 us  [swap(): return lax.ppermute(value, axis, [(i, i ^ bit) for i in range(size)])]
    ppermute x19 -> x10, starting transfers between devices: 17.4 us -> 8.02 us  [swap(): return lax.ppermute(value, axis, [(i, i ^ bit) for i in range(size)])]
    all_to_all x0 -> x1, starting transfers between devices: none -> 7.89 us  [body(): lax.all_to_all(pieces[0], ('tensor', 'corpus'), split_axis=0, concat_axis...]
    all_to_all x1, starting transfers between devices: 5.38 us -> 4.09 us  [body(): lax.all_to_all(half, ('tensor', 'corpus'), split_axis=0, concat_axis=0, t...]
    pallas_call x8 -> x9, Pallas kernels: 12.2 us -> 11.8 us  [call(): pl.pallas_call(lambda *refs: kernel(z, *refs), out_shape=outs, in_specs=[...]
    unnamed x4 -> x2, local copies, waits for them, and re-layouts: 1.23 us -> 1.22 us
  transfers between devices with their start and end apart: 20 -> 12, of which waited for: 11 -> 7; matrix products, arithmetic and copies ran while one was open for 2% -> 2% of each run, Pallas kernels for 11% -> 12%
where the time goes in v5:
time: 57.6 us; the launch traced here: 57.3 us
  waiting for transfers between devices  21.3 us (37%)
  starting transfers between devices  20 us (35%)
  Pallas kernels  11.8 us (20%)
  other arithmetic  2.15 us (4%)
  local copies, waits for them, and re-layouts  1.24 us (2%)
  between operations  0.76 us (1%)
    pallas_call x9, Pallas kernels, call(): pl.pallas_call(lambda *refs: kernel(z, *refs), out_shape=outs, in_specs=[...  11.8 us
    all_to_all x1, waiting for transfers between devices, body(): lax.all_to_all(pieces[0], ('tensor', 'corpus'), split_axis=0, concat_axis...  11.3 us
    ppermute x10, starting transfers between devices, swap(): return lax.ppermute(value, axis, [(i, i ^ bit) for i in range(size)])  8.02 us
    all_to_all x1, starting transfers between devices, body(): lax.all_to_all(pieces[0], ('tensor', 'corpus'), split_axis=0, concat_axis...  7.89 us
    all_to_all x1, waiting for transfers between devices, body(): lax.all_to_all(half, ('tensor', 'corpus'), split_axis=0, concat_axis=0, t...  6.95 us
    all_to_all x1, starting transfers between devices, body(): lax.all_to_all(half, ('tensor', 'corpus'), split_axis=0, concat_axis=0, t...  4.09 us
    ppermute x10, waiting for transfers between devices, swap(): return lax.ppermute(value, axis, [(i, i ^ bit) for i in range(size)])  3 us
    unnamed x2, local copies, waits for them, and re-layouts  1.22 us
  transfers between devices with their start and end apart: 12, of which 7 were waited for; matrix products, arithmetic and copies ran while one was open for 2% of the time, Pallas kernels for 12%

profile of v5, /device:TPU:0, one launch (start us, length us, event | category | flops | bytes accessed | tf_op | source)
XLA Modules:
  0.0 57.3 jit_solution(10033114145815574634)
XLA Ops:
  0.6 1.8 %shard_map.67 = bf16[16,16,640]{2,1,0:T(8,128)(2,1)} custom-call(s32[16]{0:T(128)} %refs_0_.1, s32[16,32]{1,0:T(8,128)} %refs_1_.1, bf16[16,2048]{1,0:T(8,128)(2,1)} %refs_2_.1), custom_call_target="tpu_custom_call" | custom-call | bytes 395328 | tf_op jit(solution)/shard_map/pallas_call | solution.py:439
  2.4 0.5 collective-permute-start
  2.9 7.9 %all-to-all-start = ((bf16[16,16,640]{2,1,0:T(8,128)(2,1)}), bf16[16,16,640]{2,1,0:T(8,128)(2,1)S(1)}, u32[]{:S(2)}, u32[]{:S(2)}) async-start(bf16[16,16,640]{2,1,0:T(8,128)(2,1)} %shard_map.67), calls=%async_computation | async-start | bytes 655360 | tf_op jit(solution)/shard_map/all_to_all | solution.py:469
  10.8 1.2 %copy-done = bf16[1024,512]{1,0:T(8,128)(2,1)S(1)} copy-done((bf16[1024,512]{1,0:T(8,128)(2,1)S(1)}, bf16[1024,512]{1,0:T(8,128)(2,1)}, u32[]{:S(2)}) %copy-start) | copy-done | bytes 1048600
  12.1 11.3 %all-to-all-done = bf16[16,16,640]{2,1,0:T(8,128)(2,1)S(1)} async-done(((bf16[16,16,640]{2,1,0:T(8,128)(2,1)}), bf16[16,16,640]{2,1,0:T(8,128)(2,1)S(1)}, u32[]{:S(2)}, u32[]{:S(2)}) %all-to-all-start) | async-done | bytes 327712 | tf_op jit(solution)/shard_map/all_to_all | solution.py:469
  23.5 0.7 %shard_map.69 = (bf16[256,512]{1,0:T(8,128)(2,1)S(1)}, f32[256,2048]{1,0:T(8,128)S(1)}) custom-call(bf16[256,640]{1,0:T(8,128)(2,1)S(1)} %bitcast.9, bf16[1024,512]{1,0:T(8,128)(2,1)S(1)} %shard_map.68.refs_1_.refs_6_, bf16[1024,512]{1,0:T(8,128)(2,1)S(1)} %collective-permute-done.refs_2_.refs_7_), custom_call_target="tpu_custom_call" | custom-call | flops 536870912 | bytes 4784128 | tf_op jit(solution)/shard_map/pallas_call | solution.py:439
  24.8 1.8 %shard_map.70 = (f32[128,128]{1,0:T(8,128)S(1)}, s32[256,128]{1,0:T(8,128)S(1)}, f32[512,128]{1,0:T(8,128)S(1)}) custom-call(bf16[256,640]{1,0:T(8,128)(2,1)S(1)} %bitcast.10, bf16[256,128]{1,0:T(8,128)(2,1)S(1)} %collective-permute-done.1.refs_1_, f32[256,2048]{1,0:T(8,128)S(1)} %get-tuple-element.30.refs_2_), custom_call_target="tpu_custom_call" | custom-call | flops 33554432 | bytes 2949120 | tf_op jit(solution)/shard_map/pallas_call | solution.py:439
  26.6 0.6 %collective-permute-start.2 = (f32[128,128]{1,0:T(8,128)S(1)}, f32[128,128]{1,0:T(8,128)S(1)}, u32[]{:S(2)}, u32[]{:S(2)}) collective-permute-start(f32[128,128]{1,0:T(8,128)S(1)} %get-tuple-element.31), channel_id=1, source_target_pairs={{0,12},{4,8},{8,4},{12,0},{1,13},{5,9},{9,5},{13,1},{2,14},{6,10},... | collective-permute-start | bytes 196616 | tf_op jit(solution)/shard_map/ppermute | solution.py:16
  27.2 0.6 collective-permute-start.3
  27.8 2.4 %collective-permute-start.4 = (f32[128,128]{1,0:T(8,128)S(1)}, f32[128,128]{1,0:T(8,128)S(1)}, u32[]{:S(2)}, u32[]{:S(2)}) collective-permute-start(f32[128,128]{1,0:T(8,128)S(1)} %get-tuple-element.31), channel_id=1, source_target_pairs={{0,4},{4,0},{8,12},{12,8},{1,5},{5,1},{9,13},{13,9},{2,6},{6,2},{1... | collective-permute-start | bytes 196616 | tf_op jit(solution)/shard_map/ppermute | solution.py:16
  30.1 0.6 %shard_map.71 = (s32[32,256]{1,0:T(8,128)S(1)}, s32[128,128]{1,0:T(8,128)S(1)}, bf16[512,2048]{1,0:T(8,128)(2,1)S(1)}) custom-call(s32[256,128]{1,0:T(8,128)S(1)} %get-tuple-element.32.refs_0_, f32[512,128]{1,0:T(8,128)S(1)} %get-tuple-element.33.refs_1_), custom_call_target="tpu_custom_call" | custom-call | flops 8388608 | bytes 2588672 | tf_op jit(solution)/shard_map/pallas_call | solution.py:439
  30.8 1.6 %collective-permute-done.2 = f32[128,128]{1,0:T(8,128)S(1)} collective-permute-done((f32[128,128]{1,0:T(8,128)S(1)}, f32[128,128]{1,0:T(8,128)S(1)}, u32[]{:S(2)}, u32[]{:S(2)}) %collective-permute-start.2) | collective-permute-done | bytes 65568 | tf_op jit(solution)/shard_map/ppermute | solution.py:16
  32.8 0.7 %collective-permute-start.5 = (f32[8,128]{1,0:T(8,128)S(1)}, f32[8,128]{1,0:T(8,128)S(1)}, u32[]{:S(2)}, u32[]{:S(2)}) collective-permute-start(f32[8,128]{1,0:T(8,128)S(1)} %get-tuple-element.35.refs_0_), channel_id=1, source_target_pairs={{0,2},{1,3},{2,0},{3,1},{4,6},{5,7},{6,4},{7,5},{8,10},{9,11},{10,... | collective-permute-start | bytes 12296 | tf_op jit(solution)/shard_map/ppermute | solution.py:16
  33.5 2.3 %collective-permute-start.6 = (f32[8,128]{1,0:T(8,128)S(1)}, f32[8,128]{1,0:T(8,128)S(1)}, u32[]{:S(2)}, u32[]{:S(2)}) collective-permute-start(f32[8,128]{1,0:T(8,128)S(1)} %get-tuple-element.35.refs_0_), channel_id=1, source_target_pairs={{0,3},{1,2},{2,1},{3,0},{4,7},{5,6},{6,5},{7,4},{8,11},{9,10},{10,... | collective-permute-start | bytes 12296 | tf_op jit(solution)/shard_map/ppermute | solution.py:16
  35.7 0.6 collective-permute-start.7
  36.3 2.9 %shard_map.73.refs_4_ = f32[256,2048]{1,0:T(8,128)S(1)} custom-call(f32[128,128]{1,0:T(8,128)S(1)} %get-tuple-element.36.refs_0_, s32[32,256]{1,0:T(8,128)S(1)} %get-tuple-element.37.refs_1_, bf16[512,2048]{1,0:T(8,128)(2,1)S(1)} %get-tuple-element.38.refs_2_.refs_5_), custom_call_target="tpu_custom_call" | custom-call | flops 1610612736 | bytes 4292608 | tf_op jit(solution)/shard_map/pallas_call | solution.py:439
  39.4 1.0 %shard_map.74 = (bf16[256,1024]{1,0:T(8,128)(2,1)S(1)}, bf16[256,1024]{1,0:T(8,128)(2,1)S(1)}, f32[16,128]{1,0:T(8,128)S(1)}, f32[16,128]{1,0:T(8,128)S(1)}, f32[256,512]{1,0:T(8,128)S(1)}) custom-call(f32[8,128]{1,0:T(8,128)S(1)} %get-tuple-element.35.refs_0_, f32[8,128]{1,0:T(8,128)S(1)} %collective-permute-done.5.refs_1_, ...), custom_call_target="tpu_custom_call" | custom-call | flops 536870912 | bytes 7897088 | tf_op jit(solution)/shard_map/pallas_call | solution.py:439
  40.4 0.7 %convert_element_type.4 = f16[256,512]{1,0:T(8,128)(2,1)} convert(f32[256,512]{1,0:T(8,128)S(1)} %get-tuple-element.39) | non-fusion elementwise | flops 131072 | bytes 786432 | tf_op jit(solution)/shard_map/convert_element_type | solution.py:524
  41.1 4.1 %all-to-all-start.1 = ((f16[16,16,512]{2,1,0:T(8,128)(2,1)}), f16[16,16,512]{2,1,0:T(8,128)(2,1)S(1)}, u32[]{:S(2)}, u32[]{:S(2)}) async-start(f16[16,16,512]{2,1,0:T(8,128)(2,1)} %bitcast.1), calls=%async_computation.1 | async-start | bytes 524288 | tf_op jit(solution)/shard_map/all_to_all | solution.py:525
  45.5 0.6 %slice_reduce_fusion = (f32[16]{0:T(128)}, f32[16]{0:T(128)S(1)}) fusion(f32[16,128]{1,0:T(8,128)S(1)} %get-tuple-element.45, f32[16,128]{1,0:T(8,128)S(1)} %get-tuple-element.44), kind=kLoop, calls=%fused_computation.3 | loop fusion | flops 16 | bytes 256 | tf_op jit(solution)/shard_map/slice | solution.py:533
  46.1 0.7 %collective-permute-done.9.refs_3_ = bf16[256,512]{1,0:T(8,128)(2,1)S(1)} collective-permute-done((bf16[256,512]{1,0:T(8,128)(2,1)S(1)}, bf16[256,512]{1,0:T(8,128)(2,1)S(1)}, u32[]{:S(2)}, u32[]{:S(2)}) %collective-permute-start.9) | collective-permute-done | bytes 262176 | tf_op jit(solution)/shard_map/ppermute | solution.py:16
  46.8 2.7 %shard_map.75 = f32[1024,512]{1,0:T(8,128)} custom-call(bf16[256,1024]{1,0:T(8,128)(2,1)S(1)} %get-tuple-element.40.refs_0_, bf16[256,512]{1,0:T(8,128)(2,1)S(1)} %get-tuple-element.41.refs_1_, bf16[256,1024]{1,0:T(8,128)(2,1)S(1)} %collective-permute-done.8.refs_2_, bf16[256,512]{1,0:T(8,128)(2,1)S(1)} %collective-permute-done.9.refs_3_), custom_call_target="tpu_custom_call" | custom-call | flops 536870912 | bytes 3670016 | tf_op jit(solution)/shard_map/pallas_call | solution.py:439
  49.5 7.0 %all-to-all-done.1 = f16[16,16,512]{2,1,0:T(8,128)(2,1)S(1)} async-done(((f16[16,16,512]{2,1,0:T(8,128)(2,1)}), f16[16,16,512]{2,1,0:T(8,128)(2,1)S(1)}, u32[]{:S(2)}, u32[]{:S(2)}) %all-to-all-start.1) | async-done | bytes 262176 | tf_op jit(solution)/shard_map/all_to_all | solution.py:525
  56.5 0.7 %broadcast_multiply_fusion = f32[16,2048]{1,0:T(8,128)} fusion(f32[16,2048]{1,0:T(8,128)S(1)} %bitcast.12, f32[16]{0:T(128)S(1)} %get-tuple-element.48), kind=kLoop, calls=%fused_computation.1 | loop fusion | flops 32768 | bytes 262208 | tf_op jit(solution)/shard_map/mul | solution.py:532
  (18 shorter events, 1.5 us)
Async XLA Ops:
  2.4 21.0 %collective-permute-start = (bf16[1024,512]{1,0:T(8,128)(2,1)}, bf16[1024,512]{1,0:T(8,128)(2,1)S(1)}, u32[]{:S(2)}, u32[]{:S(2)}) collective-permute-start(bf16[1024,512]{1,0:T(8,128)(2,1)} %refs_0_.2), channel_id=1, source_target_pairs={{0,16},{16,0},{1,17},{17,1},{2,18},{18,2},{3,19},{19,3},{4,20},{20... | collective-permute-start | bytes 3145736 | tf_op jit(solution)/shard_map/ppermute | solution.py:16
  2.9 20.5 %all-to-all-start = ((bf16[16,16,640]{2,1,0:T(8,128)(2,1)}), bf16[16,16,640]{2,1,0:T(8,128)(2,1)S(1)}, u32[]{:S(2)}, u32[]{:S(2)}) async-start(bf16[16,16,640]{2,1,0:T(8,128)(2,1)} %shard_map.67), calls=%async_computation | async-start | bytes 655360 | tf_op jit(solution)/shard_map/all_to_all | solution.py:469
  10.8 1.2 %copy-start = (bf16[1024,512]{1,0:T(8,128)(2,1)S(1)}, bf16[1024,512]{1,0:T(8,128)(2,1)}, u32[]{:S(2)}) copy-start(bf16[1024,512]{1,0:T(8,128)(2,1)} %refs_0_.2) | copy-start | bytes 3145732
  23.4 1.3 %collective-permute-start.1 = (bf16[256,128]{1,0:T(8,128)(2,1)S(1)}, bf16[256,128]{1,0:T(8,128)(2,1)S(1)}, u32[]{:S(2)}, u32[]{:S(2)}) collective-permute-start(bf16[256,128]{1,0:T(8,128)(2,1)S(1)} %slice.12), channel_id=1, source_target_pairs={{0,16},{16,0},{1,17},{17,1},{2,18},{18,2},{3,19},{19,3},{4,20},{20... | collective-permute-start | bytes 196616 | tf_op jit(solution)/shard_map/ppermute | solution.py:16
  26.6 5.8 %collective-permute-start.2 = (f32[128,128]{1,0:T(8,128)S(1)}, f32[128,128]{1,0:T(8,128)S(1)}, u32[]{:S(2)}, u32[]{:S(2)}) collective-permute-start(f32[128,128]{1,0:T(8,128)S(1)} %get-tuple-element.31), channel_id=1, source_target_pairs={{0,12},{4,8},{8,4},{12,0},{1,13},{5,9},{9,5},{13,1},{2,14},{6,10},... | collective-permute-start | bytes 196616 | tf_op jit(solution)/shard_map/ppermute | solution.py:16
  27.2 5.3 %collective-permute-start.3 = (f32[128,128]{1,0:T(8,128)S(1)}, f32[128,128]{1,0:T(8,128)S(1)}, u32[]{:S(2)}, u32[]{:S(2)}) collective-permute-start(f32[128,128]{1,0:T(8,128)S(1)} %get-tuple-element.31), channel_id=1, source_target_pairs={{0,8},{4,12},{8,0},{12,4},{1,9},{5,13},{9,1},{13,5},{2,10},{6,14},... | collective-permute-start | bytes 196616 | tf_op jit(solution)/shard_map/ppermute | solution.py:16
  27.8 4.7 %collective-permute-start.4 = (f32[128,128]{1,0:T(8,128)S(1)}, f32[128,128]{1,0:T(8,128)S(1)}, u32[]{:S(2)}, u32[]{:S(2)}) collective-permute-start(f32[128,128]{1,0:T(8,128)S(1)} %get-tuple-element.31), channel_id=1, source_target_pairs={{0,4},{4,0},{8,12},{12,8},{1,5},{5,1},{9,13},{13,9},{2,6},{6,2},{1... | collective-permute-start | bytes 196616 | tf_op jit(solution)/shard_map/ppermute | solution.py:16
  32.8 6.5 %collective-permute-start.5 = (f32[8,128]{1,0:T(8,128)S(1)}, f32[8,128]{1,0:T(8,128)S(1)}, u32[]{:S(2)}, u32[]{:S(2)}) collective-permute-start(f32[8,128]{1,0:T(8,128)S(1)} %get-tuple-element.35.refs_0_), channel_id=1, source_target_pairs={{0,2},{1,3},{2,0},{3,1},{4,6},{5,7},{6,4},{7,5},{8,10},{9,11},{10,... | collective-permute-start | bytes 12296 | tf_op jit(solution)/shard_map/ppermute | solution.py:16
  33.5 5.8 %collective-permute-start.6 = (f32[8,128]{1,0:T(8,128)S(1)}, f32[8,128]{1,0:T(8,128)S(1)}, u32[]{:S(2)}, u32[]{:S(2)}) collective-permute-start(f32[8,128]{1,0:T(8,128)S(1)} %get-tuple-element.35.refs_0_), channel_id=1, source_target_pairs={{0,3},{1,2},{2,1},{3,0},{4,7},{5,6},{6,5},{7,4},{8,11},{9,10},{10,... | collective-permute-start | bytes 12296 | tf_op jit(solution)/shard_map/ppermute | solution.py:16
  35.7 3.6 %collective-permute-start.7 = (f32[8,128]{1,0:T(8,128)S(1)}, f32[8,128]{1,0:T(8,128)S(1)}, u32[]{:S(2)}, u32[]{:S(2)}) collective-permute-start(f32[8,128]{1,0:T(8,128)S(1)} %get-tuple-element.35.refs_0_), channel_id=1, source_target_pairs={{0,1},{1,0},{2,3},{3,2},{4,5},{5,4},{6,7},{7,6},{8,9},{9,8},{10,11... | collective-permute-start | bytes 12296 | tf_op jit(solution)/shard_map/ppermute | solution.py:16
  40.3 6.5 %collective-permute-start.8 = (bf16[256,1024]{1,0:T(8,128)(2,1)S(1)}, bf16[256,1024]{1,0:T(8,128)(2,1)S(1)}, u32[]{:S(2)}, u32[]{:S(2)}) collective-permute-start(bf16[256,1024]{1,0:T(8,128)(2,1)S(1)} %get-tuple-element.42), channel_id=1, source_target_pairs={{0,16},{16,0},{1,17},{17,1},{2,18},{18,2},{3,19},{19,3},{4,20},{20... | collective-permute-start | bytes 1572872 | tf_op jit(solution)/shard_map/ppermute | solution.py:16
  41.1 15.3 %all-to-all-start.1 = ((f16[16,16,512]{2,1,0:T(8,128)(2,1)}), f16[16,16,512]{2,1,0:T(8,128)(2,1)S(1)}, u32[]{:S(2)}, u32[]{:S(2)}) async-start(f16[16,16,512]{2,1,0:T(8,128)(2,1)} %bitcast.1), calls=%async_computation.1 | async-start | bytes 524288 | tf_op jit(solution)/shard_map/all_to_all | solution.py:525
  45.2 1.6 %collective-permute-start.9 = (bf16[256,512]{1,0:T(8,128)(2,1)S(1)}, bf16[256,512]{1,0:T(8,128)(2,1)S(1)}, u32[]{:S(2)}, u32[]{:S(2)}) collective-permute-start(bf16[256,512]{1,0:T(8,128)(2,1)S(1)} %get-tuple-element.41.refs_1_), channel_id=1, source_target_pairs={{0,16},{16,0},{1,17},{17,1},{2,18},{18,2},{3,19},{19,3},{4,20},{20... | collective-permute-start | bytes 786440 | tf_op jit(solution)/shard_map/ppermute | solution.py:16

commit v6 on v5

--- a/solution.py
+++ b/solution.py
@@ -66,6 +66,9 @@
         self.run = self.joint * self.own
         self.sets = self.groups // self.joint
         self.high = -(-3 * self.pack // 8) * 8
+        self.dense_ids = self.block * self.dp * self.corpus <= 2**13 and self.own == 16
+        self.fold = self.own // 2 if self.dense_ids else self.own
+        self.message = 2 * self.width + LANES if self.dense_ids else self.width + LANES
         self.vmem = min(61, 20 + 20 * self.rows // 1024) * 2**20
 
 
@@ -95,12 +98,46 @@
         pos = jnp.where(row == i, pos_ref[i], pos)
     ids = [neg_ref[...], pos[:, : half - z.neg_at - z.negs]]
     ids = jnp.concatenate([part for part in [pos[:, : z.neg_at]] + ids if part.shape[1]], axis=1)
+    if z.dense_ids:
+        code = 1.0 + (ids & 127).astype(jnp.float32) / 128.0
+        for bit in range(6):
+            code = jnp.where((ids >> (7 + bit)) & 1 == 1, code * 2.0 ** (1 << bit), code)
+        code = code * 2.0**-32
+        code = jnp.concatenate([code[: z.fold], code[z.fold :]], axis=1)
+        for t in range(z.tensor):
+            rows = query_ref[:, t * z.width : (t + 1) * z.width].astype(jnp.float32)
+            rows = jnp.concatenate([rows[: z.fold], rows[z.fold :], code], axis=1)
+            rows = jnp.concatenate([rows, rows], axis=0).astype(jnp.bfloat16)
+            for c in range(0, z.corpus, 2):
+                out_ref[pl.ds((t * z.corpus + c) * z.fold, z.own), :] = rows
+        return
     ids = jnp.concatenate([ids >> 8, ids & 255], axis=1)
     code = ids.astype(jnp.float32).astype(jnp.bfloat16)
     for k in range(z.groups):
         t = k // z.corpus
-        out_ref[k, :, : z.width] = query_ref[:, t * z.width : (t + 1) * z.width]
-        out_ref[k, :, z.width :] = code
+        at = pl.ds(k * z.own, z.own)
+        out_ref[at, : z.width] = query_ref[:, t * z.width : (t + 1) * z.width]
+        out_ref[at, z.width :] = code
+
+
+def unfold(z, first, second):
+    width = first.shape[-1]
+    pair = [part.reshape(z.groups, z.fold, width) for part in (first, second)]
+    return jnp.concatenate(pair, axis=1).reshape(z.half, width)
+
+
+def decode(z, code):
+    code = code.astype(jnp.float32)
+    if not z.dense_ids:
+        return code * 256.0 + pltpu.roll(code, LANES // 2, 1)
+    code = code * 2.0**32
+    high = jnp.zeros_like(code)
+    for bit in range(5, -1, -1):
+        big = code >= 2.0 ** (1 << bit)
+        high = jnp.where(big, high + float(128 << bit), high)
+        code = jnp.where(big, code * 2.0 ** -(1 << bit), code)
+    ids = high + (code - 1.0) * 128.0
+    return unfold(z, ids, pltpu.roll(ids, LANES // 2, 1))
 
 
 def fetch_kernel(z, block_ref, passage_ref, sem):
@@ -126,11 +163,19 @@
 
 def score_kernel(z, *refs):
     arrived, block_refs = refs[: z.side], refs[z.side : z.side + 2]
-    query_ref, score_ref = refs[z.side + 2 :]
+    query_ref, score_ref, own_ref, near_ref = refs[z.side + 2 :]
     d = lax.axis_index("dp")
+    localize = localizer(z)
     for su in range(z.side):
         at = rows_at(((d ^ (2 * su)) >> 1) * z.half, z.half)
-        query_ref[at, :] = arrived[su][:, : z.width]
+        rows = arrived[su][:, : z.message - LANES]
+        if z.dense_ids:
+            rows = rows.astype(jnp.float32)
+            rows = unfold(z, rows[:, : z.width], rows[:, z.width :]).astype(jnp.bfloat16)
+        query_ref[at, :] = rows
+        ids = decode(z, arrived[su][:, z.message - LANES :])
+        own_ref[at, :] = ids
+        near_ref[at, :] = localize(ids)
     step = min(z.rows, 256)
 
     def score(i, carry):
@@ -160,16 +205,14 @@
 
 
 def pick_kernel(z, *refs):
-    arrived, others, score_ref = refs[: z.side], refs[z.side : 2 * z.side], refs[2 * z.side]
-    part_ref, local_ref, id_ref, logit_ref = refs[2 * z.side + 1 :]
+    others, (score_ref, own_ref, near_ref) = refs[: z.side], refs[z.side : z.side + 3]
+    part_ref, local_ref, id_ref, logit_ref = refs[z.side + 3 :]
     d = lax.axis_index("dp")
-    localize = localizer(z)
     for su in range(z.side):
         from_d = d ^ (2 * su)
-        for side, code in enumerate([arrived[su][:, z.width :], others[su][...]]):
-            code = code.astype(jnp.float32)
-            at = rows_at((from_d ^ side) * z.half, z.half)
-            id_ref[at, :] = code * 256.0 + pltpu.roll(code, LANES // 2, 1)
+        own = own_ref[rows_at((from_d >> 1) * z.half, z.half), :]
+        id_ref[rows_at(from_d * z.half, z.half), :] = own
+        id_ref[rows_at((from_d ^ 1) * z.half, z.half), :] = decode(z, others[su][...])
     wide = -(-z.columns // LANES) * LANES
     row = lax.broadcasted_iota(jnp.int32, (z.half, wide), 0) & (z.own - 1)
     col = lax.broadcasted_iota(jnp.int32, (z.half, wide), 1)
@@ -179,16 +222,16 @@
         pos = jnp.broadcast_to(id_ref[at, z.pos_at : z.pos_at + 1], (z.half, wide))
         kept = jnp.where(col == row + h * z.own, pos, 0.0)
         group_ids += jnp.sum(kept.reshape(z.groups, z.own, wide), axis=1)
-    batch_ids = jnp.broadcast_to(group_ids[:, None, :], (z.groups, z.own, wide))
-    batch_ids = batch_ids.reshape(z.half, wide)
+    batch = jnp.broadcast_to(localizer(z)(group_ids)[:, None, :], (z.groups, z.own, wide))
+    batch = batch.reshape(z.half, wide)
     lane = lax.broadcasted_iota(jnp.int32, (z.half, LANES), 1)
     for u in range(z.side):
-        ids = id_ref[rows_at((2 * u + (d & 1)) * z.half, z.half), :]
+        near = near_ref[pl.ds(u * z.half, z.half), :]
         for base in range(0, z.lanes, LANES):
-            named = ids
+            local = near
             if base < z.columns:
-                named = jnp.where(lane + base < z.columns, batch_ids[:, base : base + LANES], ids)
-            local = jnp.where(lane + base < z.items, localize(named), float(FAR))
+                local = jnp.where(lane + base < z.columns, batch[:, base : base + LANES], near)
+            local = jnp.where(lane + base < z.items, local, float(FAR))
             local_ref[pl.ds(u * z.half, z.half), base : base + LANES] = local.astype(jnp.int32)
     step = min(z.rows, 256)
 
@@ -453,7 +496,7 @@
     shape = jax.ShapeDtypeStruct
 
     pieces = call(
-        z, message_kernel, [shape((z.groups, z.own, z.width + LANES), bf16)],
+        z, message_kernel, [shape((z.groups * z.fold, z.message), bf16)],
         [
             pltpu.SMEM(pos_ids.shape, i32), pltpu.VMEM(neg_ids.shape, i32),
             pltpu.VMEM(queries.shape, bf16), pltpu.SemaphoreType.DMA((3,)),
@@ -468,13 +511,15 @@
     other_block = swap(passages, "dp", 1)
     chip = lax.all_to_all(pieces[0], ("tensor", "corpus"), split_axis=0, concat_axis=0, tiled=True)
     chip, own_block, other_block = lax.optimization_barrier((chip, own_block, other_block))
-    arrived = gather_pairs([chip.reshape(z.half, z.width + LANES)])
-    others = [swap(piece[:, z.width :], "dp", 1) for piece in arrived]
+    arrived = gather_pairs([chip])
+    others = [swap(piece[:, z.message - LANES :], "dp", 1) for piece in arrived]
     blocks = [own_block, other_block]
 
     work = 2 * z.rows * z.wide * z.width
-    query_rows, scores = call(
-        z, score_kernel, [shape((z.rows, z.width), bf16), shape((z.rows, z.wide), f32)], [],
+    query_rows, scores, own_ids, near = call(
+        z, score_kernel,
+        [shape((z.rows, z.width), bf16), shape((z.rows, z.wide), f32)]
+        + [shape((z.rows, LANES), f32)] * 2, [],
         arrived + blocks, work,
     )
     part, local, ids = call(
@@ -483,7 +528,7 @@
             shape((z.packed, z.lanes), f32), shape((z.rows, z.lanes), i32),
             shape((z.named, LANES), f32),
         ],
-        [pltpu.VMEM((z.rows, z.lanes), f32)], arrived + others + [scores], work // 16,
+        [pltpu.VMEM((z.rows, z.lanes), f32)], others + [scores, own_ids, near], work // 16,
     )
     index, inside, hot = call(
         z, index_kernel,
@@ -521,14 +566,16 @@
         ],
         stats + [raw, hot] + blocks, work,
     )
-    half = scatter_pairs(grads).astype(jnp.float16).reshape(z.groups, z.own, z.width)
-    half = lax.all_to_all(half, ("tensor", "corpus"), split_axis=0, concat_axis=0, tiled=True)
+    half = scatter_pairs(grads).astype(jnp.float16)
+    half = half.reshape(z.tensor, z.corpus, z.own, z.width).swapaxes(0, 1)
+    half = half.reshape(z.groups, z.own, z.width)
+    half = lax.all_to_all(half, ("corpus", "tensor"), split_axis=0, concat_axis=0, tiled=True)
     (grad_pass,) = call(
         z, passage_kernel, [shape((z.block, z.width), f32)], [],
         [dense, query_rows, swap(other_dense, "dp", 1), swap(query_rows, "dp", 1)], work,
     )
     half, grad_pass = lax.optimization_barrier((half, grad_pass))
-    half = half.astype(f32).reshape(z.tensor, z.corpus, z.own, z.width).sum(axis=1)
+    half = half.astype(f32).reshape(z.corpus, z.tensor, z.own, z.width).sum(axis=0)
     grad_query = half.swapaxes(0, 1).reshape(z.own, z.feat) * (size[:, :1] * z.scale)
     return (grad_query, loss[:, 0], grad_pass)
 

time: 57.6 us -> 56.2 us (0.976)
  waiting for transfers between devices: 21.3 us -> 19.9 us
  local copies, waits for them, and re-layouts: 1.24 us -> 1.99 us
  other arithmetic: 2.15 us -> 1.45 us
    reshape x0 -> x1, local copies, waits for them, and re-layouts: none -> 0.75 us  [body(): half = half.reshape(z.tensor, z.corpus, z.own, z.width).swapaxes(0, 1)]
    all_to_all x1, waiting for transfers between devices: 6.95 us -> 6.24 us  [body(): lax.all_to_all(half, ('corpus', 'tensor'), split_axis=0, concat_axis=0, t...]
    convert_element_type x1, other arithmetic: 0.74 us -> 0.04 us  [body(): half = scatter_pairs(grads).astype(jnp.float16)]
    all_to_all x1, waiting for transfers between devices: 11.3 us -> 10.6 us  [body(): lax.all_to_all(pieces[0], ('tensor', 'corpus'), split_axis=0, concat_axis...]
  transfers between devices with their start and end apart: 12 -> 12, of which waited for: 7 -> 7; matrix products, arithmetic and copies ran while one was open for 2% -> 3% of each run, Pallas kernels for 12% -> 13%
where the time goes in v6:
time: 56.2 us; the launch traced here: 55.8 us
  starting transfers between devices  19.9 us (35%)
  waiting for transfers between devices  19.9 us (35%)
  Pallas kernels  11.9 us (21%)
  local copies, waits for them, and re-layouts  1.99 us (4%)
  other arithmetic  1.45 us (3%)
  between operations  0.77 us (1%)
    pallas_call x9, Pallas kernels, call(): pl.pallas_call(lambda *refs: kernel(z, *refs), out_shape=outs, in_specs=[...  11.9 us
    all_to_all x1, waiting for transfers between devices, body(): lax.all_to_all(pieces[0], ('tensor', 'corpus'), split_axis=0, concat_axis...  10.6 us
    ppermute x10, starting transfers between devices, swap(): return lax.ppermute(value, axis, [(i, i ^ bit) for i in range(size)])  7.95 us
    all_to_all x1, starting transfers between devices, body(): lax.all_to_all(pieces[0], ('tensor', 'corpus'), split_axis=0, concat_axis...  7.89 us
    all_to_all x1, waiting for transfers between devices, body(): lax.all_to_all(half, ('corpus', 'tensor'), split_axis=0, concat_axis=0, t...  6.24 us
    all_to_all x1, starting transfers between devices, body(): lax.all_to_all(half, ('corpus', 'tensor'), split_axis=0, concat_axis=0, t...  4.09 us
    ppermute x10, waiting for transfers between devices, swap(): return lax.ppermute(value, axis, [(i, i ^ bit) for i in range(size)])  3.02 us
    unnamed x2, local copies, waits for them, and re-layouts  1.22 us
  transfers between devices with their start and end apart: 12, of which 7 were waited for; matrix products, arithmetic and copies ran while one was open for 3% of the time, Pallas kernels for 13%

profile of v6, /device:TPU:0, one launch (start us, length us, event | category | flops | bytes accessed | tf_op | source)
XLA Modules:
  0.0 55.8 jit_solution(1038699818015328915)
XLA Ops:
  0.6 1.8 %shard_map.67 = bf16[128,1152]{1,0:T(8,128)(2,1)} custom-call(s32[16]{0:T(128)} %refs_0_.1, s32[16,32]{1,0:T(8,128)} %refs_1_.1, bf16[16,2048]{1,0:T(8,128)(2,1)} %refs_2_.1), custom_call_target="tpu_custom_call" | custom-call | bytes 362560 | tf_op jit(solution)/shard_map/pallas_call | solution.py:482
  2.4 0.5 collective-permute-start
  2.9 7.9 %all-to-all-start = ((bf16[16,8,1152]{2,1,0:T(8,128)(2,1)}), bf16[16,8,1152]{2,1,0:T(8,128)(2,1)S(1)}, u32[]{:S(2)}, u32[]{:S(2)}) async-start(bf16[16,8,1152]{2,1,0:T(8,128)(2,1)} %bitcast.13), calls=%async_computation | async-start | bytes 589824 | tf_op jit(solution)/shard_map/all_to_all | solution.py:512
  10.8 1.2 %copy-done = bf16[1024,512]{1,0:T(8,128)(2,1)S(1)} copy-done((bf16[1024,512]{1,0:T(8,128)(2,1)S(1)}, bf16[1024,512]{1,0:T(8,128)(2,1)}, u32[]{:S(2)}) %copy-start) | copy-done | bytes 1048600
  12.1 10.6 %all-to-all-done = bf16[16,8,1152]{2,1,0:T(8,128)(2,1)S(1)} async-done(((bf16[16,8,1152]{2,1,0:T(8,128)(2,1)}), bf16[16,8,1152]{2,1,0:T(8,128)(2,1)S(1)}, u32[]{:S(2)}, u32[]{:S(2)}) %all-to-all-start) | async-done | bytes 294944 | tf_op jit(solution)/shard_map/all_to_all | solution.py:512
  22.7 0.7 %shard_map.69 = (bf16[256,512]{1,0:T(8,128)(2,1)S(1)}, f32[256,2048]{1,0:T(8,128)S(1)}, f32[256,128]{1,0:T(8,128)S(1)}, f32[256,128]{1,0:T(8,128)S(1)}) custom-call(bf16[128,1152]{1,0:T(8,128)(2,1)S(1)} %bitcast.12, bf16[1024,512]{1,0:T(8,128)(2,1)S(1)} %shard_map.68.refs_1_.refs_6_, bf16[1024,512]{1,0:T(8,128)(2,1)S(1)} %collective-permute-done.refs_2_.refs_7_), custom_call_target="tpu_custom_call" | custom-call | flops 536870912 | bytes 5013504 | tf_op jit(solution)/shard_map/pallas_call | solution.py:482
  23.9 1.8 %shard_map.70 = (f32[128,128]{1,0:T(8,128)S(1)}, s32[256,128]{1,0:T(8,128)S(1)}, f32[512,128]{1,0:T(8,128)S(1)}) custom-call(bf16[128,128]{1,0:T(8,128)(2,1)S(1)} %collective-permute-done.1.refs_0_, f32[256,2048]{1,0:T(8,128)S(1)} %get-tuple-element.32.refs_1_, f32[256,128]{1,0:T(8,128)S(1)} %get-tuple-element.33.refs_2_, ...), custom_call_target="tpu_custom_call" | custom-call | flops 33554432 | bytes 2850816 | tf_op jit(solution)/shard_map/pallas_call | solution.py:482
  25.8 0.6 %collective-permute-start.2 = (f32[128,128]{1,0:T(8,128)S(1)}, f32[128,128]{1,0:T(8,128)S(1)}, u32[]{:S(2)}, u32[]{:S(2)}) collective-permute-start(f32[128,128]{1,0:T(8,128)S(1)} %get-tuple-element.35), channel_id=1, source_target_pairs={{0,12},{4,8},{8,4},{12,0},{1,13},{5,9},{9,5},{13,1},{2,14},{6,10},... | collective-permute-start | bytes 196616 | tf_op jit(solution)/shard_map/ppermute | solution.py:16
  26.4 0.6 %collective-permute-start.3 = (f32[128,128]{1,0:T(8,128)S(1)}, f32[128,128]{1,0:T(8,128)S(1)}, u32[]{:S(2)}, u32[]{:S(2)}) collective-permute-start(f32[128,128]{1,0:T(8,128)S(1)} %get-tuple-element.35), channel_id=1, source_target_pairs={{0,8},{4,12},{8,0},{12,4},{1,9},{5,13},{9,1},{13,5},{2,10},{6,14},... | collective-permute-start | bytes 196616 | tf_op jit(solution)/shard_map/ppermute | solution.py:16
  27.0 2.4 %collective-permute-start.4 = (f32[128,128]{1,0:T(8,128)S(1)}, f32[128,128]{1,0:T(8,128)S(1)}, u32[]{:S(2)}, u32[]{:S(2)}) collective-permute-start(f32[128,128]{1,0:T(8,128)S(1)} %get-tuple-element.35), channel_id=1, source_target_pairs={{0,4},{4,0},{8,12},{12,8},{1,5},{5,1},{9,13},{13,9},{2,6},{6,2},{1... | collective-permute-start | bytes 196616 | tf_op jit(solution)/shard_map/ppermute | solution.py:16
  29.3 0.6 %shard_map.71 = (s32[32,256]{1,0:T(8,128)S(1)}, s32[128,128]{1,0:T(8,128)S(1)}, bf16[512,2048]{1,0:T(8,128)(2,1)S(1)}) custom-call(s32[256,128]{1,0:T(8,128)S(1)} %get-tuple-element.36.refs_0_, f32[512,128]{1,0:T(8,128)S(1)} %get-tuple-element.37.refs_1_), custom_call_target="tpu_custom_call" | custom-call | flops 8388608 | bytes 2588672 | tf_op jit(solution)/shard_map/pallas_call | solution.py:482
  30.0 1.6 %collective-permute-done.2 = f32[128,128]{1,0:T(8,128)S(1)} collective-permute-done((f32[128,128]{1,0:T(8,128)S(1)}, f32[128,128]{1,0:T(8,128)S(1)}, u32[]{:S(2)}, u32[]{:S(2)}) %collective-permute-start.2) | collective-permute-done | bytes 65568 | tf_op jit(solution)/shard_map/ppermute | solution.py:16
  32.0 0.8 %collective-permute-start.5 = (f32[8,128]{1,0:T(8,128)S(1)}, f32[8,128]{1,0:T(8,128)S(1)}, u32[]{:S(2)}, u32[]{:S(2)}) collective-permute-start(f32[8,128]{1,0:T(8,128)S(1)} %get-tuple-element.39.refs_0_), channel_id=1, source_target_pairs={{0,2},{1,3},{2,0},{3,1},{4,6},{5,7},{6,4},{7,5},{8,10},{9,11},{10,... | collective-permute-start | bytes 12296 | tf_op jit(solution)/shard_map/ppermute | solution.py:16
  32.8 2.2 %collective-permute-start.6 = (f32[8,128]{1,0:T(8,128)S(1)}, f32[8,128]{1,0:T(8,128)S(1)}, u32[]{:S(2)}, u32[]{:S(2)}) collective-permute-start(f32[8,128]{1,0:T(8,128)S(1)} %get-tuple-element.39.refs_0_), channel_id=1, source_target_pairs={{0,3},{1,2},{2,1},{3,0},{4,7},{5,6},{6,5},{7,4},{8,11},{9,10},{10,... | collective-permute-start | bytes 12296 | tf_op jit(solution)/shard_map/ppermute | solution.py:16
  35.0 0.5 collective-permute-start.7
  35.5 2.9 %shard_map.73.refs_4_ = f32[256,2048]{1,0:T(8,128)S(1)} custom-call(f32[128,128]{1,0:T(8,128)S(1)} %get-tuple-element.40.refs_0_, s32[32,256]{1,0:T(8,128)S(1)} %get-tuple-element.41.refs_1_, bf16[512,2048]{1,0:T(8,128)(2,1)S(1)} %get-tuple-element.42.refs_2_.refs_5_), custom_call_target="tpu_custom_call" | custom-call | flops 1610612736 | bytes 4292608 | tf_op jit(solution)/shard_map/pallas_call | solution.py:482
  38.6 0.9 %shard_map.74 = (bf16[256,1024]{1,0:T(8,128)(2,1)S(1)}, bf16[256,1024]{1,0:T(8,128)(2,1)S(1)}, f32[16,128]{1,0:T(8,128)S(1)}, f32[16,128]{1,0:T(8,128)S(1)}, f32[256,512]{1,0:T(8,128)S(1)}) custom-call(f32[8,128]{1,0:T(8,128)S(1)} %get-tuple-element.39.refs_0_, f32[8,128]{1,0:T(8,128)S(1)} %collective-permute-done.5.refs_1_, ...), custom_call_target="tpu_custom_call" | custom-call | flops 536870912 | bytes 7897088 | tf_op jit(solution)/shard_map/pallas_call | solution.py:482
  39.7 0.8 %copy.9 = f16[4,4,16,512]{3,2,0,1:T(8,128)(2,1)} copy(f16[4,4,16,512]{3,2,1,0:T(8,128)(2,1)S(1)} %bitcast.14) | data formatting | bytes 524288 | tf_op jit(solution)/shard_map/reshape | solution.py:570
  40.4 4.1 %all-to-all-start.1 = ((f16[16,16,512]{2,1,0:T(8,128)(2,1)}), f16[16,16,512]{2,1,0:T(8,128)(2,1)S(1)}, u32[]{:S(2)}, u32[]{:S(2)}) async-start(f16[16,16,512]{2,1,0:T(8,128)(2,1)} %bitcast.4), calls=%async_computation.1 | async-start | bytes 524288 | tf_op jit(solution)/shard_map/all_to_all | solution.py:572
  44.8 0.6 %slice_reduce_fusion = (f32[16]{0:T(128)}, f32[16]{0:T(128)S(1)}) fusion(f32[16,128]{1,0:T(8,128)S(1)} %get-tuple-element.49, f32[16,128]{1,0:T(8,128)S(1)} %get-tuple-element.48), kind=kLoop, calls=%fused_computation.3 | loop fusion | flops 16 | bytes 256 | tf_op jit(solution)/shard_map/slice | solution.py:580
  45.4 0.7 %collective-permute-done.9.refs_3_ = bf16[256,512]{1,0:T(8,128)(2,1)S(1)} collective-permute-done((bf16[256,512]{1,0:T(8,128)(2,1)S(1)}, bf16[256,512]{1,0:T(8,128)(2,1)S(1)}, u32[]{:S(2)}, u32[]{:S(2)}) %collective-permute-start.9) | collective-permute-done | bytes 262176 | tf_op jit(solution)/shard_map/ppermute | solution.py:16
  46.1 2.7 %shard_map.75 = f32[1024,512]{1,0:T(8,128)} custom-call(bf16[256,1024]{1,0:T(8,128)(2,1)S(1)} %get-tuple-element.44.refs_0_, bf16[256,512]{1,0:T(8,128)(2,1)S(1)} %get-tuple-element.45.refs_1_, bf16[256,1024]{1,0:T(8,128)(2,1)S(1)} %collective-permute-done.8.refs_2_, bf16[256,512]{1,0:T(8,128)(2,1)S(1)} %collective-permute-done.9.refs_3_), custom_call_target="tpu_custom_call" | custom-call | flops 536870912 | bytes 3670016 | tf_op jit(solution)/shard_map/pallas_call | solution.py:482
  48.8 6.2 %all-to-all-done.1 = f16[16,16,512]{2,1,0:T(8,128)(2,1)S(1)} async-done(((f16[16,16,512]{2,1,0:T(8,128)(2,1)}), f16[16,16,512]{2,1,0:T(8,128)(2,1)S(1)}, u32[]{:S(2)}, u32[]{:S(2)}) %all-to-all-start.1) | async-done | bytes 262176 | tf_op jit(solution)/shard_map/all_to_all | solution.py:572
  55.1 0.7 %broadcast_multiply_fusion = f32[16,2048]{1,0:T(8,128)} fusion(f32[16,2048]{1,0:T(8,128)S(1)} %bitcast.17, f32[16]{0:T(128)S(1)} %get-tuple-element.52), kind=kLoop, calls=%fused_computation.1 | loop fusion | flops 32768 | bytes 262208 | tf_op jit(solution)/shard_map/mul | solution.py:579
  (19 shorter events, 1.5 us)
Async XLA Ops:
  2.4 20.3 %collective-permute-start = (bf16[1024,512]{1,0:T(8,128)(2,1)}, bf16[1024,512]{1,0:T(8,128)(2,1)S(1)}, u32[]{:S(2)}, u32[]{:S(2)}) collective-permute-start(bf16[1024,512]{1,0:T(8,128)(2,1)} %refs_0_.2), channel_id=1, source_target_pairs={{0,16},{16,0},{1,17},{17,1},{2,18},{18,2},{3,19},{19,3},{4,20},{20... | collective-permute-start | bytes 3145736 | tf_op jit(solution)/shard_map/ppermute | solution.py:16
  2.9 19.8 %all-to-all-start = ((bf16[16,8,1152]{2,1,0:T(8,128)(2,1)}), bf16[16,8,1152]{2,1,0:T(8,128)(2,1)S(1)}, u32[]{:S(2)}, u32[]{:S(2)}) async-start(bf16[16,8,1152]{2,1,0:T(8,128)(2,1)} %bitcast.13), calls=%async_computation | async-start | bytes 589824 | tf_op jit(solution)/shard_map/all_to_all | solution.py:512
  10.8 1.2 %copy-start = (bf16[1024,512]{1,0:T(8,128)(2,1)S(1)}, bf16[1024,512]{1,0:T(8,128)(2,1)}, u32[]{:S(2)}) copy-start(bf16[1024,512]{1,0:T(8,128)(2,1)} %refs_0_.2) | copy-start | bytes 3145732
  22.7 1.2 %collective-permute-start.1 = (bf16[128,128]{1,0:T(8,128)(2,1)S(1)}, bf16[128,128]{1,0:T(8,128)(2,1)S(1)}, u32[]{:S(2)}, u32[]{:S(2)}) collective-permute-start(bf16[128,128]{1,0:T(8,128)(2,1)S(1)} %slice.9), channel_id=1, source_target_pairs={{0,16},{16,0},{1,17},{17,1},{2,18},{18,2},{3,19},{19,3},{4,20},{20... | collective-permute-start | bytes 98312 | tf_op jit(solution)/shard_map/ppermute | solution.py:16
  25.8 5.8 %collective-permute-start.2 = (f32[128,128]{1,0:T(8,128)S(1)}, f32[128,128]{1,0:T(8,128)S(1)}, u32[]{:S(2)}, u32[]{:S(2)}) collective-permute-start(f32[128,128]{1,0:T(8,128)S(1)} %get-tuple-element.35), channel_id=1, source_target_pairs={{0,12},{4,8},{8,4},{12,0},{1,13},{5,9},{9,5},{13,1},{2,14},{6,10},... | collective-permute-start | bytes 196616 | tf_op jit(solution)/shard_map/ppermute | solution.py:16
  26.4 5.3 %collective-permute-start.3 = (f32[128,128]{1,0:T(8,128)S(1)}, f32[128,128]{1,0:T(8,128)S(1)}, u32[]{:S(2)}, u32[]{:S(2)}) collective-permute-start(f32[128,128]{1,0:T(8,128)S(1)} %get-tuple-element.35), channel_id=1, source_target_pairs={{0,8},{4,12},{8,0},{12,4},{1,9},{5,13},{9,1},{13,5},{2,10},{6,14},... | collective-permute-start | bytes 196616 | tf_op jit(solution)/shard_map/ppermute | solution.py:16
  27.0 4.7 %collective-permute-start.4 = (f32[128,128]{1,0:T(8,128)S(1)}, f32[128,128]{1,0:T(8,128)S(1)}, u32[]{:S(2)}, u32[]{:S(2)}) collective-permute-start(f32[128,128]{1,0:T(8,128)S(1)} %get-tuple-element.35), channel_id=1, source_target_pairs={{0,4},{4,0},{8,12},{12,8},{1,5},{5,1},{9,13},{13,9},{2,6},{6,2},{1... | collective-permute-start | bytes 196616 | tf_op jit(solution)/shard_map/ppermute | solution.py:16
  32.0 6.5 %collective-permute-start.5 = (f32[8,128]{1,0:T(8,128)S(1)}, f32[8,128]{1,0:T(8,128)S(1)}, u32[]{:S(2)}, u32[]{:S(2)}) collective-permute-start(f32[8,128]{1,0:T(8,128)S(1)} %get-tuple-element.39.refs_0_), channel_id=1, source_target_pairs={{0,2},{1,3},{2,0},{3,1},{4,6},{5,7},{6,4},{7,5},{8,10},{9,11},{10,... | collective-permute-start | bytes 12296 | tf_op jit(solution)/shard_map/ppermute | solution.py:16
  32.8 5.7 %collective-permute-start.6 = (f32[8,128]{1,0:T(8,128)S(1)}, f32[8,128]{1,0:T(8,128)S(1)}, u32[]{:S(2)}, u32[]{:S(2)}) collective-permute-start(f32[8,128]{1,0:T(8,128)S(1)} %get-tuple-element.39.refs_0_), channel_id=1, source_target_pairs={{0,3},{1,2},{2,1},{3,0},{4,7},{5,6},{6,5},{7,4},{8,11},{9,10},{10,... | collective-permute-start | bytes 12296 | tf_op jit(solution)/shard_map/ppermute | solution.py:16
  35.0 3.6 %collective-permute-start.7 = (f32[8,128]{1,0:T(8,128)S(1)}, f32[8,128]{1,0:T(8,128)S(1)}, u32[]{:S(2)}, u32[]{:S(2)}) collective-permute-start(f32[8,128]{1,0:T(8,128)S(1)} %get-tuple-element.39.refs_0_), channel_id=1, source_target_pairs={{0,1},{1,0},{2,3},{3,2},{4,5},{5,4},{6,7},{7,6},{8,9},{9,8},{10,11... | collective-permute-start | bytes 12296 | tf_op jit(solution)/shard_map/ppermute | solution.py:16
  39.6 6.6 %collective-permute-start.8 = (bf16[256,1024]{1,0:T(8,128)(2,1)S(1)}, bf16[256,1024]{1,0:T(8,128)(2,1)S(1)}, u32[]{:S(2)}, u32[]{:S(2)}) collective-permute-start(bf16[256,1024]{1,0:T(8,128)(2,1)S(1)} %get-tuple-element.46), channel_id=1, source_target_pairs={{0,16},{16,0},{1,17},{17,1},{2,18},{18,2},{3,19},{19,3},{4,20},{20... | collective-permute-start | bytes 1572872 | tf_op jit(solution)/shard_map/ppermute | solution.py:16
  40.4 14.6 %all-to-all-start.1 = ((f16[16,16,512]{2,1,0:T(8,128)(2,1)}), f16[16,16,512]{2,1,0:T(8,128)(2,1)S(1)}, u32[]{:S(2)}, u32[]{:S(2)}) async-start(f16[16,16,512]{2,1,0:T(8,128)(2,1)} %bitcast.4), calls=%async_computation.1 | async-start | bytes 524288 | tf_op jit(solution)/shard_map/all_to_all | solution.py:572
  44.5 1.6 %collective-permute-start.9 = (bf16[256,512]{1,0:T(8,128)(2,1)S(1)}, bf16[256,512]{1,0:T(8,128)(2,1)S(1)}, u32[]{:S(2)}, u32[]{:S(2)}) collective-permute-start(bf16[256,512]{1,0:T(8,128)(2,1)S(1)} %get-tuple-element.45.refs_1_), channel_id=1, source_target_pairs={{0,16},{16,0},{1,17},{17,1},{2,18},{18,2},{3,19},{19,3},{4,20},{20... | collective-permute-start | bytes 786440 | tf_op jit(solution)/shard_map/ppermute | solution.py:16

commit v7 on v6

--- a/solution.py
+++ b/solution.py
@@ -548,7 +548,7 @@
         z, place_kernel, [shape((z.rows, z.wide), f32)],
         [
             pltpu.VMEM((z.nrows, z.deep), f32), pltpu.VMEM((3, z.nrows, z.deep), f32),
-            pltpu.VMEM((z.rows * z.chunks, LANES), f32),
+            pltpu.VMEM(((z.rows + 1) * z.chunks, LANES), f32),
         ],
         [exponent, index, hot], 3 * work,
     )
@@ -569,6 +569,7 @@
     half = scatter_pairs(grads).astype(jnp.float16)
     half = half.reshape(z.tensor, z.corpus, z.own, z.width).swapaxes(0, 1)
     half = half.reshape(z.groups, z.own, z.width)
+    half, other_dense = lax.optimization_barrier((half, other_dense))
     half = lax.all_to_all(half, ("corpus", "tensor"), split_axis=0, concat_axis=0, tiled=True)
     (grad_pass,) = call(
         z, passage_kernel, [shape((z.block, z.width), f32)], [],

time: 56.2 us -> 56.2 us (level)
  transfers between devices with their start and end apart: 12 -> 12, of which waited for: 7 -> 7; matrix products, arithmetic and copies ran while one was open for 3% -> 1% of each run, Pallas kernels for 13% -> 13%
where the time goes in v7:
time: 56.2 us; the launch traced here: 55.8 us
  starting transfers between devices  19.9 us (35%)
  waiting for transfers between devices  19.8 us (35%)
  Pallas kernels  11.9 us (21%)
  local copies, waits for them, and re-layouts  1.99 us (4%)
  other arithmetic  1.45 us (3%)
  between operations  0.76 us (1%)
    pallas_call x9, Pallas kernels, call(): pl.pallas_call(lambda *refs: kernel(z, *refs), out_shape=outs, in_specs=[...  11.9 us
    all_to_all x1, waiting for transfers between devices, body(): lax.all_to_all(pieces[0], ('tensor', 'corpus'), split_axis=0, concat_axis...  10.6 us
    ppermute x10, starting transfers between devices, swap(): return lax.ppermute(value, axis, [(i, i ^ bit) for i in range(size)])  7.9 us
    all_to_all x1, starting transfers between devices, body(): lax.all_to_all(pieces[0], ('tensor', 'corpus'), split_axis=0, concat_axis...  7.89 us
    all_to_all x1, waiting for transfers between devices, body(): lax.all_to_all(half, ('corpus', 'tensor'), split_axis=0, concat_axis=0, t...  6.25 us
    all_to_all x1, starting transfers between devices, body(): lax.all_to_all(half, ('corpus', 'tensor'), split_axis=0, concat_axis=0, t...  4.09 us
    ppermute x10, waiting for transfers between devices, swap(): return lax.ppermute(value, axis, [(i, i ^ bit) for i in range(size)])  2.98 us
    unnamed x2, local copies, waits for them, and re-layouts  1.22 us
  transfers between devices with their start and end apart: 12, of which 7 were waited for; matrix products, arithmetic and copies ran while one was open for 1% of the time, Pallas kernels for 13%

profile of v7, /device:TPU:0, one launch (start us, length us, event | category | flops | bytes accessed | tf_op | source)
XLA Modules:
  0.0 55.8 jit_solution(3717975386388288834)
XLA Ops:
  0.6 1.8 %shard_map.67 = bf16[128,1152]{1,0:T(8,128)(2,1)} custom-call(s32[16]{0:T(128)} %refs_0_.1, s32[16,32]{1,0:T(8,128)} %refs_1_.1, bf16[16,2048]{1,0:T(8,128)(2,1)} %refs_2_.1), custom_call_target="tpu_custom_call" | custom-call | bytes 362560 | tf_op jit(solution)/shard_map/pallas_call | solution.py:482
  2.4 0.5 collective-permute-start
  2.9 7.9 %all-to-all-start = ((bf16[16,8,1152]{2,1,0:T(8,128)(2,1)}), bf16[16,8,1152]{2,1,0:T(8,128)(2,1)S(1)}, u32[]{:S(2)}, u32[]{:S(2)}) async-start(bf16[16,8,1152]{2,1,0:T(8,128)(2,1)} %bitcast.13), calls=%async_computation | async-start | bytes 589824 | tf_op jit(solution)/shard_map/all_to_all | solution.py:512
  10.8 1.2 %copy-done = bf16[1024,512]{1,0:T(8,128)(2,1)S(1)} copy-done((bf16[1024,512]{1,0:T(8,128)(2,1)S(1)}, bf16[1024,512]{1,0:T(8,128)(2,1)}, u32[]{:S(2)}) %copy-start) | copy-done | bytes 1048600
  12.1 10.6 %all-to-all-done = bf16[16,8,1152]{2,1,0:T(8,128)(2,1)S(1)} async-done(((bf16[16,8,1152]{2,1,0:T(8,128)(2,1)}), bf16[16,8,1152]{2,1,0:T(8,128)(2,1)S(1)}, u32[]{:S(2)}, u32[]{:S(2)}) %all-to-all-start) | async-done | bytes 294944 | tf_op jit(solution)/shard_map/all_to_all | solution.py:512
  22.7 0.7 %shard_map.69 = (bf16[256,512]{1,0:T(8,128)(2,1)S(1)}, f32[256,2048]{1,0:T(8,128)S(1)}, f32[256,128]{1,0:T(8,128)S(1)}, f32[256,128]{1,0:T(8,128)S(1)}) custom-call(bf16[128,1152]{1,0:T(8,128)(2,1)S(1)} %bitcast.12, bf16[1024,512]{1,0:T(8,128)(2,1)S(1)} %shard_map.68.refs_1_.refs_6_, bf16[1024,512]{1,0:T(8,128)(2,1)S(1)} %collective-permute-done.refs_2_.refs_7_), custom_call_target="tpu_custom_call" | custom-call | flops 536870912 | bytes 5013504 | tf_op jit(solution)/shard_map/pallas_call | solution.py:482
  23.9 1.8 %shard_map.70 = (f32[128,128]{1,0:T(8,128)S(1)}, s32[256,128]{1,0:T(8,128)S(1)}, f32[512,128]{1,0:T(8,128)S(1)}) custom-call(bf16[128,128]{1,0:T(8,128)(2,1)S(1)} %collective-permute-done.1.refs_0_, f32[256,2048]{1,0:T(8,128)S(1)} %get-tuple-element.34.refs_1_, f32[256,128]{1,0:T(8,128)S(1)} %get-tuple-element.35.refs_2_, ...), custom_call_target="tpu_custom_call" | custom-call | flops 33554432 | bytes 2850816 | tf_op jit(solution)/shard_map/pallas_call | solution.py:482
  25.8 0.6 %collective-permute-start.2 = (f32[128,128]{1,0:T(8,128)S(1)}, f32[128,128]{1,0:T(8,128)S(1)}, u32[]{:S(2)}, u32[]{:S(2)}) collective-permute-start(f32[128,128]{1,0:T(8,128)S(1)} %get-tuple-element.37), channel_id=1, source_target_pairs={{0,12},{4,8},{8,4},{12,0},{1,13},{5,9},{9,5},{13,1},{2,14},{6,10},... | collective-permute-start | bytes 196616 | tf_op jit(solution)/shard_map/ppermute | solution.py:16
  26.4 0.6 %collective-permute-start.3 = (f32[128,128]{1,0:T(8,128)S(1)}, f32[128,128]{1,0:T(8,128)S(1)}, u32[]{:S(2)}, u32[]{:S(2)}) collective-permute-start(f32[128,128]{1,0:T(8,128)S(1)} %get-tuple-element.37), channel_id=1, source_target_pairs={{0,8},{4,12},{8,0},{12,4},{1,9},{5,13},{9,1},{13,5},{2,10},{6,14},... | collective-permute-start | bytes 196616 | tf_op jit(solution)/shard_map/ppermute | solution.py:16
  27.0 2.4 %collective-permute-start.4 = (f32[128,128]{1,0:T(8,128)S(1)}, f32[128,128]{1,0:T(8,128)S(1)}, u32[]{:S(2)}, u32[]{:S(2)}) collective-permute-start(f32[128,128]{1,0:T(8,128)S(1)} %get-tuple-element.37), channel_id=1, source_target_pairs={{0,4},{4,0},{8,12},{12,8},{1,5},{5,1},{9,13},{13,9},{2,6},{6,2},{1... | collective-permute-start | bytes 196616 | tf_op jit(solution)/shard_map/ppermute | solution.py:16
  29.3 0.6 %shard_map.71 = (s32[32,256]{1,0:T(8,128)S(1)}, s32[128,128]{1,0:T(8,128)S(1)}, bf16[512,2048]{1,0:T(8,128)(2,1)S(1)}) custom-call(s32[256,128]{1,0:T(8,128)S(1)} %get-tuple-element.38.refs_0_, f32[512,128]{1,0:T(8,128)S(1)} %get-tuple-element.39.refs_1_), custom_call_target="tpu_custom_call" | custom-call | flops 8388608 | bytes 2588672 | tf_op jit(solution)/shard_map/pallas_call | solution.py:482
  30.0 1.6 %collective-permute-done.2 = f32[128,128]{1,0:T(8,128)S(1)} collective-permute-done((f32[128,128]{1,0:T(8,128)S(1)}, f32[128,128]{1,0:T(8,128)S(1)}, u32[]{:S(2)}, u32[]{:S(2)}) %collective-permute-start.2) | collective-permute-done | bytes 65568 | tf_op jit(solution)/shard_map/ppermute | solution.py:16
  32.0 0.8 %collective-permute-start.5 = (f32[8,128]{1,0:T(8,128)S(1)}, f32[8,128]{1,0:T(8,128)S(1)}, u32[]{:S(2)}, u32[]{:S(2)}) collective-permute-start(f32[8,128]{1,0:T(8,128)S(1)} %get-tuple-element.41.refs_0_), channel_id=1, source_target_pairs={{0,2},{1,3},{2,0},{3,1},{4,6},{5,7},{6,4},{7,5},{8,10},{9,11},{10,... | collective-permute-start | bytes 12296 | tf_op jit(solution)/shard_map/ppermute | solution.py:16
  32.8 2.2 %collective-permute-start.6 = (f32[8,128]{1,0:T(8,128)S(1)}, f32[8,128]{1,0:T(8,128)S(1)}, u32[]{:S(2)}, u32[]{:S(2)}) collective-permute-start(f32[8,128]{1,0:T(8,128)S(1)} %get-tuple-element.41.refs_0_), channel_id=1, source_target_pairs={{0,3},{1,2},{2,1},{3,0},{4,7},{5,6},{6,5},{7,4},{8,11},{9,10},{10,... | collective-permute-start | bytes 12296 | tf_op jit(solution)/shard_map/ppermute | solution.py:16
  35.0 0.5 collective-permute-start.7
  35.5 3.0 %shard_map.73.refs_4_ = f32[256,2048]{1,0:T(8,128)S(1)} custom-call(f32[128,128]{1,0:T(8,128)S(1)} %get-tuple-element.42.refs_0_, s32[32,256]{1,0:T(8,128)S(1)} %get-tuple-element.43.refs_1_, bf16[512,2048]{1,0:T(8,128)(2,1)S(1)} %get-tuple-element.44.refs_2_.refs_5_), custom_call_target="tpu_custom_call" | custom-call | flops 1610612736 | bytes 4292608 | tf_op jit(solution)/shard_map/pallas_call | solution.py:482
  38.6 0.9 %shard_map.74 = (bf16[256,1024]{1,0:T(8,128)(2,1)S(1)}, bf16[256,1024]{1,0:T(8,128)(2,1)S(1)}, f32[16,128]{1,0:T(8,128)S(1)}, f32[16,128]{1,0:T(8,128)S(1)}, f32[256,512]{1,0:T(8,128)S(1)}) custom-call(f32[8,128]{1,0:T(8,128)S(1)} %get-tuple-element.41.refs_0_, f32[8,128]{1,0:T(8,128)S(1)} %collective-permute-done.5.refs_1_, ...), custom_call_target="tpu_custom_call" | custom-call | flops 536870912 | bytes 7897088 | tf_op jit(solution)/shard_map/pallas_call | solution.py:482
  39.6 0.8 %copy.9 = f16[4,4,16,512]{3,2,0,1:T(8,128)(2,1)} copy(f16[4,4,16,512]{3,2,1,0:T(8,128)(2,1)S(1)} %bitcast.14) | data formatting | bytes 524288 | tf_op jit(solution)/shard_map/reshape | solution.py:570
  40.4 4.1 %all-to-all-start.1 = ((f16[16,16,512]{2,1,0:T(8,128)(2,1)}), f16[16,16,512]{2,1,0:T(8,128)(2,1)S(1)}, u32[]{:S(2)}, u32[]{:S(2)}) async-start(f16[16,16,512]{2,1,0:T(8,128)(2,1)} %bitcast.4), calls=%async_computation.1 | async-start | bytes 524288 | tf_op jit(solution)/shard_map/all_to_all | solution.py:573
  44.7 0.6 %slice_reduce_fusion = (f32[16]{0:T(128)}, f32[16]{0:T(128)S(1)}) fusion(f32[16,128]{1,0:T(8,128)S(1)} %get-tuple-element.53, f32[16,128]{1,0:T(8,128)S(1)} %get-tuple-element.52), kind=kLoop, calls=%fused_computation.3 | loop fusion | flops 16 | bytes 256 | tf_op jit(solution)/shard_map/slice | solution.py:581
  45.4 0.7 %collective-permute-done.9.refs_3_ = bf16[256,512]{1,0:T(8,128)(2,1)S(1)} collective-permute-done((bf16[256,512]{1,0:T(8,128)(2,1)S(1)}, bf16[256,512]{1,0:T(8,128)(2,1)S(1)}, u32[]{:S(2)}, u32[]{:S(2)}) %collective-permute-start.9) | collective-permute-done | bytes 262176 | tf_op jit(solution)/shard_map/ppermute | solution.py:16
  46.1 2.7 %shard_map.75 = f32[1024,512]{1,0:T(8,128)} custom-call(bf16[256,1024]{1,0:T(8,128)(2,1)S(1)} %get-tuple-element.48.refs_0_, bf16[256,512]{1,0:T(8,128)(2,1)S(1)} %get-tuple-element.49.refs_1_, bf16[256,1024]{1,0:T(8,128)(2,1)S(1)} %collective-permute-done.8.refs_2_, bf16[256,512]{1,0:T(8,128)(2,1)S(1)} %collective-permute-done.9.refs_3_), custom_call_target="tpu_custom_call" | custom-call | flops 536870912 | bytes 3670016 | tf_op jit(solution)/shard_map/pallas_call | solution.py:482
  48.7 6.3 %all-to-all-done.1 = f16[16,16,512]{2,1,0:T(8,128)(2,1)S(1)} async-done(((f16[16,16,512]{2,1,0:T(8,128)(2,1)}), f16[16,16,512]{2,1,0:T(8,128)(2,1)S(1)}, u32[]{:S(2)}, u32[]{:S(2)}) %all-to-all-start.1) | async-done | bytes 262176 | tf_op jit(solution)/shard_map/all_to_all | solution.py:573
  55.1 0.7 %broadcast_multiply_fusion = f32[16,2048]{1,0:T(8,128)} fusion(f32[16,2048]{1,0:T(8,128)S(1)} %bitcast.17, f32[16]{0:T(128)S(1)} %get-tuple-element.56), kind=kLoop, calls=%fused_computation.1 | loop fusion | flops 32768 | bytes 262208 | tf_op jit(solution)/shard_map/mul | solution.py:580
  (19 shorter events, 1.4 us)
Async XLA Ops:
  2.4 20.3 %collective-permute-start = (bf16[1024,512]{1,0:T(8,128)(2,1)}, bf16[1024,512]{1,0:T(8,128)(2,1)S(1)}, u32[]{:S(2)}, u32[]{:S(2)}) collective-permute-start(bf16[1024,512]{1,0:T(8,128)(2,1)} %refs_0_.2), channel_id=1, source_target_pairs={{0,16},{16,0},{1,17},{17,1},{2,18},{18,2},{3,19},{19,3},{4,20},{20... | collective-permute-start | bytes 3145736 | tf_op jit(solution)/shard_map/ppermute | solution.py:16
  2.9 19.8 %all-to-all-start = ((bf16[16,8,1152]{2,1,0:T(8,128)(2,1)}), bf16[16,8,1152]{2,1,0:T(8,128)(2,1)S(1)}, u32[]{:S(2)}, u32[]{:S(2)}) async-start(bf16[16,8,1152]{2,1,0:T(8,128)(2,1)} %bitcast.13), calls=%async_computation | async-start | bytes 589824 | tf_op jit(solution)/shard_map/all_to_all | solution.py:512
  10.8 1.2 %copy-start = (bf16[1024,512]{1,0:T(8,128)(2,1)S(1)}, bf16[1024,512]{1,0:T(8,128)(2,1)}, u32[]{:S(2)}) copy-start(bf16[1024,512]{1,0:T(8,128)(2,1)} %refs_0_.2) | copy-start | bytes 3145732
  22.7 1.2 %collective-permute-start.1 = (bf16[128,128]{1,0:T(8,128)(2,1)S(1)}, bf16[128,128]{1,0:T(8,128)(2,1)S(1)}, u32[]{:S(2)}, u32[]{:S(2)}) collective-permute-start(bf16[128,128]{1,0:T(8,128)(2,1)S(1)} %slice.9), channel_id=1, source_target_pairs={{0,16},{16,0},{1,17},{17,1},{2,18},{18,2},{3,19},{19,3},{4,20},{20... | collective-permute-start | bytes 98312 | tf_op jit(solution)/shard_map/ppermute | solution.py:16
  25.8 5.8 %collective-permute-start.2 = (f32[128,128]{1,0:T(8,128)S(1)}, f32[128,128]{1,0:T(8,128)S(1)}, u32[]{:S(2)}, u32[]{:S(2)}) collective-permute-start(f32[128,128]{1,0:T(8,128)S(1)} %get-tuple-element.37), channel_id=1, source_target_pairs={{0,12},{4,8},{8,4},{12,0},{1,13},{5,9},{9,5},{13,1},{2,14},{6,10},... | collective-permute-start | bytes 196616 | tf_op jit(solution)/shard_map/ppermute | solution.py:16
  26.4 5.3 %collective-permute-start.3 = (f32[128,128]{1,0:T(8,128)S(1)}, f32[128,128]{1,0:T(8,128)S(1)}, u32[]{:S(2)}, u32[]{:S(2)}) collective-permute-start(f32[128,128]{1,0:T(8,128)S(1)} %get-tuple-element.37), channel_id=1, source_target_pairs={{0,8},{4,12},{8,0},{12,4},{1,9},{5,13},{9,1},{13,5},{2,10},{6,14},... | collective-permute-start | bytes 196616 | tf_op jit(solution)/shard_map/ppermute | solution.py:16
  27.0 4.7 %collective-permute-start.4 = (f32[128,128]{1,0:T(8,128)S(1)}, f32[128,128]{1,0:T(8,128)S(1)}, u32[]{:S(2)}, u32[]{:S(2)}) collective-permute-start(f32[128,128]{1,0:T(8,128)S(1)} %get-tuple-element.37), channel_id=1, source_target_pairs={{0,4},{4,0},{8,12},{12,8},{1,5},{5,1},{9,13},{13,9},{2,6},{6,2},{1... | collective-permute-start | bytes 196616 | tf_op jit(solution)/shard_map/ppermute | solution.py:16
  32.0 6.5 %collective-permute-start.5 = (f32[8,128]{1,0:T(8,128)S(1)}, f32[8,128]{1,0:T(8,128)S(1)}, u32[]{:S(2)}, u32[]{:S(2)}) collective-permute-start(f32[8,128]{1,0:T(8,128)S(1)} %get-tuple-element.41.refs_0_), channel_id=1, source_target_pairs={{0,2},{1,3},{2,0},{3,1},{4,6},{5,7},{6,4},{7,5},{8,10},{9,11},{10,... | collective-permute-start | bytes 12296 | tf_op jit(solution)/shard_map/ppermute | solution.py:16
  32.8 5.7 %collective-permute-start.6 = (f32[8,128]{1,0:T(8,128)S(1)}, f32[8,128]{1,0:T(8,128)S(1)}, u32[]{:S(2)}, u32[]{:S(2)}) collective-permute-start(f32[8,128]{1,0:T(8,128)S(1)} %get-tuple-element.41.refs_0_), channel_id=1, source_target_pairs={{0,3},{1,2},{2,1},{3,0},{4,7},{5,6},{6,5},{7,4},{8,11},{9,10},{10,... | collective-permute-start | bytes 12296 | tf_op jit(solution)/shard_map/ppermute | solution.py:16
  35.0 3.6 %collective-permute-start.7 = (f32[8,128]{1,0:T(8,128)S(1)}, f32[8,128]{1,0:T(8,128)S(1)}, u32[]{:S(2)}, u32[]{:S(2)}) collective-permute-start(f32[8,128]{1,0:T(8,128)S(1)} %get-tuple-element.41.refs_0_), channel_id=1, source_target_pairs={{0,1},{1,0},{2,3},{3,2},{4,5},{5,4},{6,7},{7,6},{8,9},{9,8},{10,11... | collective-permute-start | bytes 12296 | tf_op jit(solution)/shard_map/ppermute | solution.py:16
  40.4 5.7 %collective-permute-start.8 = (bf16[256,1024]{1,0:T(8,128)(2,1)S(1)}, bf16[256,1024]{1,0:T(8,128)(2,1)S(1)}, u32[]{:S(2)}, u32[]{:S(2)}) collective-permute-start(bf16[256,1024]{1,0:T(8,128)(2,1)S(1)} %get-tuple-element.50), channel_id=1, source_target_pairs={{0,16},{16,0},{1,17},{17,1},{2,18},{18,2},{3,19},{19,3},{4,20},{20... | collective-permute-start | bytes 1572872 | tf_op jit(solution)/shard_map/ppermute | solution.py:16
  40.4 14.6 %all-to-all-start.1 = ((f16[16,16,512]{2,1,0:T(8,128)(2,1)}), f16[16,16,512]{2,1,0:T(8,128)(2,1)S(1)}, u32[]{:S(2)}, u32[]{:S(2)}) async-start(f16[16,16,512]{2,1,0:T(8,128)(2,1)} %bitcast.4), calls=%async_computation.1 | async-start | bytes 524288 | tf_op jit(solution)/shard_map/all_to_all | solution.py:573
  44.5 1.6 %collective-permute-start.9 = (bf16[256,512]{1,0:T(8,128)(2,1)S(1)}, bf16[256,512]{1,0:T(8,128)(2,1)S(1)}, u32[]{:S(2)}, u32[]{:S(2)}) collective-permute-start(bf16[256,512]{1,0:T(8,128)(2,1)S(1)} %get-tuple-element.49.refs_1_), channel_id=1, source_target_pairs={{0,16},{16,0},{1,17},{17,1},{2,18},{18,2},{3,19},{19,3},{4,20},{20... | collective-permute-start | bytes 786440 | tf_op jit(solution)/shard_map/ppermute | solution.py:16

commit v8 on v7

--- a/solution.py
+++ b/solution.py
@@ -109,12 +109,13 @@
             rows = jnp.concatenate([rows[: z.fold], rows[z.fold :], code], axis=1)
             rows = jnp.concatenate([rows, rows], axis=0).astype(jnp.bfloat16)
             for c in range(0, z.corpus, 2):
-                out_ref[pl.ds((t * z.corpus + c) * z.fold, z.own), :] = rows
+                k = (t * z.corpus + c + z.groups // 2) % z.groups
+                out_ref[pl.ds(k * z.fold, z.own), :] = rows
         return
     ids = jnp.concatenate([ids >> 8, ids & 255], axis=1)
     code = ids.astype(jnp.float32).astype(jnp.bfloat16)
     for k in range(z.groups):
-        t = k // z.corpus
+        t = (k + z.groups // 2) % z.groups // z.corpus
         at = pl.ds(k * z.own, z.own)
         out_ref[at, : z.width] = query_ref[:, t * z.width : (t + 1) * z.width]
         out_ref[at, z.width :] = code
@@ -509,7 +510,13 @@
         [passages], 0, [pltpu.HBM],
     )
     other_block = swap(passages, "dp", 1)
-    chip = lax.all_to_all(pieces[0], ("tensor", "corpus"), split_axis=0, concat_axis=0, tiled=True)
+    order = list(range(z.groups))
+    order = [order[z.groups // 2 :] + order[: z.groups // 2]]
+    chip = lax.all_to_all(
+        pieces[0], ("tensor", "corpus"), split_axis=0, concat_axis=0, tiled=True,
+        axis_index_groups=order,
+    )
+    chip = jnp.roll(chip, chip.shape[0] // 2, axis=0)
     chip, own_block, other_block = lax.optimization_barrier((chip, own_block, other_block))
     arrived = gather_pairs([chip])
     others = [swap(piece[:, z.message - LANES :], "dp", 1) for piece in arrived]
@@ -568,9 +575,15 @@
     )
     half = scatter_pairs(grads).astype(jnp.float16)
     half = half.reshape(z.tensor, z.corpus, z.own, z.width).swapaxes(0, 1)
+    half = jnp.roll(half, z.corpus // 2, axis=0)
     half = half.reshape(z.groups, z.own, z.width)
     half, other_dense = lax.optimization_barrier((half, other_dense))
-    half = lax.all_to_all(half, ("corpus", "tensor"), split_axis=0, concat_axis=0, tiled=True)
+    order = list(range(z.groups))
+    order = [order[z.groups // 2 :] + order[: z.groups // 2]]
+    half = lax.all_to_all(
+        half, ("corpus", "tensor"), split_axis=0, concat_axis=0, tiled=True,
+        axis_index_groups=order,
+    )
     (grad_pass,) = call(
         z, passage_kernel, [shape((z.block, z.width), f32)], [],
         [dense, query_rows, swap(other_dense, "dp", 1), swap(query_rows, "dp", 1)], work,

time: 56.2 us -> 54.8 us (0.975)
  waiting for transfers between devices: 19.8 us -> 16.3 us
  starting transfers between devices: 19.9 us -> 21.8 us
  other arithmetic: 1.45 us -> 2.24 us
  local copies, waits for them, and re-layouts: 1.99 us -> 1.35 us
    all_to_all x1, waiting for transfers between devices: 6.25 us -> 4.05 us  [body(): lax.all_to_all(half, ('corpus', 'tensor'), split_axis=0, concat_axis=0, t...]
    all_to_all x1, waiting for transfers between devices: 10.6 us -> 8.58 us  [body(): lax.all_to_all(pieces[0], ('tensor', 'corpus'), split_axis=0, concat_axis...]
    all_to_all x1, starting transfers between devices: 4.09 us -> 5.84 us  [body(): lax.all_to_all(half, ('corpus', 'tensor'), split_axis=0, concat_axis=0, t...]
    all_to_all x1, starting transfers between devices: 7.89 us -> 8.8 us  [body(): lax.all_to_all(pieces[0], ('tensor', 'corpus'), split_axis=0, concat_axis...]
    concatenate x0 -> x2, other arithmetic: none -> 0.79 us  [the longest x1 0.77 us: body(): half = jnp.roll(half, z.corpus // 2, axis=0)]
    ppermute x10, starting transfers between devices: 7.9 us -> 7.16 us  [swap(): return lax.ppermute(value, axis, [(i, i ^ bit) for i in range(size)])]
    ppermute x10, waiting for transfers between devices: 2.98 us -> 3.7 us  [swap(): return lax.ppermute(value, axis, [(i, i ^ bit) for i in range(size)])]
    reshape x1, local copies, waits for them, and re-layouts: 0.75 us -> 0.05 us  [body(): half = half.reshape(z.tensor, z.corpus, z.own, z.width).swapaxes(0, 1)]
where the time goes in v8:
time: 54.8 us; the launch traced here: 54.4 us
  starting transfers between devices  21.8 us (40%)
  waiting for transfers between devices  16.3 us (30%)
  Pallas kernels  11.9 us (22%)
  other arithmetic  2.24 us (4%)
  local copies, waits for them, and re-layouts  1.35 us (2%)
  between operations  0.8 us (1%)
    pallas_call x9, Pallas kernels, call(): pl.pallas_call(lambda *refs: kernel(z, *refs), out_shape=outs, in_specs=[...  11.9 us
    all_to_all x1, starting transfers between devices, body(): lax.all_to_all(pieces[0], ('tensor', 'corpus'), split_axis=0, concat_axis...  8.8 us
    all_to_all x1, waiting for transfers between devices, body(): lax.all_to_all(pieces[0], ('tensor', 'corpus'), split_axis=0, concat_axis...  8.58 us
    ppermute x10, starting transfers between devices, swap(): return lax.ppermute(value, axis, [(i, i ^ bit) for i in range(size)])  7.16 us
    all_to_all x1, starting transfers between devices, body(): lax.all_to_all(half, ('corpus', 'tensor'), split_axis=0, concat_axis=0, t...  5.84 us
    all_to_all x1, waiting for transfers between devices, body(): lax.all_to_all(half, ('corpus', 'tensor'), split_axis=0, concat_axis=0, t...  4.05 us
    ppermute x10, waiting for transfers between devices, swap(): return lax.ppermute(value, axis, [(i, i ^ bit) for i in range(size)])  3.7 us
    unnamed x2, local copies, waits for them, and re-layouts  1.22 us
  transfers between devices with their start and end apart: 12, of which 7 were waited for; matrix products, arithmetic and copies ran while one was open for 1% of the time, Pallas kernels for 13%

profile of v8, /device:TPU:0, one launch (start us, length us, event | category | flops | bytes accessed | tf_op | source)
XLA Modules:
  0.0 54.4 jit_solution(7473084331488316781)
XLA Ops:
  0.6 1.8 %shard_map.67 = bf16[128,1152]{1,0:T(8,128)(2,1)} custom-call(s32[16]{0:T(128)} %refs_0_.1, s32[16,32]{1,0:T(8,128)} %refs_1_.1, bf16[16,2048]{1,0:T(8,128)(2,1)} %refs_2_.1), custom_call_target="tpu_custom_call" | custom-call | bytes 362560 | tf_op jit(solution)/shard_map/pallas_call | solution.py:483
  2.4 8.8 %all-to-all-start = ((bf16[16,8,1152]{2,1,0:T(8,128)(2,1)}), bf16[16,8,1152]{2,1,0:T(8,128)(2,1)S(1)}, u32[]{:S(2)}, u32[]{:S(2)}) async-start(bf16[16,8,1152]{2,1,0:T(8,128)(2,1)} %bitcast.15), calls=%async_computation | async-start | bytes 589824 | tf_op jit(solution)/shard_map/all_to_all | solution.py:515
  11.2 1.2 %copy-done = bf16[1024,512]{1,0:T(8,128)(2,1)S(1)} copy-done((bf16[1024,512]{1,0:T(8,128)(2,1)S(1)}, bf16[1024,512]{1,0:T(8,128)(2,1)}, u32[]{:S(2)}) %copy-start) | copy-done | bytes 1048600
  12.5 8.6 %all-to-all-done = bf16[16,8,1152]{2,1,0:T(8,128)(2,1)S(1)} async-done(((bf16[16,8,1152]{2,1,0:T(8,128)(2,1)}), bf16[16,8,1152]{2,1,0:T(8,128)(2,1)S(1)}, u32[]{:S(2)}, u32[]{:S(2)}) %all-to-all-start) | async-done | bytes 294944 | tf_op jit(solution)/shard_map/all_to_all | solution.py:515
  21.3 0.7 %shard_map.69 = (bf16[256,512]{1,0:T(8,128)(2,1)S(1)}, f32[256,2048]{1,0:T(8,128)S(1)}, f32[256,128]{1,0:T(8,128)S(1)}, f32[256,128]{1,0:T(8,128)S(1)}) custom-call(bf16[128,1152]{1,0:T(8,128)(2,1)S(1)} %pad_maximum_fusion.refs_0_, bf16[1024,512]{1,0:T(8,128)(2,1)S(1)} %shard_map.68.refs_1_.refs_6_, bf16[1024,512]{1,0:T(8,128)(2,1)S(1)} %collective-permute-done.refs_2_.refs_7_), custom_call_target="tpu_custom_call" | custom-call | flops 536870912 | bytes 5013504 | tf_op jit(solution)/shard_map/pallas_call | solution.py:483
  22.0 0.4 collective-permute-done.1.refs_0_
  22.5 1.8 %shard_map.70 = (f32[128,128]{1,0:T(8,128)S(1)}, s32[256,128]{1,0:T(8,128)S(1)}, f32[512,128]{1,0:T(8,128)S(1)}) custom-call(bf16[128,128]{1,0:T(8,128)(2,1)S(1)} %collective-permute-done.1.refs_0_, f32[256,2048]{1,0:T(8,128)S(1)} %get-tuple-element.34.refs_1_, f32[256,128]{1,0:T(8,128)S(1)} %get-tuple-element.35.refs_2_, ...), custom_call_target="tpu_custom_call" | custom-call | flops 33554432 | bytes 2850816 | tf_op jit(solution)/shard_map/pallas_call | solution.py:483
  24.3 0.6 %collective-permute-start.2 = (f32[128,128]{1,0:T(8,128)S(1)}, f32[128,128]{1,0:T(8,128)S(1)}, u32[]{:S(2)}, u32[]{:S(2)}) collective-permute-start(f32[128,128]{1,0:T(8,128)S(1)} %get-tuple-element.37), channel_id=1, source_target_pairs={{0,12},{4,8},{8,4},{12,0},{1,13},{5,9},{9,5},{13,1},{2,14},{6,10},... | collective-permute-start | bytes 196616 | tf_op jit(solution)/shard_map/ppermute | solution.py:16
  24.9 1.5 %collective-permute-start.3 = (f32[128,128]{1,0:T(8,128)S(1)}, f32[128,128]{1,0:T(8,128)S(1)}, u32[]{:S(2)}, u32[]{:S(2)}) collective-permute-start(f32[128,128]{1,0:T(8,128)S(1)} %get-tuple-element.37), channel_id=1, source_target_pairs={{0,8},{4,12},{8,0},{12,4},{1,9},{5,13},{9,1},{13,5},{2,10},{6,14},... | collective-permute-start | bytes 196616 | tf_op jit(solution)/shard_map/ppermute | solution.py:16
  26.4 1.5 %collective-permute-start.4 = (f32[128,128]{1,0:T(8,128)S(1)}, f32[128,128]{1,0:T(8,128)S(1)}, u32[]{:S(2)}, u32[]{:S(2)}) collective-permute-start(f32[128,128]{1,0:T(8,128)S(1)} %get-tuple-element.37), channel_id=1, source_target_pairs={{0,4},{4,0},{8,12},{12,8},{1,5},{5,1},{9,13},{13,9},{2,6},{6,2},{1... | collective-permute-start | bytes 196616 | tf_op jit(solution)/shard_map/ppermute | solution.py:16
  27.9 0.6 %shard_map.71 = (s32[32,256]{1,0:T(8,128)S(1)}, s32[128,128]{1,0:T(8,128)S(1)}, bf16[512,2048]{1,0:T(8,128)(2,1)S(1)}) custom-call(s32[256,128]{1,0:T(8,128)S(1)} %get-tuple-element.38.refs_0_, f32[512,128]{1,0:T(8,128)S(1)} %get-tuple-element.39.refs_1_), custom_call_target="tpu_custom_call" | custom-call | flops 8388608 | bytes 2588672 | tf_op jit(solution)/shard_map/pallas_call | solution.py:483
  28.5 1.4 %collective-permute-done.2 = f32[128,128]{1,0:T(8,128)S(1)} collective-permute-done((f32[128,128]{1,0:T(8,128)S(1)}, f32[128,128]{1,0:T(8,128)S(1)}, u32[]{:S(2)}, u32[]{:S(2)}) %collective-permute-start.2) | collective-permute-done | bytes 65568 | tf_op jit(solution)/shard_map/ppermute | solution.py:16
  30.2 0.6 %collective-permute-done.4 = f32[128,128]{1,0:T(8,128)S(1)} collective-permute-done((f32[128,128]{1,0:T(8,128)S(1)}, f32[128,128]{1,0:T(8,128)S(1)}, u32[]{:S(2)}, u32[]{:S(2)}) %collective-permute-start.4) | collective-permute-done | bytes 65568 | tf_op jit(solution)/shard_map/ppermute | solution.py:16
  31.5 2.2 %collective-permute-start.6 = (f32[8,128]{1,0:T(8,128)S(1)}, f32[8,128]{1,0:T(8,128)S(1)}, u32[]{:S(2)}, u32[]{:S(2)}) collective-permute-start(f32[8,128]{1,0:T(8,128)S(1)} %get-tuple-element.41.refs_0_), channel_id=1, source_target_pairs={{0,3},{1,2},{2,1},{3,0},{4,7},{5,6},{6,5},{7,4},{8,11},{9,10},{10,... | collective-permute-start | bytes 12296 | tf_op jit(solution)/shard_map/ppermute | solution.py:16
  33.7 0.9 %collective-permute-start.7 = (f32[8,128]{1,0:T(8,128)S(1)}, f32[8,128]{1,0:T(8,128)S(1)}, u32[]{:S(2)}, u32[]{:S(2)}) collective-permute-start(f32[8,128]{1,0:T(8,128)S(1)} %get-tuple-element.41.refs_0_), channel_id=1, source_target_pairs={{0,1},{1,0},{2,3},{3,2},{4,5},{5,4},{6,7},{7,6},{8,9},{9,8},{10,11... | collective-permute-start | bytes 12296 | tf_op jit(solution)/shard_map/ppermute | solution.py:16
  34.6 3.0 %shard_map.73.refs_4_ = f32[256,2048]{1,0:T(8,128)S(1)} custom-call(f32[128,128]{1,0:T(8,128)S(1)} %get-tuple-element.42.refs_0_, s32[32,256]{1,0:T(8,128)S(1)} %get-tuple-element.43.refs_1_, bf16[512,2048]{1,0:T(8,128)(2,1)S(1)} %get-tuple-element.44.refs_2_.refs_5_), custom_call_target="tpu_custom_call" | custom-call | flops 1610612736 | bytes 4292608 | tf_op jit(solution)/shard_map/pallas_call | solution.py:483
  37.6 1.0 %shard_map.74 = (bf16[256,1024]{1,0:T(8,128)(2,1)S(1)}, bf16[256,1024]{1,0:T(8,128)(2,1)S(1)}, f32[16,128]{1,0:T(8,128)S(1)}, f32[16,128]{1,0:T(8,128)S(1)}, f32[256,512]{1,0:T(8,128)S(1)}) custom-call(f32[8,128]{1,0:T(8,128)S(1)} %get-tuple-element.41.refs_0_, f32[8,128]{1,0:T(8,128)S(1)} %collective-permute-done.5.refs_1_, ...), custom_call_target="tpu_custom_call" | custom-call | flops 536870912 | bytes 7897088 | tf_op jit(solution)/shard_map/pallas_call | solution.py:483
  38.8 0.8 %pad_maximum_fusion.1 = f16[4,4,16,512]{3,2,1,0:T(8,128)(2,1)} fusion(f16[2,4,16,512]{3,2,1,0:T(8,128)(2,1)S(1)} %get-tuple-element.58, f16[2,4,16,512]{3,2,1,0:T(8,128)(2,1)S(1)} %get-tuple-element.57), kind=kLoop, calls=%fused_computation.2 | loop fusion | flops 131072 | bytes 524288 | tf_op jit(solution)/shard_map/jit(_roll_static)/concatenate | solution.py:578
  39.5 5.8 %all-to-all-start.1 = ((f16[16,16,512]{2,1,0:T(8,128)(2,1)}), f16[16,16,512]{2,1,0:T(8,128)(2,1)S(1)}, u32[]{:S(2)}, u32[]{:S(2)}) async-start(f16[16,16,512]{2,1,0:T(8,128)(2,1)} %bitcast.5), calls=%async_computation.1 | async-start | bytes 524288 | tf_op jit(solution)/shard_map/all_to_all | solution.py:583
  45.4 0.6 %slice_reduce_fusion = (f32[16]{0:T(128)}, f32[16]{0:T(128)S(1)}) fusion(f32[16,128]{1,0:T(8,128)S(1)} %get-tuple-element.53, f32[16,128]{1,0:T(8,128)S(1)} %get-tuple-element.52), kind=kLoop, calls=%fused_computation.8 | loop fusion | flops 16 | bytes 256 | tf_op jit(solution)/shard_map/slice | solution.py:594
  46.0 0.9 %collective-permute-done.9.refs_3_ = bf16[256,512]{1,0:T(8,128)(2,1)S(1)} collective-permute-done((bf16[256,512]{1,0:T(8,128)(2,1)S(1)}, bf16[256,512]{1,0:T(8,128)(2,1)S(1)}, u32[]{:S(2)}, u32[]{:S(2)}) %collective-permute-start.9) | collective-permute-done | bytes 262176 | tf_op jit(solution)/shard_map/ppermute | solution.py:16
  46.9 2.7 %shard_map.75 = f32[1024,512]{1,0:T(8,128)} custom-call(bf16[256,1024]{1,0:T(8,128)(2,1)S(1)} %get-tuple-element.48.refs_0_, bf16[256,512]{1,0:T(8,128)(2,1)S(1)} %get-tuple-element.49.refs_1_, bf16[256,1024]{1,0:T(8,128)(2,1)S(1)} %collective-permute-done.8.refs_2_, bf16[256,512]{1,0:T(8,128)(2,1)S(1)} %collective-permute-done.9.refs_3_), custom_call_target="tpu_custom_call" | custom-call | flops 536870912 | bytes 3670016 | tf_op jit(solution)/shard_map/pallas_call | solution.py:483
  49.6 4.1 %all-to-all-done.1 = f16[16,16,512]{2,1,0:T(8,128)(2,1)S(1)} async-done(((f16[16,16,512]{2,1,0:T(8,128)(2,1)}), f16[16,16,512]{2,1,0:T(8,128)(2,1)S(1)}, u32[]{:S(2)}, u32[]{:S(2)}) %all-to-all-start.1) | async-done | bytes 262176 | tf_op jit(solution)/shard_map/all_to_all | solution.py:583
  53.7 0.7 %broadcast_multiply_fusion = f32[16,2048]{1,0:T(8,128)} fusion(f32[16,2048]{1,0:T(8,128)S(1)} %bitcast.20, f32[16]{0:T(128)S(1)} %get-tuple-element.60), kind=kLoop, calls=%fused_computation.6 | loop fusion | flops 32768 | bytes 262208 | tf_op jit(solution)/shard_map/mul | solution.py:593
  (23 shorter events, 1.4 us)
Async XLA Ops:
  2.4 18.7 %all-to-all-start = ((bf16[16,8,1152]{2,1,0:T(8,128)(2,1)}), bf16[16,8,1152]{2,1,0:T(8,128)(2,1)S(1)}, u32[]{:S(2)}, u32[]{:S(2)}) async-start(bf16[16,8,1152]{2,1,0:T(8,128)(2,1)} %bitcast.15), calls=%async_computation | async-start | bytes 589824 | tf_op jit(solution)/shard_map/all_to_all | solution.py:515
  11.2 10.0 %collective-permute-start = (bf16[1024,512]{1,0:T(8,128)(2,1)}, bf16[1024,512]{1,0:T(8,128)(2,1)S(1)}, u32[]{:S(2)}, u32[]{:S(2)}) collective-permute-start(bf16[1024,512]{1,0:T(8,128)(2,1)} %refs_0_.2), channel_id=1, source_target_pairs={{0,16},{16,0},{1,17},{17,1},{2,18},{18,2},{3,19},{19,3},{4,20},{20... | collective-permute-start | bytes 3145736 | tf_op jit(solution)/shard_map/ppermute | solution.py:16
  11.2 1.2 %copy-start = (bf16[1024,512]{1,0:T(8,128)(2,1)S(1)}, bf16[1024,512]{1,0:T(8,128)(2,1)}, u32[]{:S(2)}) copy-start(bf16[1024,512]{1,0:T(8,128)(2,1)} %refs_0_.2) | copy-start | bytes 3145732
  21.2 1.3 %collective-permute-start.1 = (bf16[128,128]{1,0:T(8,128)(2,1)S(1)}, bf16[128,128]{1,0:T(8,128)(2,1)S(1)}, u32[]{:S(2)}, u32[]{:S(2)}) collective-permute-start(bf16[128,128]{1,0:T(8,128)(2,1)S(1)} %slice.35), channel_id=1, source_target_pairs={{0,16},{16,0},{1,17},{17,1},{2,18},{18,2},{3,19},{19,3},{4,20},{20... | collective-permute-start | bytes 98312 | tf_op jit(solution)/shard_map/ppermute | solution.py:16
  24.3 5.6 %collective-permute-start.2 = (f32[128,128]{1,0:T(8,128)S(1)}, f32[128,128]{1,0:T(8,128)S(1)}, u32[]{:S(2)}, u32[]{:S(2)}) collective-permute-start(f32[128,128]{1,0:T(8,128)S(1)} %get-tuple-element.37), channel_id=1, source_target_pairs={{0,12},{4,8},{8,4},{12,0},{1,13},{5,9},{9,5},{13,1},{2,14},{6,10},... | collective-permute-start | bytes 196616 | tf_op jit(solution)/shard_map/ppermute | solution.py:16
  24.9 5.3 %collective-permute-start.3 = (f32[128,128]{1,0:T(8,128)S(1)}, f32[128,128]{1,0:T(8,128)S(1)}, u32[]{:S(2)}, u32[]{:S(2)}) collective-permute-start(f32[128,128]{1,0:T(8,128)S(1)} %get-tuple-element.37), channel_id=1, source_target_pairs={{0,8},{4,12},{8,0},{12,4},{1,9},{5,13},{9,1},{13,5},{2,10},{6,14},... | collective-permute-start | bytes 196616 | tf_op jit(solution)/shard_map/ppermute | solution.py:16
  26.4 4.4 %collective-permute-start.4 = (f32[128,128]{1,0:T(8,128)S(1)}, f32[128,128]{1,0:T(8,128)S(1)}, u32[]{:S(2)}, u32[]{:S(2)}) collective-permute-start(f32[128,128]{1,0:T(8,128)S(1)} %get-tuple-element.37), channel_id=1, source_target_pairs={{0,4},{4,0},{8,12},{12,8},{1,5},{5,1},{9,13},{13,9},{2,6},{6,2},{1... | collective-permute-start | bytes 196616 | tf_op jit(solution)/shard_map/ppermute | solution.py:16
  31.1 6.5 %collective-permute-start.5 = (f32[8,128]{1,0:T(8,128)S(1)}, f32[8,128]{1,0:T(8,128)S(1)}, u32[]{:S(2)}, u32[]{:S(2)}) collective-permute-start(f32[8,128]{1,0:T(8,128)S(1)} %get-tuple-element.41.refs_0_), channel_id=1, source_target_pairs={{0,2},{1,3},{2,0},{3,1},{4,6},{5,7},{6,4},{7,5},{8,10},{9,11},{10,... | collective-permute-start | bytes 12296 | tf_op jit(solution)/shard_map/ppermute | solution.py:16
  31.5 6.1 %collective-permute-start.6 = (f32[8,128]{1,0:T(8,128)S(1)}, f32[8,128]{1,0:T(8,128)S(1)}, u32[]{:S(2)}, u32[]{:S(2)}) collective-permute-start(f32[8,128]{1,0:T(8,128)S(1)} %get-tuple-element.41.refs_0_), channel_id=1, source_target_pairs={{0,3},{1,2},{2,1},{3,0},{4,7},{5,6},{6,5},{7,4},{8,11},{9,10},{10,... | collective-permute-start | bytes 12296 | tf_op jit(solution)/shard_map/ppermute | solution.py:16
  33.7 3.9 %collective-permute-start.7 = (f32[8,128]{1,0:T(8,128)S(1)}, f32[8,128]{1,0:T(8,128)S(1)}, u32[]{:S(2)}, u32[]{:S(2)}) collective-permute-start(f32[8,128]{1,0:T(8,128)S(1)} %get-tuple-element.41.refs_0_), channel_id=1, source_target_pairs={{0,1},{1,0},{2,3},{3,2},{4,5},{5,4},{6,7},{7,6},{8,9},{9,8},{10,11... | collective-permute-start | bytes 12296 | tf_op jit(solution)/shard_map/ppermute | solution.py:16
  39.5 7.4 %collective-permute-start.8 = (bf16[256,1024]{1,0:T(8,128)(2,1)S(1)}, bf16[256,1024]{1,0:T(8,128)(2,1)S(1)}, u32[]{:S(2)}, u32[]{:S(2)}) collective-permute-start(bf16[256,1024]{1,0:T(8,128)(2,1)S(1)} %get-tuple-element.50), channel_id=1, source_target_pairs={{0,16},{16,0},{1,17},{17,1},{2,18},{18,2},{3,19},{19,3},{4,20},{20... | collective-permute-start | bytes 1572872 | tf_op jit(solution)/shard_map/ppermute | solution.py:16
  39.5 14.1 %all-to-all-start.1 = ((f16[16,16,512]{2,1,0:T(8,128)(2,1)}), f16[16,16,512]{2,1,0:T(8,128)(2,1)S(1)}, u32[]{:S(2)}, u32[]{:S(2)}) async-start(f16[16,16,512]{2,1,0:T(8,128)(2,1)} %bitcast.5), calls=%async_computation.1 | async-start | bytes 524288 | tf_op jit(solution)/shard_map/all_to_all | solution.py:583
  45.4 1.5 %collective-permute-start.9 = (bf16[256,512]{1,0:T(8,128)(2,1)S(1)}, bf16[256,512]{1,0:T(8,128)(2,1)S(1)}, u32[]{:S(2)}, u32[]{:S(2)}) collective-permute-start(bf16[256,512]{1,0:T(8,128)(2,1)S(1)} %get-tuple-element.49.refs_1_), channel_id=1, source_target_pairs={{0,16},{16,0},{1,17},{17,1},{2,18},{18,2},{3,19},{19,3},{4,20},{20... | collective-permute-start | bytes 786440 | tf_op jit(solution)/shard_map/ppermute | solution.py:16

commit v9 on v8

--- a/solution.py
+++ b/solution.py
@@ -575,11 +575,11 @@
     )
     half = scatter_pairs(grads).astype(jnp.float16)
     half = half.reshape(z.tensor, z.corpus, z.own, z.width).swapaxes(0, 1)
-    half = jnp.roll(half, z.corpus // 2, axis=0)
+    half = jnp.roll(half, (z.corpus // 2, z.tensor // 2), axis=(0, 1))
     half = half.reshape(z.groups, z.own, z.width)
     half, other_dense = lax.optimization_barrier((half, other_dense))
-    order = list(range(z.groups))
-    order = [order[z.groups // 2 :] + order[: z.groups // 2]]
+    turned = [(c + z.corpus // 2) % z.corpus for c in range(z.corpus)]
+    order = [[c * z.tensor + (t + z.tensor // 2) % z.tensor for c in turned for t in range(z.tensor)]]
     half = lax.all_to_all(
         half, ("corpus", "tensor"), split_axis=0, concat_axis=0, tiled=True,
         axis_index_groups=order,
@@ -590,6 +590,7 @@
     )
     half, grad_pass = lax.optimization_barrier((half, grad_pass))
     half = half.astype(f32).reshape(z.corpus, z.tensor, z.own, z.width).sum(axis=0)
+    half = jnp.roll(half, z.tensor // 2, axis=0)
     grad_query = half.swapaxes(0, 1).reshape(z.own, z.feat) * (size[:, :1] * z.scale)
     return (grad_query, loss[:, 0], grad_pass)
 

time: 54.8 us -> 54.4 us (level)
    all_to_all x1, waiting for transfers between devices: 4.05 us -> 3.5 us  [body(): lax.all_to_all(half, ('corpus', 'tensor'), split_axis=0, concat_axis=0, t...]
where the time goes in v9:
time: 54.4 us; the launch traced here: 54 us
  starting transfers between devices  21.8 us (40%)
  waiting for transfers between devices  15.8 us (29%)
  Pallas kernels  11.9 us (22%)
  other arithmetic  2.29 us (4%)
  local copies, waits for them, and re-layouts  1.36 us (2%)
  between operations  0.83 us (2%)
    pallas_call x9, Pallas kernels, call(): pl.pallas_call(lambda *refs: kernel(z, *refs), out_shape=outs, in_specs=[...  11.9 us
    all_to_all x1, starting transfers between devices, body(): lax.all_to_all(pieces[0], ('tensor', 'corpus'), split_axis=0, concat_axis...  8.8 us
    all_to_all x1, waiting for transfers between devices, body(): lax.all_to_all(pieces[0], ('tensor', 'corpus'), split_axis=0, concat_axis...  8.58 us
    ppermute x10, starting transfers between devices, swap(): return lax.ppermute(value, axis, [(i, i ^ bit) for i in range(size)])  7.16 us
    all_to_all x1, starting transfers between devices, body(): lax.all_to_all(half, ('corpus', 'tensor'), split_axis=0, concat_axis=0, t...  5.84 us
    ppermute x10, waiting for transfers between devices, swap(): return lax.ppermute(value, axis, [(i, i ^ bit) for i in range(size)])  3.71 us
    all_to_all x1, waiting for transfers between devices, body(): lax.all_to_all(half, ('corpus', 'tensor'), split_axis=0, concat_axis=0, t...  3.5 us
    unnamed x2, local copies, waits for them, and re-layouts  1.22 us
  transfers between devices with their start and end apart: 12, of which 7 were waited for; matrix products, arithmetic and copies ran while one was open for 1% of the time, Pallas kernels for 13%

profile of v9, /device:TPU:0, one launch (start us, length us, event | category | flops | bytes accessed | tf_op | source)
XLA Modules:
  0.0 54.0 jit_solution(15076447609948111957)
XLA Ops:
  0.6 1.8 %shard_map.67 = bf16[128,1152]{1,0:T(8,128)(2,1)} custom-call(s32[16]{0:T(128)} %refs_0_.1, s32[16,32]{1,0:T(8,128)} %refs_1_.1, bf16[16,2048]{1,0:T(8,128)(2,1)} %refs_2_.1), custom_call_target="tpu_custom_call" | custom-call | bytes 362560 | tf_op jit(solution)/shard_map/pallas_call | solution.py:483
  2.4 8.8 %all-to-all-start = ((bf16[16,8,1152]{2,1,0:T(8,128)(2,1)}), bf16[16,8,1152]{2,1,0:T(8,128)(2,1)S(1)}, u32[]{:S(2)}, u32[]{:S(2)}) async-start(bf16[16,8,1152]{2,1,0:T(8,128)(2,1)} %bitcast.16), calls=%async_computation | async-start | bytes 589824 | tf_op jit(solution)/shard_map/all_to_all | solution.py:515
  11.2 1.2 %copy-done = bf16[1024,512]{1,0:T(8,128)(2,1)S(1)} copy-done((bf16[1024,512]{1,0:T(8,128)(2,1)S(1)}, bf16[1024,512]{1,0:T(8,128)(2,1)}, u32[]{:S(2)}) %copy-start) | copy-done | bytes 1048600
  12.5 8.6 %all-to-all-done = bf16[16,8,1152]{2,1,0:T(8,128)(2,1)S(1)} async-done(((bf16[16,8,1152]{2,1,0:T(8,128)(2,1)}), bf16[16,8,1152]{2,1,0:T(8,128)(2,1)S(1)}, u32[]{:S(2)}, u32[]{:S(2)}) %all-to-all-start) | async-done | bytes 294944 | tf_op jit(solution)/shard_map/all_to_all | solution.py:515
  21.3 0.7 %shard_map.69 = (bf16[256,512]{1,0:T(8,128)(2,1)S(1)}, f32[256,2048]{1,0:T(8,128)S(1)}, f32[256,128]{1,0:T(8,128)S(1)}, f32[256,128]{1,0:T(8,128)S(1)}) custom-call(bf16[128,1152]{1,0:T(8,128)(2,1)S(1)} %pad_maximum_fusion.refs_0_, bf16[1024,512]{1,0:T(8,128)(2,1)S(1)} %shard_map.68.refs_1_.refs_6_, bf16[1024,512]{1,0:T(8,128)(2,1)S(1)} %collective-permute-done.refs_2_.refs_7_), custom_call_target="tpu_custom_call" | custom-call | flops 536870912 | bytes 5013504 | tf_op jit(solution)/shard_map/pallas_call | solution.py:483
  22.0 0.5 collective-permute-done.1.refs_0_
  22.5 1.8 %shard_map.70 = (f32[128,128]{1,0:T(8,128)S(1)}, s32[256,128]{1,0:T(8,128)S(1)}, f32[512,128]{1,0:T(8,128)S(1)}) custom-call(bf16[128,128]{1,0:T(8,128)(2,1)S(1)} %collective-permute-done.1.refs_0_, f32[256,2048]{1,0:T(8,128)S(1)} %get-tuple-element.34.refs_1_, f32[256,128]{1,0:T(8,128)S(1)} %get-tuple-element.35.refs_2_, ...), custom_call_target="tpu_custom_call" | custom-call | flops 33554432 | bytes 2850816 | tf_op jit(solution)/shard_map/pallas_call | solution.py:483
  24.3 0.6 %collective-permute-start.2 = (f32[128,128]{1,0:T(8,128)S(1)}, f32[128,128]{1,0:T(8,128)S(1)}, u32[]{:S(2)}, u32[]{:S(2)}) collective-permute-start(f32[128,128]{1,0:T(8,128)S(1)} %get-tuple-element.37), channel_id=1, source_target_pairs={{0,12},{4,8},{8,4},{12,0},{1,13},{5,9},{9,5},{13,1},{2,14},{6,10},... | collective-permute-start | bytes 196616 | tf_op jit(solution)/shard_map/ppermute | solution.py:16
  24.9 1.5 %collective-permute-start.3 = (f32[128,128]{1,0:T(8,128)S(1)}, f32[128,128]{1,0:T(8,128)S(1)}, u32[]{:S(2)}, u32[]{:S(2)}) collective-permute-start(f32[128,128]{1,0:T(8,128)S(1)} %get-tuple-element.37), channel_id=1, source_target_pairs={{0,8},{4,12},{8,0},{12,4},{1,9},{5,13},{9,1},{13,5},{2,10},{6,14},... | collective-permute-start | bytes 196616 | tf_op jit(solution)/shard_map/ppermute | solution.py:16
  26.4 1.5 %collective-permute-start.4 = (f32[128,128]{1,0:T(8,128)S(1)}, f32[128,128]{1,0:T(8,128)S(1)}, u32[]{:S(2)}, u32[]{:S(2)}) collective-permute-start(f32[128,128]{1,0:T(8,128)S(1)} %get-tuple-element.37), channel_id=1, source_target_pairs={{0,4},{4,0},{8,12},{12,8},{1,5},{5,1},{9,13},{13,9},{2,6},{6,2},{1... | collective-permute-start | bytes 196616 | tf_op jit(solution)/shard_map/ppermute | solution.py:16
  27.9 0.6 %shard_map.71 = (s32[32,256]{1,0:T(8,128)S(1)}, s32[128,128]{1,0:T(8,128)S(1)}, bf16[512,2048]{1,0:T(8,128)(2,1)S(1)}) custom-call(s32[256,128]{1,0:T(8,128)S(1)} %get-tuple-element.38.refs_0_, f32[512,128]{1,0:T(8,128)S(1)} %get-tuple-element.39.refs_1_), custom_call_target="tpu_custom_call" | custom-call | flops 8388608 | bytes 2588672 | tf_op jit(solution)/shard_map/pallas_call | solution.py:483
  28.5 1.4 %collective-permute-done.2 = f32[128,128]{1,0:T(8,128)S(1)} collective-permute-done((f32[128,128]{1,0:T(8,128)S(1)}, f32[128,128]{1,0:T(8,128)S(1)}, u32[]{:S(2)}, u32[]{:S(2)}) %collective-permute-start.2) | collective-permute-done | bytes 65568 | tf_op jit(solution)/shard_map/ppermute | solution.py:16
  30.2 0.6 %collective-permute-done.4 = f32[128,128]{1,0:T(8,128)S(1)} collective-permute-done((f32[128,128]{1,0:T(8,128)S(1)}, f32[128,128]{1,0:T(8,128)S(1)}, u32[]{:S(2)}, u32[]{:S(2)}) %collective-permute-start.4) | collective-permute-done | bytes 65568 | tf_op jit(solution)/shard_map/ppermute | solution.py:16
  31.5 2.2 %collective-permute-start.6 = (f32[8,128]{1,0:T(8,128)S(1)}, f32[8,128]{1,0:T(8,128)S(1)}, u32[]{:S(2)}, u32[]{:S(2)}) collective-permute-start(f32[8,128]{1,0:T(8,128)S(1)} %get-tuple-element.41.refs_0_), channel_id=1, source_target_pairs={{0,3},{1,2},{2,1},{3,0},{4,7},{5,6},{6,5},{7,4},{8,11},{9,10},{10,... | collective-permute-start | bytes 12296 | tf_op jit(solution)/shard_map/ppermute | solution.py:16
  33.7 0.9 %collective-permute-start.7 = (f32[8,128]{1,0:T(8,128)S(1)}, f32[8,128]{1,0:T(8,128)S(1)}, u32[]{:S(2)}, u32[]{:S(2)}) collective-permute-start(f32[8,128]{1,0:T(8,128)S(1)} %get-tuple-element.41.refs_0_), channel_id=1, source_target_pairs={{0,1},{1,0},{2,3},{3,2},{4,5},{5,4},{6,7},{7,6},{8,9},{9,8},{10,11... | collective-permute-start | bytes 12296 | tf_op jit(solution)/shard_map/ppermute | solution.py:16
  34.6 3.0 %shard_map.73.refs_4_ = f32[256,2048]{1,0:T(8,128)S(1)} custom-call(f32[128,128]{1,0:T(8,128)S(1)} %get-tuple-element.42.refs_0_, s32[32,256]{1,0:T(8,128)S(1)} %get-tuple-element.43.refs_1_, bf16[512,2048]{1,0:T(8,128)(2,1)S(1)} %get-tuple-element.44.refs_2_.refs_5_), custom_call_target="tpu_custom_call" | custom-call | flops 1610612736 | bytes 4292608 | tf_op jit(solution)/shard_map/pallas_call | solution.py:483
  37.6 1.0 %shard_map.74 = (bf16[256,1024]{1,0:T(8,128)(2,1)S(1)}, bf16[256,1024]{1,0:T(8,128)(2,1)S(1)}, f32[16,128]{1,0:T(8,128)S(1)}, f32[16,128]{1,0:T(8,128)S(1)}, f32[256,512]{1,0:T(8,128)S(1)}) custom-call(f32[8,128]{1,0:T(8,128)S(1)} %get-tuple-element.41.refs_0_, f32[8,128]{1,0:T(8,128)S(1)} %collective-permute-done.5.refs_1_, ...), custom_call_target="tpu_custom_call" | custom-call | flops 536870912 | bytes 7897088 | tf_op jit(solution)/shard_map/pallas_call | solution.py:483
  38.8 0.8 %fusion = f16[4,4,16,512]{3,2,1,0:T(8,128)(2,1)} fusion(f16[2,4,16,512]{3,2,1,0:T(8,128)(2,1)S(1)} %get-tuple-element.58, f16[2,4,16,512]{3,2,1,0:T(8,128)(2,1)S(1)} %get-tuple-element.57, f16[4,2,16,512]{3,2,1,0:T(8,128)(2,1)S(1)} %fusion.1), kind=kLoop, calls=%fused_computation.3 | loop fusion | flops 262144 | bytes 655360 | tf_op jit(solution)/shard_map/jit(_roll_static)/concatenate | solution.py:578
  39.6 5.8 %all-to-all-start.1 = ((f16[16,16,512]{2,1,0:T(8,128)(2,1)}), f16[16,16,512]{2,1,0:T(8,128)(2,1)S(1)}, u32[]{:S(2)}, u32[]{:S(2)}) async-start(f16[16,16,512]{2,1,0:T(8,128)(2,1)} %bitcast.5), calls=%async_computation.1 | async-start | bytes 524288 | tf_op jit(solution)/shard_map/all_to_all | solution.py:583
  45.4 0.6 %slice_reduce_fusion = (f32[16]{0:T(128)}, f32[16]{0:T(128)S(1)}) fusion(f32[16,128]{1,0:T(8,128)S(1)} %get-tuple-element.53, f32[16,128]{1,0:T(8,128)S(1)} %get-tuple-element.52), kind=kLoop, calls=%fused_computation.13 | loop fusion | flops 16 | bytes 256 | tf_op jit(solution)/shard_map/slice | solution.py:595
  46.1 0.9 %collective-permute-done.9.refs_3_ = bf16[256,512]{1,0:T(8,128)(2,1)S(1)} collective-permute-done((bf16[256,512]{1,0:T(8,128)(2,1)S(1)}, bf16[256,512]{1,0:T(8,128)(2,1)S(1)}, u32[]{:S(2)}, u32[]{:S(2)}) %collective-permute-start.9) | collective-permute-done | bytes 262176 | tf_op jit(solution)/shard_map/ppermute | solution.py:16
  47.0 2.7 %shard_map.75 = f32[1024,512]{1,0:T(8,128)} custom-call(bf16[256,1024]{1,0:T(8,128)(2,1)S(1)} %get-tuple-element.48.refs_0_, bf16[256,512]{1,0:T(8,128)(2,1)S(1)} %get-tuple-element.49.refs_1_, bf16[256,1024]{1,0:T(8,128)(2,1)S(1)} %collective-permute-done.8.refs_2_, bf16[256,512]{1,0:T(8,128)(2,1)S(1)} %collective-permute-done.9.refs_3_), custom_call_target="tpu_custom_call" | custom-call | flops 536870912 | bytes 3670016 | tf_op jit(solution)/shard_map/pallas_call | solution.py:483
  49.6 3.5 %all-to-all-done.1 = f16[16,16,512]{2,1,0:T(8,128)(2,1)S(1)} async-done(((f16[16,16,512]{2,1,0:T(8,128)(2,1)}), f16[16,16,512]{2,1,0:T(8,128)(2,1)S(1)}, u32[]{:S(2)}, u32[]{:S(2)}) %all-to-all-start.1) | async-done | bytes 262176 | tf_op jit(solution)/shard_map/all_to_all | solution.py:583
  53.2 0.7 %broadcast_multiply_fusion = f32[16,2048]{1,0:T(8,128)} fusion(f32[16,2048]{1,0:T(8,128)S(1)} %bitcast.20, f32[16]{0:T(128)S(1)} %get-tuple-element.62), kind=kLoop, calls=%fused_computation.11 | loop fusion | flops 32768 | bytes 262208 | tf_op jit(solution)/shard_map/mul | solution.py:594
  (26 shorter events, 1.4 us)
Async XLA Ops:
  2.4 18.7 %all-to-all-start = ((bf16[16,8,1152]{2,1,0:T(8,128)(2,1)}), bf16[16,8,1152]{2,1,0:T(8,128)(2,1)S(1)}, u32[]{:S(2)}, u32[]{:S(2)}) async-start(bf16[16,8,1152]{2,1,0:T(8,128)(2,1)} %bitcast.16), calls=%async_computation | async-start | bytes 589824 | tf_op jit(solution)/shard_map/all_to_all | solution.py:515
  11.2 10.0 %collective-permute-start = (bf16[1024,512]{1,0:T(8,128)(2,1)}, bf16[1024,512]{1,0:T(8,128)(2,1)S(1)}, u32[]{:S(2)}, u32[]{:S(2)}) collective-permute-start(bf16[1024,512]{1,0:T(8,128)(2,1)} %refs_0_.2), channel_id=1, source_target_pairs={{0,16},{16,0},{1,17},{17,1},{2,18},{18,2},{3,19},{19,3},{4,20},{20... | collective-permute-start | bytes 3145736 | tf_op jit(solution)/shard_map/ppermute | solution.py:16
  11.2 1.2 %copy-start = (bf16[1024,512]{1,0:T(8,128)(2,1)S(1)}, bf16[1024,512]{1,0:T(8,128)(2,1)}, u32[]{:S(2)}) copy-start(bf16[1024,512]{1,0:T(8,128)(2,1)} %refs_0_.2) | copy-start | bytes 3145732
  21.2 1.3 %collective-permute-start.1 = (bf16[128,128]{1,0:T(8,128)(2,1)S(1)}, bf16[128,128]{1,0:T(8,128)(2,1)S(1)}, u32[]{:S(2)}, u32[]{:S(2)}) collective-permute-start(bf16[128,128]{1,0:T(8,128)(2,1)S(1)} %slice.51), channel_id=1, source_target_pairs={{0,16},{16,0},{1,17},{17,1},{2,18},{18,2},{3,19},{19,3},{4,20},{20... | collective-permute-start | bytes 98312 | tf_op jit(solution)/shard_map/ppermute | solution.py:16
  24.3 5.6 %collective-permute-start.2 = (f32[128,128]{1,0:T(8,128)S(1)}, f32[128,128]{1,0:T(8,128)S(1)}, u32[]{:S(2)}, u32[]{:S(2)}) collective-permute-start(f32[128,128]{1,0:T(8,128)S(1)} %get-tuple-element.37), channel_id=1, source_target_pairs={{0,12},{4,8},{8,4},{12,0},{1,13},{5,9},{9,5},{13,1},{2,14},{6,10},... | collective-permute-start | bytes 196616 | tf_op jit(solution)/shard_map/ppermute | solution.py:16
  24.9 5.3 %collective-permute-start.3 = (f32[128,128]{1,0:T(8,128)S(1)}, f32[128,128]{1,0:T(8,128)S(1)}, u32[]{:S(2)}, u32[]{:S(2)}) collective-permute-start(f32[128,128]{1,0:T(8,128)S(1)} %get-tuple-element.37), channel_id=1, source_target_pairs={{0,8},{4,12},{8,0},{12,4},{1,9},{5,13},{9,1},{13,5},{2,10},{6,14},... | collective-permute-start | bytes 196616 | tf_op jit(solution)/shard_map/ppermute | solution.py:16
  26.4 4.4 %collective-permute-start.4 = (f32[128,128]{1,0:T(8,128)S(1)}, f32[128,128]{1,0:T(8,128)S(1)}, u32[]{:S(2)}, u32[]{:S(2)}) collective-permute-start(f32[128,128]{1,0:T(8,128)S(1)} %get-tuple-element.37), channel_id=1, source_target_pairs={{0,4},{4,0},{8,12},{12,8},{1,5},{5,1},{9,13},{13,9},{2,6},{6,2},{1... | collective-permute-start | bytes 196616 | tf_op jit(solution)/shard_map/ppermute | solution.py:16
  31.1 6.5 %collective-permute-start.5 = (f32[8,128]{1,0:T(8,128)S(1)}, f32[8,128]{1,0:T(8,128)S(1)}, u32[]{:S(2)}, u32[]{:S(2)}) collective-permute-start(f32[8,128]{1,0:T(8,128)S(1)} %get-tuple-element.41.refs_0_), channel_id=1, source_target_pairs={{0,2},{1,3},{2,0},{3,1},{4,6},{5,7},{6,4},{7,5},{8,10},{9,11},{10,... | collective-permute-start | bytes 12296 | tf_op jit(solution)/shard_map/ppermute | solution.py:16
  31.5 6.1 %collective-permute-start.6 = (f32[8,128]{1,0:T(8,128)S(1)}, f32[8,128]{1,0:T(8,128)S(1)}, u32[]{:S(2)}, u32[]{:S(2)}) collective-permute-start(f32[8,128]{1,0:T(8,128)S(1)} %get-tuple-element.41.refs_0_), channel_id=1, source_target_pairs={{0,3},{1,2},{2,1},{3,0},{4,7},{5,6},{6,5},{7,4},{8,11},{9,10},{10,... | collective-permute-start | bytes 12296 | tf_op jit(solution)/shard_map/ppermute | solution.py:16
  33.7 3.9 %collective-permute-start.7 = (f32[8,128]{1,0:T(8,128)S(1)}, f32[8,128]{1,0:T(8,128)S(1)}, u32[]{:S(2)}, u32[]{:S(2)}) collective-permute-start(f32[8,128]{1,0:T(8,128)S(1)} %get-tuple-element.41.refs_0_), channel_id=1, source_target_pairs={{0,1},{1,0},{2,3},{3,2},{4,5},{5,4},{6,7},{7,6},{8,9},{9,8},{10,11... | collective-permute-start | bytes 12296 | tf_op jit(solution)/shard_map/ppermute | solution.py:16
  39.6 7.4 %collective-permute-start.8 = (bf16[256,1024]{1,0:T(8,128)(2,1)S(1)}, bf16[256,1024]{1,0:T(8,128)(2,1)S(1)}, u32[]{:S(2)}, u32[]{:S(2)}) collective-permute-start(bf16[256,1024]{1,0:T(8,128)(2,1)S(1)} %get-tuple-element.50), channel_id=1, source_target_pairs={{0,16},{16,0},{1,17},{17,1},{2,18},{18,2},{3,19},{19,3},{4,20},{20... | collective-permute-start | bytes 1572872 | tf_op jit(solution)/shard_map/ppermute | solution.py:16
  39.6 13.6 %all-to-all-start.1 = ((f16[16,16,512]{2,1,0:T(8,128)(2,1)}), f16[16,16,512]{2,1,0:T(8,128)(2,1)S(1)}, u32[]{:S(2)}, u32[]{:S(2)}) async-start(f16[16,16,512]{2,1,0:T(8,128)(2,1)} %bitcast.5), calls=%async_computation.1 | async-start | bytes 524288 | tf_op jit(solution)/shard_map/all_to_all | solution.py:583
  45.4 1.5 %collective-permute-start.9 = (bf16[256,512]{1,0:T(8,128)(2,1)S(1)}, bf16[256,512]{1,0:T(8,128)(2,1)S(1)}, u32[]{:S(2)}, u32[]{:S(2)}) collective-permute-start(bf16[256,512]{1,0:T(8,128)(2,1)S(1)} %get-tuple-element.49.refs_1_), channel_id=1, source_target_pairs={{0,16},{16,0},{1,17},{17,1},{2,18},{18,2},{3,19},{19,3},{4,20},{20... | collective-permute-start | bytes 786440 | tf_op jit(solution)/shard_map/ppermute | solution.py:16
